TPU v7x, 128 devices: a whole 4x4x4 slice. The times are simulated.
128 devices in a mesh: dp: 16 (over x, y), tensor: 8 (over z, core).
Axes of the slice: x: 4, y: 4, z: 4, core: 2. Of those that a mesh axis runs over, the one named last changes fastest.
Arguments:
- teacher_hidden: bfloat16 [2048, 4096], P('dp'), may hold values from -70 to 70
- student_hidden: bfloat16 [2048, 4096], P('dp'), may hold values from -70 to 70
- teacher_head: bfloat16 [4096, 76288], P(None, ('dp', 'tensor')), may hold values from -0.25 to 0.25
- student_head: bfloat16 [4096, 76288], P(None, ('dp', 'tensor')), may hold values from -0.25 to 0.25
- sampled_ids: int32 [2048], replicated, may hold values from 0 to 76287
- valid_mask: int32 [2048], replicated, may hold values 0 or 1
Outputs:
- head_grad: bfloat16 [4096, 76288], P(None, ('dp', 'tensor'))
- reverse_kl: float32 [], replicated
All inputs are finite; a program needn't handle non-finite values.
Results may differ from a plain program's by a relative error of at most 0.0075.
Values may be sent and summed in bfloat16 or wider, within the bound.
No kernel may reach another device: no remote copies, remote signals or barrier semaphores. Data moves between devices by JAX's collectives and lax.ppermute only.
A program may use at most 192 MiB of HBM per device.

v0:
```python
import jax
import jax.numpy as jnp
from jax import lax
from jax.sharding import PartitionSpec as P

loss_scale = 64.0
sampled_weight = 0.0625


def logit_gradient(factor, student_prob, difference, divergence, advantage, chosen):
    onehot = chosen.astype(jnp.float32)
    inner = student_prob * (difference - divergence[:, None])
    inner = inner - sampled_weight * advantage[:, None] * (onehot - student_prob)
    return (factor[:, None] * inner).astype(jnp.bfloat16)


def local(teacher_hidden, student_hidden, teacher_head, student_head, sampled_ids, valid_mask):
    stacked = jnp.stack([teacher_hidden, student_hidden])
    gathered = lax.all_gather(stacked, "dp", axis=1, tiled=True)
    teacher_logits = jnp.dot(gathered[0], teacher_head, preferred_element_type=jnp.float32)
    student_logits = jnp.dot(gathered[1], student_head, preferred_element_type=jnp.float32)
    weights = valid_mask.astype(jnp.float32)
    token_count = jnp.sum(weights)
    factor = loss_scale * weights / jnp.sqrt(token_count)
    both_logits = jnp.stack([teacher_logits, student_logits])
    regrouped = lax.all_to_all(
        both_logits, ("dp", "tensor"), split_axis=1, concat_axis=2, tiled=True
    )
    row_count = regrouped.shape[1]
    offset = lax.axis_index(("dp", "tensor")) * row_count
    local_ids = lax.dynamic_slice_in_dim(sampled_ids, offset, row_count, 0)
    local_factor = lax.dynamic_slice_in_dim(factor, offset, row_count, 0)
    local_weights = lax.dynamic_slice_in_dim(weights, offset, row_count, 0)
    teacher_rows = regrouped[0]
    student_rows = regrouped[1]
    teacher_norm = jax.nn.logsumexp(teacher_rows, axis=1)
    student_norm = jax.nn.logsumexp(student_rows, axis=1)
    student_logp = student_rows - student_norm[:, None]
    difference = student_logp - (teacher_rows - teacher_norm[:, None])
    student_prob = jnp.exp(student_logp)
    divergence = jnp.sum(student_prob * difference, axis=1)
    vocab_index = jnp.arange(teacher_rows.shape[1], dtype=jnp.int32)
    chosen = local_ids[:, None] == vocab_index[None, :]
    advantage = jnp.sum(jnp.where(chosen, -difference, jnp.float32(0.0)), axis=1)
    row_grad = logit_gradient(local_factor, student_prob, difference, divergence, advantage, chosen)
    logit_grad = lax.all_to_all(row_grad, ("dp", "tensor"), split_axis=1, concat_axis=0, tiled=True)
    partial_kl = jnp.sum(local_weights * divergence)
    reverse_kl = lax.psum(partial_kl, ("dp", "tensor")) / token_count
    head_grad = lax.dot_general(
        gathered[1], logit_grad, (((0,), (0,)), ((), ())), preferred_element_type=jnp.float32
    ).astype(jnp.bfloat16)
    return (head_grad, reverse_kl)


def solution(mesh):
    placed = (
        P("dp", None),
        P("dp", None),
        P(None, ("dp", "tensor")),
        P(None, ("dp", "tensor")),
        P(),
        P(),
    )
    return jax.shard_map(
        local,
        mesh=mesh,
        in_specs=placed,
        out_specs=(P(None, ("dp", "tensor")), P()),
        check_vma=False,
    )
```

profile of v0, /device:TPU:1, one launch (start us, length us, event | category | flops | bytes accessed | tf_op | source)
XLA Modules:
  0.0 539.3 jit_solution(9596472662643146099)
XLA Ops:
  7.2 0.0 all-gather.2.cloned.1.call-start
  7.2 3.1 pad_maximum_fusion.1
  10.3 0.0 all-gather.2.cloned.1.call-update
  10.3 200.7 %all-gather.2.cloned.1.call-done = bf16[2,2048,4096]{2,1,0:T(8,128)(2,1)} async-done(((bf16[2,128,4096]{2,1,0:T(8,128)(2,1)}), bf16[2,2048,4096]{2,1,0:T(8,128)(2,1)}) %all-gather.2.cloned.1.call-update) | async-done | bytes 33554448 | tf_op jit(solution)/shard_map/all_gather | solution.py:19
  211.0 14.7 %fusion.10 = f32[1,2048,596]{1,2,0:T(8,128)S(1)} fusion(bf16[4096,596]{0,1:T(8,128)(2,1)} %param.9, bf16[2,2048,4096]{2,1,0:T(8,128)(2,1)} %all-gather.2.cloned.1.call-done), kind=kOutput, calls=%fused_computation.22 | convolution fusion | flops 9999220736 | bytes 26574848 | tf_op jit(solution)/shard_map/dot_general | solution.py:21
  225.6 14.7 %fusion.11 = f32[1,2048,596]{1,2,0:T(8,128)S(1)} fusion(bf16[4096,596]{0,1:T(8,128)(2,1)} %param.8, bf16[2,2048,4096]{2,1,0:T(8,128)(2,1)} %all-gather.2.cloned.1.call-done), kind=kOutput, calls=%fused_computation.23 | convolution fusion | flops 9999220736 | bytes 26574848 | tf_op jit(solution)/shard_map/dot_general | solution.py:20
  240.3 4.5 pad_maximum_fusion
  244.8 16.2 %copy.9 = f32[2,2048,596]{2,0,1:T(2,128)} copy(f32[2,2048,596]{1,2,0:T(8,128)} %pad_maximum_fusion) | data formatting | bytes 19529728 | tf_op jit(solution)/shard_map/stack | solution.py:25
  261.0 0.0 copy-start
  261.0 8.4 %all-to-all-start = ((f32[2,2048,596]{2,0,1:T(2,128)}), f32[2,2048,596]{2,0,1:T(2,128)}, u32[]{:S(2)}, u32[]{:S(2)}) async-start(f32[2,2048,596]{2,0,1:T(2,128)} %copy.9), calls=%async_computation | async-start | bytes 20971520 | tf_op jit(solution)/shard_map/all_to_all | solution.py:26
  269.5 0.0 copy-done
  269.5 0.6 convert_reduce_fusion
  270.8 0.8 dynamic_slice.10
  271.6 127.2 %all-to-all-done = f32[2,2048,596]{2,0,1:T(2,128)} async-done(((f32[2,2048,596]{2,0,1:T(2,128)}), f32[2,2048,596]{2,0,1:T(2,128)}, u32[]{:S(2)}, u32[]{:S(2)}) %all-to-all-start) | async-done | bytes 9764896 | tf_op jit(solution)/shard_map/all_to_all | solution.py:26
  398.8 4.7 copy.10
  403.5 0.8 slice_reduce_fusion.1
  404.3 1.5 exponential_reduce_fusion.1
  405.8 1.4 exponential_reduce_fusion
  407.2 2.3 multiply_reduce_fusion
  409.5 0.7 multiply_reduce_fusion.1
  410.2 3.6 fusion.9
  413.8 12.7 %all-to-all-start.1 = ((bf16[16,128,596]{2,0,1:T(8,128)(2,1)}), bf16[16,128,596]{2,0,1:T(8,128)(2,1)S(1)}, u32[]{:S(2)}, u32[]{:S(2)}) async-start(bf16[16,128,596]{2,0,1:T(8,128)(2,1)} %fusion.9), calls=%async_computation.1 | async-start | bytes 5242880 | tf_op jit(solution)/shard_map/all_to_all | solution.py:46
  426.5 88.0 %psum.7 = f32[]{:T(128)} all-reduce(f32[]{:T(128)} %get-tuple-element.6), channel_id=1, replica_groups=mesh['dp'=16,'tensor'=8] {'dp','tensor'}, use_global_device_ids=true, to_apply=%region_8.9 | all-reduce | flops 1 | bytes 8 | tf_op jit(solution)/shard_map/psum | solution.py:48
  515.8 0.0 all-to-all-done.1
  515.8 15.5 %fusion.3 = bf16[4096,596]{0,1:T(8,128)(2,1)} fusion(bf16[2048,596]{1,0:T(8,128)(2,1)S(1)} %bitcast.51, bf16[2,2048,4096]{2,1,0:T(8,128)(2,1)} %all-gather.2.cloned.1.call-done), kind=kOutput, calls=%fused_computation.6 | convolution fusion | flops 10001661952 | bytes 24100864 | tf_op jit(solution)/shard_map/dot_general | solution.py:49
  (6 shorter events, 0.1 us)
Async XLA Ops:
  7.2 203.8 %all-gather.2.cloned.1.call-start = ((), (), s32[]{:S(2)}) async-start(), calls=%async_computation.2 | async-start | bytes 35651584 | tf_op jit(solution)/shard_map/all_gather | solution.py:19
  261.0 8.5 %copy-start = (s32[2048]{0:T(1024)S(1)}, s32[2048]{0:T(1024)}, u32[]{:S(2)}) copy-start(s32[2048]{0:T(1024)} %param.11) | copy-start | bytes 24580
  261.0 137.8 %all-to-all-start = ((f32[2,2048,596]{2,0,1:T(2,128)}), f32[2,2048,596]{2,0,1:T(2,128)}, u32[]{:S(2)}, u32[]{:S(2)}) async-start(f32[2,2048,596]{2,0,1:T(2,128)} %copy.9), calls=%async_computation | async-start | bytes 20971520 | tf_op jit(solution)/shard_map/all_to_all | solution.py:26
  413.8 102.0 %all-to-all-start.1 = ((bf16[16,128,596]{2,0,1:T(8,128)(2,1)}), bf16[16,128,596]{2,0,1:T(8,128)(2,1)S(1)}, u32[]{:S(2)}, u32[]{:S(2)}) async-start(bf16[16,128,596]{2,0,1:T(8,128)(2,1)} %fusion.9), calls=%async_computation.1 | async-start | bytes 5242880 | tf_op jit(solution)/shard_map/all_to_all | solution.py:46
Sparse Core Ops, SparseCore 0:
  10.8 200.1 all-gather.1
where the time goes:
time: 540 us; the launch traced here: 539 us
  waiting for transfers between devices  328 us (61%)
  blocking collectives  88 us (16%)
  matrix products  44.9 us (8%)
  local copies, waits for them, and re-layouts  21.6 us (4%)
  starting transfers between devices  21.2 us (4%)
  other arithmetic  18.5 us (3%)
  between operations  17.2 us (3%)
    all_gather x1, waiting for transfers between devices, local(): gathered = lax.all_gather(stacked, 'dp', axis=1, tiled=True)  201 us
    all_to_all x1, waiting for transfers between devices, local(): lax.all_to_all(both_logits, ('dp', 'tensor'), split_axis=1, concat_axis=2...  127 us
    psum x1, blocking collectives, local(): reverse_kl = lax.psum(partial_kl, ('dp', 'tensor')) / token_count  88 us
    another operation x1, local copies, waits for them, and re-layouts, local(): both_logits = jnp.stack([teacher_logits, student_logits])  16.2 us
    dot_general x1, matrix products, local(): lax.dot_general(gathered[1], logit_grad, (((0,), (0,)), ((), ())), prefer...  15.5 us
    dot_general x1, matrix products, local(): jnp.dot(gathered[0], teacher_head, preferred_element_type=jnp.float32)  14.7 us
    dot_general x1, matrix products, local(): jnp.dot(gathered[1], student_head, preferred_element_type=jnp.float32)  14.7 us
    all_to_all x1, starting transfers between devices, local(): lax.all_to_all(row_grad, ('dp', 'tensor'), split_axis=1, concat_axis=0, t...  12.7 us
  transfers between devices with their start and end apart: 3, of which 2 were waited for; matrix products, arithmetic and copies ran while one was open for 0% of the time, Pallas kernels for 0%

commit v1 on v0

v1 whole, which is shorter than its diff:
```python
import functools

import jax
import jax.numpy as jnp
from jax import lax
from jax.experimental import pallas as pl
from jax.experimental.pallas import tpu as pltpu
from jax.sharding import PartitionSpec as P

LOSS_SCALE = 64.0
SAMPLED_WEIGHT = 0.0625
SIDE = 4
AXES = ("dp", "tensor")
OFFSETS = (0, -1, 1, 2)
F32 = jnp.float32
MIB = 1 << 20


def flat(x, y, z, c):
    return (((x % SIDE) * SIDE + y % SIDE) * SIDE + z % SIDE) * 2 + c


def pairs(step):
    return [
        (flat(x, y, z, c), flat(*step(x, y, z, c)))
        for x in range(SIDE) for y in range(SIDE) for z in range(SIDE) for c in range(2)
    ]


def first(d):
    return pairs(lambda x, y, z, c: (x + d * (1 - c), y + d * c, z, c))


def second(d):
    return pairs(lambda x, y, z, c: (x + d * c, y + d * (1 - c), z, c))


def along(axis, d):
    return pairs(lambda x, y, z, c: (x + d * (axis == 0), y + d * (axis == 1), z + d * (axis == 2), c))


SIBLING = pairs(lambda x, y, z, c: (x, y, z, 1 - c))


def send(array, perm):
    return lax.ppermute(array, AXES, perm)


def nt(a, b):
    return lax.dot_general(a, b, (((1,), (1,)), ((), ())), preferred_element_type=F32)


def stats_of(s, t, chosen):
    u = s - t
    ms = jnp.max(s, axis=0, keepdims=True)
    mt = jnp.max(t, axis=0, keepdims=True)
    es = jnp.exp(s - ms)
    zs = jnp.sum(es, axis=0, keepdims=True)
    zt = jnp.sum(jnp.exp(t - mt), axis=0, keepdims=True)
    mean = jnp.sum(es * u, axis=0, keepdims=True) / zs
    picked = jnp.sum(jnp.where(chosen, u, 0.0), axis=0, keepdims=True)
    return u, (mt + jnp.log(zt), ms + jnp.log(zs), mean, picked)


def add_all(values):
    if len(values) == 4:
        return (values[0] + values[3]) + (values[1] + values[2])
    return sum(values[1:], values[0])


def join(parts):
    def lse(values):
        top = functools.reduce(jnp.maximum, values)
        return top + jnp.log(add_all([jnp.exp(v - top) for v in values]))
    nt_all = lse([p[0] for p in parts])
    ns_all = lse([p[1] for p in parts])
    mean = add_all([jnp.exp(p[1] - ns_all) * p[2] for p in parts])
    return nt_all, ns_all, mean, add_all([p[3] for p in parts])


def logits_kernel(steps, first_ref, ids_ref, t_ref, s_ref, ta_ref, sa_ref, tb_ref, sb_ref,
                  oas_ref, oau_ref, obs_ref, obu_ref, st_ref):
    k = pl.program_id(0)
    t_hid = t_ref[0] if len(t_ref.shape) == 3 else t_ref[...]
    s_hid = s_ref[0] if len(s_ref.shape) == 3 else s_ref[...]
    for head, hid, out in ((sa_ref, s_hid, oas_ref), (ta_ref, t_hid, oau_ref),
                           (sb_ref, s_hid, obs_ref), (tb_ref, t_hid, obu_ref)):
        part = nt(head[...], hid)

        @pl.when(k == 0)
        def _():
            out[...] = part

        @pl.when(k > 0)
        def _():
            out[...] += part

    @pl.when(k == steps - 1)
    def _():
        parts = []
        for i, (so, uo) in enumerate(((oas_ref, oau_ref), (obs_ref, obu_ref))):
            s, t = so[...], uo[...]
            rows = lax.broadcasted_iota(jnp.int32, s.shape, 0) + first_ref[i]
            u, part = stats_of(s, t, rows == ids_ref[...])
            uo[...] = u
            parts.append(part)
        total = join(parts)
        tokens = total[0].shape[1] // SIDE
        for q in range(4):
            for b in range(SIDE):
                st_ref[b, q:q + 1, :] = total[q][:, b * tokens:(b + 1) * tokens]


def logits_call(firsts, ids, stack, heads, t_alone=None, s_alone=None):
    ta, sa, tb, sb = heads
    vocab, depth = ta.shape
    tile = 1024
    steps = depth // tile
    if t_alone is None:
        tokens = stack.shape[1]
        hids = [stack, stack]
        hid_specs = [pl.BlockSpec((1, tokens, tile), lambda k, j=j: (j, 0, k)) for j in range(2)]
    else:
        tokens = t_alone.shape[0]
        hids = [t_alone, s_alone]
        hid_specs = [pl.BlockSpec((tokens, tile), lambda k: (0, k))] * 2
    head_spec = pl.BlockSpec((vocab, tile), lambda k: (0, k))
    out = jax.ShapeDtypeStruct((vocab, tokens), F32)
    whole = pl.BlockSpec((vocab, tokens), lambda k: (0, 0))
    return pl.pallas_call(
        functools.partial(logits_kernel, steps),
        grid=(steps,),
        in_specs=[pl.BlockSpec(memory_space=pltpu.SMEM), pl.BlockSpec((1, tokens), lambda k: (0, 0))]
        + hid_specs + [head_spec] * 4,
        out_specs=[whole] * 4 + [pl.BlockSpec((SIDE, 4, tokens // SIDE), lambda k: (0, 0, 0))],
        out_shape=[out] * 4 + [jax.ShapeDtypeStruct((SIDE, 4, tokens // SIDE), F32)],
        compiler_params=pltpu.CompilerParams(vmem_limit_bytes=32 * MIB),
        cost_estimate=pl.CostEstimate(flops=8 * vocab * tokens * depth, bytes_accessed=8 * vocab * depth, transcendentals=0),
    )(firsts, ids, *hids, ta, sa, tb, sb)


def order_kernel(place_ref, *refs):
    *groups, out_ref = refs
    for j, group in enumerate(groups):
        for i in range(SIDE):
            b = place_ref[j * SIDE + i]
            for q in range(4):
                out_ref[q, pl.ds(b, 1), :] = group[i, q:q + 1, :]


def order_call(place, groups):
    tokens = groups[0].shape[-1]
    return pl.pallas_call(
        order_kernel,
        in_specs=[pl.BlockSpec(memory_space=pltpu.SMEM)] + [pl.BlockSpec(memory_space=pltpu.VMEM)] * len(groups),
        out_specs=pl.BlockSpec(memory_space=pltpu.VMEM),
        out_shape=jax.ShapeDtypeStruct((4, SIDE * SIDE, tokens), F32),
    )(place, *groups)


def join_kernel(*refs):
    *ins, out_ref = refs
    total = join([[r[q] for q in range(4)] for r in ins])
    for q in range(4):
        out_ref[q] = total[q]


def join_call(parts):
    vmem = pl.BlockSpec(memory_space=pltpu.VMEM)
    return pl.pallas_call(
        join_kernel,
        in_specs=[vmem] * len(parts),
        out_specs=vmem,
        out_shape=jax.ShapeDtypeStruct(parts[0].shape, F32),
    )(*parts)


def finish_kernel(place_ref, factor_ref, weight_ref, *refs):
    *ins, coef_ref, kl_ref, rows_ref = refs
    n_t, n_s, mean, picked = join([[r[q] for q in range(4)] for r in ins])
    kl_ref[...] = jnp.sum(weight_ref[...] * (mean + n_t - n_s), keepdims=True)
    pull = SAMPLED_WEIGHT * -(picked + n_t - n_s)
    for q, value in enumerate((n_s, factor_ref[...], pull - mean, pull)):
        rows_ref[q] = value
    tokens = n_s.shape[1]
    for j in range(SIDE):
        for q in range(4):
            for i in range(SIDE):
                coef_ref[j, q:q + 1, i * tokens:(i + 1) * tokens] = rows_ref[q, pl.ds(place_ref[j * SIDE + i], 1), :]


def finish_call(place, factor, weight, parts):
    vmem = pl.BlockSpec(memory_space=pltpu.VMEM)
    tokens = factor.shape[1]
    return pl.pallas_call(
        finish_kernel,
        in_specs=[pl.BlockSpec(memory_space=pltpu.SMEM)] + [vmem] * (2 + len(parts)),
        out_specs=[vmem, vmem],
        out_shape=[jax.ShapeDtypeStruct((SIDE, 4, SIDE * tokens), F32), jax.ShapeDtypeStruct((1, 1), F32)],
        scratch_shapes=[pltpu.VMEM((4, SIDE * SIDE, tokens), F32)],
    )(place, factor, weight, *parts)


def grad_kernel(first_ref, ids_ref, coef_ref, *refs):
    *ins, out_ref = refs
    for j in range(SIDE):
        s, u = ins[2 * j][...], ins[2 * j + 1][...]
        n_s, factor, shift, pull = (coef_ref[j, q:q + 1, :] for q in range(4))
        rows = lax.broadcasted_iota(jnp.int32, s.shape, 0) + first_ref[0]
        inner = jnp.exp(s - n_s) * (u + shift)
        inner = inner - jnp.where(rows == ids_ref[j:j + 1, :], pull, 0.0)
        tokens = s.shape[1]
        out_ref[:, j * tokens:(j + 1) * tokens] = (factor * inner).astype(jnp.bfloat16)


def grad_call(first_row, ids, coef, logits):
    vocab, tokens = logits[0].shape
    vmem = pl.BlockSpec(memory_space=pltpu.VMEM)
    return pl.pallas_call(
        grad_kernel,
        in_specs=[pl.BlockSpec(memory_space=pltpu.SMEM)] + [vmem] * (2 + len(logits)),
        out_specs=vmem,
        out_shape=jax.ShapeDtypeStruct((vocab, SIDE * tokens), jnp.bfloat16),
        compiler_params=pltpu.CompilerParams(vmem_limit_bytes=32 * MIB),
        cost_estimate=pl.CostEstimate(flops=10 * vocab * tokens * SIDE, bytes_accessed=10 * vocab * tokens * SIDE, transcendentals=0),
    )(first_row, ids, coef, *logits)


def head_kernel(ga_ref, gb_ref, *refs):
    *hids, out_ref = refs
    half = len(hids) // 2
    total = None
    for g, group in ((ga_ref, hids[:half]), (gb_ref, hids[half:])):
        rows = jnp.concatenate([r[0] if len(r.shape) == 3 else r[...] for r in group], axis=0)
        part = jnp.dot(g[...], rows, preferred_element_type=F32)
        total = part if total is None else total + part
    out_ref[...] = total.astype(jnp.bfloat16)


def head_call(ga, gb, hids):
    vocab, tokens = ga.shape
    depth = hids[0].shape[-1]
    tile = 512
    specs = []
    for h in hids:
        if h.ndim == 3:
            specs.append(pl.BlockSpec((1, h.shape[1], tile), lambda i: (1, 0, i)))
        else:
            specs.append(pl.BlockSpec((h.shape[0], tile), lambda i: (0, i)))
    whole = pl.BlockSpec((vocab, tokens), lambda i: (0, 0))
    return pl.pallas_call(
        head_kernel,
        grid=(depth // tile,),
        in_specs=[whole, whole] + specs,
        out_specs=pl.BlockSpec((vocab, tile), lambda i: (0, i)),
        out_shape=jax.ShapeDtypeStruct((vocab, depth), jnp.bfloat16),
        compiler_params=pltpu.CompilerParams(vmem_limit_bytes=32 * MIB),
        cost_estimate=pl.CostEstimate(flops=4 * vocab * tokens * depth, bytes_accessed=4 * tokens * depth, transcendentals=0),
    )(ga, gb, *hids)


def local(teacher_hidden, student_hidden, teacher_head, student_head, sampled_ids, valid_mask):
    dp, tensor = lax.axis_index("dp"), lax.axis_index("tensor")
    x, y, core = dp // SIDE, dp % SIDE, tensor % 2
    half = teacher_hidden.shape[0] // 2
    vocab = teacher_head.shape[1]

    ta, sa = teacher_head.T, student_head.T
    tb, sb = send(ta, SIBLING), send(sa, SIBLING)
    heads = (ta, sa, tb, sb)

    shift = jnp.array([o % SIDE for o in OFFSETS], jnp.int32)
    one = (jnp.where(core == 0, x, y) + shift) % SIDE
    two = (jnp.where(core == 0, y, x) + shift) % SIDE
    place = jnp.where(core == 0, one[None, :] * SIDE + two[:, None], two[:, None] * SIDE + one[None, :]).reshape(-1)

    def mine(a):
        return lax.dynamic_index_in_dim(a.reshape(SIDE * SIDE, 2, half), core, 1, keepdims=False)

    ids = jnp.take(mine(sampled_ids), place, axis=0).reshape(SIDE, SIDE * half)
    all_weights = valid_mask.astype(F32)
    token_count = jnp.sum(all_weights)
    weights = mine(all_weights)
    factor = LOSS_SCALE * weights / jnp.sqrt(token_count)
    row_of = flat(x, y, tensor // 2, core) * vocab
    other_of = flat(x, y, tensor // 2, 1 - core) * vocab
    firsts = jnp.stack([row_of, other_of])

    own = lax.dynamic_slice_in_dim(jnp.stack([teacher_hidden, student_hidden]), core * half, half, 1)
    low, high = send(own, first(1)), send(own, first(-1))
    far_t, far_s = send(low[0], first(1)), send(high[1], first(-1))
    far = jnp.stack([far_t, far_s])
    row = jnp.concatenate([own, low, high, far], axis=1)
    row_low, row_high = send(row, second(1)), send(row, second(-1))
    far_t, far_s = send(row_low[0], second(1)), send(row_high[1], second(-1))

    groups = [
        logits_call(firsts, ids[0:1], row, heads),
        logits_call(firsts, ids[1:2], row_low, heads),
        logits_call(firsts, ids[2:3], row_high, heads),
        logits_call(firsts, ids[3:4], None, heads, far_t, far_s),
    ]
    students = [row, row_low, row_high, far_s]
    others = [send(h, SIBLING) for h in students]

    total = order_call(place, [g[4] for g in groups])
    for axis in range(3):
        parts = [total, send(total, along(axis, 1)), send(total, along(axis, -1)), send(total, along(axis, 2))]
        if axis < 2:
            total = join_call(parts)
    coef, kl = finish_call(place, factor, weights, parts)

    away = grad_call(firsts[1:], ids, coef, [a for g in groups for a in g[2:4]])
    arrived = send(away, SIBLING)
    kl = kl + send(kl, SIBLING)
    kept = grad_call(firsts[:1], ids, coef, [a for g in groups for a in g[0:2]])
    head_grad = head_call(kept, arrived, students + others).T
    return head_grad, kl[0, 0] / token_count


def solution(mesh):
    placed = (
        P("dp", None),
        P("dp", None),
        P(None, AXES),
        P(None, AXES),
        P(),
        P(),
    )
    return jax.shard_map(
        local,
        mesh=mesh,
        in_specs=placed,
        out_specs=(P(None, AXES), P()),
        check_vma=False,
    )
```

time: 540 us -> 274 us (0.51)
  waiting for transfers between devices: 328 us -> 93.2 us
  Pallas kernels: 0 us -> 97.1 us
  blocking collectives: 88 us -> 0 us
  matrix products: 44.9 us -> 0 us
  local copies, waits for them, and re-layouts: 21.6 us -> 37.3 us
  starting transfers between devices: 21.2 us -> 35.2 us
  other arithmetic: 18.5 us -> 5.1 us
  between operations: 17.2 us -> 4.56 us
    all_gather x1 -> x0, waiting for transfers between devices: 201 us -> none  [local(): gathered = lax.all_gather(stacked, 'dp', axis=1, tiled=True)]
    all_to_all x2 -> x0, waiting for transfers between devices: 127 us -> none  [the longest x1 127 us: local(): lax.all_to_all(both_logits, ('dp', 'tensor'), split_axis=1, concat_axis=2...]
    pallas_call x0 -> x11, Pallas kernels: none -> 97.1 us  [the longest x4 73.4 us: logits_call(): pl.pallas_call(functools.partial(logits_kernel, steps), grid=(steps,), in...]
    ppermute x0 -> x25, waiting for transfers between devices: none -> 93.2 us  [send(): return lax.ppermute(array, AXES, perm)]
    psum x1 -> x0, blocking collectives: 88 us -> none  [local(): reverse_kl = lax.psum(partial_kl, ('dp', 'tensor')) / token_count]
    dot_general x3 -> x0, matrix products: 44.9 us -> none  [the longest x1 15.5 us: local(): lax.dot_general(gathered[1], logit_grad, (((0,), (0,)), ((), ())), prefer...]
    ppermute x0 -> x25, starting transfers between devices: none -> 35.2 us  [send(): return lax.ppermute(array, AXES, perm)]
    unnamed x2 -> x94, local copies, waits for them, and re-layouts: 0.01 us -> 29.4 us
  transfers between devices with their start and end apart: 3 -> 25, of which waited for: 2 -> 13; matrix products, arithmetic and copies ran while one was open for 0% -> 3% of each run, Pallas kernels for 0% -> 30%
where the time goes in v1:
time: 274 us; the launch traced here: 272 us
  Pallas kernels  97.1 us (35%)
  waiting for transfers between devices  93.2 us (34%)
  local copies, waits for them, and re-layouts  37.3 us (14%)
  starting transfers between devices  35.2 us (13%)
  other arithmetic  5.1 us (2%)
  between operations  4.56 us (2%)
    ppermute x25, waiting for transfers between devices, send(): return lax.ppermute(array, AXES, perm)  93.2 us
    pallas_call x4, Pallas kernels, logits_call(): pl.pallas_call(functools.partial(logits_kernel, steps), grid=(steps,), in...  73.4 us
    ppermute x25, starting transfers between devices, send(): return lax.ppermute(array, AXES, perm)  35.2 us
    unnamed x94, local copies, waits for them, and re-layouts  29.4 us
    pallas_call x1, Pallas kernels, head_call(): pl.pallas_call(head_kernel, grid=(depth // tile,), in_specs=[whole, whole...  15.1 us
    squeeze x2, local copies, waits for them, and re-layouts, local(): far_t, far_s = (send(row_low[0], second(1)), send(row_high[1], second(-1)))  6.27 us
  transfers between devices with their start and end apart: 25, of which 13 were waited for; matrix products, arithmetic and copies ran while one was open for 3% of the time, Pallas kernels for 30%

profile of v1, /device:TPU:1, one launch (start us, length us, event | category | flops | bytes accessed | tf_op | source)
XLA Modules:
  0.0 272.4 jit_solution(9363115869226115457)
XLA Ops:
  0.6 1.3 fusion
  1.9 3.6 %collective-permute-start.1 = (bf16[2,64,4096]{2,1,0:T(8,128)(2,1)S(1)}, bf16[2,64,4096]{2,1,0:T(8,128)(2,1)S(1)}, u32[]{:S(2)}, u32[]{:S(2)}) collective-permute-start(bf16[2,64,4096]{2,1,0:T(8,128)(2,1)S(1)} %fusion), channel_id=1, source_target_pairs={{0,96},{1,25},{2,98},{3,27},{4,100},{5,29},{6,102},{7,31},{8,104},... | collective-permute-start | bytes 3145736 | tf_op jit(solution)/shard_map/ppermute | solution.py:46
  5.6 11.7 %collective-permute-done.1 = bf16[2,64,4096]{2,1,0:T(8,128)(2,1)S(1)} collective-permute-done((bf16[2,64,4096]{2,1,0:T(8,128)(2,1)S(1)}, bf16[2,64,4096]{2,1,0:T(8,128)(2,1)S(1)}, u32[]{:S(2)}, u32[]{:S(2)}) %collective-permute-start.1) | collective-permute-done | bytes 1048608 | tf_op jit(solution)/shard_map/ppermute | solution.py:46
  17.4 3.5 %collective-permute-start.3 = (bf16[64,4096]{1,0:T(8,128)(2,1)S(1)}, bf16[64,4096]{1,0:T(8,128)(2,1)S(1)}, u32[]{:S(2)}, u32[]{:S(2)}) collective-permute-start(bf16[64,4096]{1,0:T(8,128)(2,1)S(1)} %slice_bitcast_fusion.2), channel_id=1, source_target_pairs={{0,96},{1,25},{2,98},{3,27},{4,100},{5,29},{6,102},{7,31},{8,104},... | collective-permute-start | bytes 1572872 | tf_op jit(solution)/shard_map/ppermute | solution.py:46
  21.0 6.0 %collective-permute-done.3 = bf16[64,4096]{1,0:T(8,128)(2,1)S(1)} collective-permute-done((bf16[64,4096]{1,0:T(8,128)(2,1)S(1)}, bf16[64,4096]{1,0:T(8,128)(2,1)S(1)}, u32[]{:S(2)}, u32[]{:S(2)}) %collective-permute-start.3) | collective-permute-done | bytes 524320 | tf_op jit(solution)/shard_map/ppermute | solution.py:46
  27.0 3.5 %collective-permute-done.2 = bf16[64,4096]{1,0:T(8,128)(2,1)S(1)} collective-permute-done((bf16[64,4096]{1,0:T(8,128)(2,1)S(1)}, bf16[64,4096]{1,0:T(8,128)(2,1)S(1)}, u32[]{:S(2)}, u32[]{:S(2)}) %collective-permute-start.2) | collective-permute-done | bytes 524320 | tf_op jit(solution)/shard_map/ppermute | solution.py:46
  30.5 2.3 maximum_maximum_fusion.t_ref.s_ref.refs_0_
  33.4 2.1 collective-permute-start.7
  35.5 3.0 %collective-permute-start.4 = (bf16[596,4096]{1,0:T(8,128)(2,1)}, bf16[596,4096]{1,0:T(8,128)(2,1)}, u32[]{:S(2)}, u32[]{:S(2)}) collective-permute-start(bf16[596,4096]{1,0:T(8,128)(2,1)} %bitcast.11.ta_ref), channel_id=1, source_target_pairs={{0,1},{1,0},{2,3},{3,2},{4,5},{5,4},{6,7},{7,6},{8,9},{9,8},{10,11... | collective-permute-start | bytes 14647304 | tf_op jit(solution)/shard_map/ppermute | solution.py:46
  39.4 42.6 %collective-permute-done.6.t_ref.s_ref.refs_1_ = bf16[2,256,4096]{2,1,0:T(8,128)(2,1)} collective-permute-done((bf16[2,256,4096]{2,1,0:T(8,128)(2,1)}, bf16[2,256,4096]{2,1,0:T(8,128)(2,1)}, u32[]{:S(2)}, u32[]{:S(2)}) %collective-permute-start.6) | collective-permute-done | bytes 4194336 | tf_op jit(solution)/shard_map/ppermute | solution.py:46
  82.0 3.1 %slice_bitcast_fusion.1 = bf16[256,4096]{1,0:T(8,128)(2,1)} fusion(bf16[2,256,4096]{2,1,0:T(8,128)(2,1)} %collective-permute-done.6.t_ref.s_ref.refs_1_), kind=kLoop, calls=%fused_computation.3 | loop fusion | bytes 4194304 | tf_op jit(solution)/shard_map/squeeze | solution.py:295
  85.1 3.1 %slice_bitcast_fusion = bf16[256,4096]{1,0:T(8,128)(2,1)} fusion(bf16[2,256,4096]{2,1,0:T(8,128)(2,1)} %collective-permute-done.7.t_ref.s_ref.refs_2_), kind=kLoop, calls=%fused_computation.2 | loop fusion | bytes 4194304 | tf_op jit(solution)/shard_map/squeeze | solution.py:295
  88.2 2.7 collective-permute-start.9
  90.9 3.9 %collective-permute-start.20 = (bf16[2,256,4096]{2,1,0:T(8,128)(2,1)}, bf16[2,256,4096]{2,1,0:T(8,128)(2,1)}, u32[]{:S(2)}, u32[]{:S(2)}) collective-permute-start(bf16[2,256,4096]{2,1,0:T(8,128)(2,1)} %maximum_maximum_fusion.t_ref.s_ref.refs_0_), channel_id=1, source_target_pairs={{0,1},{1,0},{2,3},{3,2},{4,5},{5,4},{6,7},{7,6},{8,9},{9,8},{10,11... | collective-permute-start | bytes 12582920 | tf_op jit(solution)/shard_map/ppermute | solution.py:46
  95.8 18.3 %shard_map.86 = (f32[596,256]{1,0:T(8,128)S(1)}, f32[596,256]{1,0:T(8,128)S(1)}, f32[596,256]{1,0:T(8,128)S(1)}, f32[596,256]{1,0:T(8,128)S(1)}, f32[4,4,64]{2,1,0:T(4,128)S(1)}) custom-call(s32[2]{0:T(128)S(1)} %pad_add_fusion.first_ref, s32[1,256]{1,0:T(1,128)S(1)} %slice.37.ids_ref, bf16[2,256,4096]{2,1,0:T(8,128)(2,1)} %maximum_maximum_fusion.t_ref.s_ref.refs_0_, ...), custom_call_target="tpu_custom_call" | custom-call | flops 4999610368 | bytes 19529728 | tf_op jit(solution)/shard_map/pallas_call | solution.py:130
  116.4 18.4 %shard_map.87 = (f32[596,256]{1,0:T(8,128)S(1)}, f32[596,256]{1,0:T(8,128)S(1)}, f32[596,256]{1,0:T(8,128)S(1)}, f32[596,256]{1,0:T(8,128)S(1)}, f32[4,4,64]{2,1,0:T(4,128)S(1)}) custom-call(s32[2]{0:T(128)S(1)} %pad_add_fusion.first_ref, s32[1,256]{1,0:T(1,128)S(1)} %slice.41.ids_ref, bf16[2,256,4096]{2,1,0:T(8,128)(2,1)} %collective-permute-done.6.t_ref.s_ref.refs_1_, ...), custom_call_target="tpu_custom_call" | custom-call | flops 4999610368 | bytes 19529728 | tf_op jit(solution)/shard_map/pallas_call | solution.py:130
  138.6 18.4 %shard_map.88 = (f32[596,256]{1,0:T(8,128)S(1)}, f32[596,256]{1,0:T(8,128)S(1)}, f32[596,256]{1,0:T(8,128)S(1)}, f32[596,256]{1,0:T(8,128)S(1)}, f32[4,4,64]{2,1,0:T(4,128)S(1)}) custom-call(s32[2]{0:T(128)S(1)} %pad_add_fusion.first_ref, s32[1,256]{1,0:T(1,128)S(1)} %slice.43.ids_ref, bf16[2,256,4096]{2,1,0:T(8,128)(2,1)} %collective-permute-done.7.t_ref.s_ref.refs_2_, ...), custom_call_target="tpu_custom_call" | custom-call | flops 4999610368 | bytes 19529728 | tf_op jit(solution)/shard_map/pallas_call | solution.py:130
  161.2 18.3 %shard_map.89 = (f32[596,256]{1,0:T(8,128)S(1)}, f32[596,256]{1,0:T(8,128)S(1)}, f32[596,256]{1,0:T(8,128)S(1)}, f32[596,256]{1,0:T(8,128)S(1)}, f32[4,4,64]{2,1,0:T(4,128)S(1)}) custom-call(s32[2]{0:T(128)S(1)} %pad_add_fusion.first_ref, s32[1,256]{1,0:T(1,128)S(1)} %slice.45.ids_ref, bf16[256,4096]{1,0:T(8,128)(2,1)} %collective-permute-done.8.t_ref, ...), custom_call_target="tpu_custom_call" | custom-call | flops 4999610368 | bytes 19529728 | tf_op jit(solution)/shard_map/pallas_call | solution.py:130
  183.5 1.4 shard_map.90.refs_0_
  184.9 4.2 %collective-permute-done.10.refs_1_ = f32[4,16,64]{2,1,0:T(8,128)S(1)} collective-permute-done((f32[4,16,64]{2,1,0:T(8,128)}, f32[4,16,64]{2,1,0:T(8,128)S(1)}, u32[]{:S(2)}, u32[]{:S(2)}) %collective-permute-start.10) | collective-permute-done | bytes 16416 | tf_op jit(solution)/shard_map/ppermute | solution.py:46
  189.1 3.0 %collective-permute-done.11.refs_2_ = f32[4,16,64]{2,1,0:T(8,128)S(1)} collective-permute-done((f32[4,16,64]{2,1,0:T(8,128)}, f32[4,16,64]{2,1,0:T(8,128)S(1)}, u32[]{:S(2)}, u32[]{:S(2)}) %collective-permute-start.11) | collective-permute-done | bytes 16416 | tf_op jit(solution)/shard_map/ppermute | solution.py:46
  192.1 4.5 %collective-permute-done.12.refs_3_ = f32[4,16,64]{2,1,0:T(8,128)S(1)} collective-permute-done((f32[4,16,64]{2,1,0:T(8,128)}, f32[4,16,64]{2,1,0:T(8,128)S(1)}, u32[]{:S(2)}, u32[]{:S(2)}) %collective-permute-start.12) | collective-permute-done | bytes 16416 | tf_op jit(solution)/shard_map/ppermute | solution.py:46
  197.2 1.4 shard_map.91.refs_0_
  198.6 4.2 %collective-permute-done.13.refs_1_ = f32[4,16,64]{2,1,0:T(8,128)S(1)} collective-permute-done((f32[4,16,64]{2,1,0:T(8,128)}, f32[4,16,64]{2,1,0:T(8,128)S(1)}, u32[]{:S(2)}, u32[]{:S(2)}) %collective-permute-start.13) | collective-permute-done | bytes 16416 | tf_op jit(solution)/shard_map/ppermute | solution.py:46
  202.8 3.0 %collective-permute-done.14.refs_2_ = f32[4,16,64]{2,1,0:T(8,128)S(1)} collective-permute-done((f32[4,16,64]{2,1,0:T(8,128)}, f32[4,16,64]{2,1,0:T(8,128)S(1)}, u32[]{:S(2)}, u32[]{:S(2)}) %collective-permute-start.14) | collective-permute-done | bytes 16416 | tf_op jit(solution)/shard_map/ppermute | solution.py:46
  206.6 3.7 %collective-permute-done.15.refs_3_ = f32[4,16,64]{2,1,0:T(8,128)S(1)} collective-permute-done((f32[4,16,64]{2,1,0:T(8,128)}, f32[4,16,64]{2,1,0:T(8,128)S(1)}, u32[]{:S(2)}, u32[]{:S(2)}) %collective-permute-start.15) | collective-permute-done | bytes 16416 | tf_op jit(solution)/shard_map/ppermute | solution.py:46
  210.9 1.5 shard_map.92.refs_0_
  212.3 1.6 collective-permute-start.16
  214.7 2.9 %collective-permute-done.16.refs_1_ = f32[4,16,64]{2,1,0:T(8,128)S(1)} collective-permute-done((f32[4,16,64]{2,1,0:T(8,128)}, f32[4,16,64]{2,1,0:T(8,128)S(1)}, u32[]{:S(2)}, u32[]{:S(2)}) %collective-permute-start.16) | collective-permute-done | bytes 16416 | tf_op jit(solution)/shard_map/ppermute | solution.py:46
  217.6 1.5 collective-permute-start.17
  220.6 1.3 collective-permute-start.18
  221.9 3.3 %collective-permute-done.18.refs_3_ = f32[4,16,64]{2,1,0:T(8,128)S(1)} collective-permute-done((f32[4,16,64]{2,1,0:T(8,128)}, f32[4,16,64]{2,1,0:T(8,128)S(1)}, u32[]{:S(2)}, u32[]{:S(2)}) %collective-permute-start.18) | collective-permute-done | bytes 16416 | tf_op jit(solution)/shard_map/ppermute | solution.py:46
  225.8 1.6 shard_map.93
  227.4 10.6 %collective-permute-start.24 = (f32[1,1]{1,0:T(1,128)}, f32[1,1]{1,0:T(1,128)}, u32[]{:S(2)}, u32[]{:S(2)}) collective-permute-start(f32[1,1]{1,0:T(1,128)} %get-tuple-element.45), channel_id=1, source_target_pairs={{0,1},{1,0},{2,3},{3,2},{4,5},{5,4},{6,7},{7,6},{8,9},{9,8},{10,11... | collective-permute-start | bytes 20 | tf_op jit(solution)/shard_map/ppermute | solution.py:46
  238.0 1.1 copy-done.13
  239.0 1.1 copy-done.15
  240.1 1.1 copy-done.21
  241.2 1.1 copy-done.23
  242.3 1.1 copy-done.25
  243.3 1.1 copy-done.27
  245.1 1.8 shard_map.95
  247.0 1.1 copy-done.1
  248.1 1.1 copy-done.3
  249.1 1.1 copy-done.5
  250.2 1.1 copy-done.7
  251.3 1.1 copy-done.9
  252.4 1.1 copy-done.11
  256.1 15.1 %shard_map.96 = bf16[596,4096]{1,0:T(8,128)(2,1)} custom-call(bf16[596,1024]{1,0:T(8,128)(2,1)S(1)} %shard_map.94.ga_ref, bf16[596,1024]{1,0:T(8,128)(2,1)} %collective-permute-done.19.gb_ref, bf16[2,256,4096]{2,1,0:T(8,128)(2,1)} %maximum_maximum_fusion.t_ref.s_ref.refs_0_, bf16[2,256,4096]{2,1,0:T(8,128)(2,1)} %collective-permute-done.6.t_ref.s_ref.refs_1_, ...), custom_call_target="tpu_custom_call" | custom-call | flops 9999220736 | bytes 16777216 | tf_op jit(solution)/shard_map/pallas_call | solution.py:251
  (139 shorter events, 22.7 us)
Async XLA Ops:
  1.9 15.4 %collective-permute-start.1 = (bf16[2,64,4096]{2,1,0:T(8,128)(2,1)S(1)}, bf16[2,64,4096]{2,1,0:T(8,128)(2,1)S(1)}, u32[]{:S(2)}, u32[]{:S(2)}) collective-permute-start(bf16[2,64,4096]{2,1,0:T(8,128)(2,1)S(1)} %fusion), channel_id=1, source_target_pairs={{0,96},{1,25},{2,98},{3,27},{4,100},{5,29},{6,102},{7,31},{8,104},... | collective-permute-start | bytes 3145736 | tf_op jit(solution)/shard_map/ppermute | solution.py:46
  5.6 15.3 %collective-permute-start = (bf16[2,64,4096]{2,1,0:T(8,128)(2,1)S(1)}, bf16[2,64,4096]{2,1,0:T(8,128)(2,1)S(1)}, u32[]{:S(2)}, u32[]{:S(2)}) collective-permute-start(bf16[2,64,4096]{2,1,0:T(8,128)(2,1)S(1)} %fusion), channel_id=1, source_target_pairs={{0,32},{1,9},{2,34},{3,11},{4,36},{5,13},{6,38},{7,15},{8,40},{9,1... | collective-permute-start | bytes 3145736 | tf_op jit(solution)/shard_map/ppermute | solution.py:46
  17.4 9.6 %collective-permute-start.3 = (bf16[64,4096]{1,0:T(8,128)(2,1)S(1)}, bf16[64,4096]{1,0:T(8,128)(2,1)S(1)}, u32[]{:S(2)}, u32[]{:S(2)}) collective-permute-start(bf16[64,4096]{1,0:T(8,128)(2,1)S(1)} %slice_bitcast_fusion.2), channel_id=1, source_target_pairs={{0,96},{1,25},{2,98},{3,27},{4,100},{5,29},{6,102},{7,31},{8,104},... | collective-permute-start | bytes 1572872 | tf_op jit(solution)/shard_map/ppermute | solution.py:46
  20.9 9.6 %collective-permute-start.2 = (bf16[64,4096]{1,0:T(8,128)(2,1)S(1)}, bf16[64,4096]{1,0:T(8,128)(2,1)S(1)}, u32[]{:S(2)}, u32[]{:S(2)}) collective-permute-start(bf16[64,4096]{1,0:T(8,128)(2,1)S(1)} %slice_bitcast_fusion.3), channel_id=1, source_target_pairs={{0,32},{1,9},{2,34},{3,11},{4,36},{5,13},{6,38},{7,15},{8,40},{9,1... | collective-permute-start | bytes 1572872 | tf_op jit(solution)/shard_map/ppermute | solution.py:46
  30.5 7.9 %copy-start.46 = (s32[4]{0:T(128)S(1)}, s32[4]{0:T(128)}, u32[]{:S(2)}) copy-start(s32[4]{0:T(128)} %constant.123.clone) | copy-start | bytes 52
  30.5 8.2 %copy-start.44 = (s32[2048]{0:T(1024)S(1)}, s32[2048]{0:T(1024)}, u32[]{:S(2)}) copy-start(s32[2048]{0:T(1024)} %param.11) | copy-start | bytes 24580
  32.8 49.2 %collective-permute-start.6 = (bf16[2,256,4096]{2,1,0:T(8,128)(2,1)}, bf16[2,256,4096]{2,1,0:T(8,128)(2,1)}, u32[]{:S(2)}, u32[]{:S(2)}) collective-permute-start(bf16[2,256,4096]{2,1,0:T(8,128)(2,1)} %maximum_maximum_fusion.t_ref.s_ref.refs_0_), channel_id=1, source_target_pairs={{0,8},{1,33},{2,10},{3,35},{4,12},{5,37},{6,14},{7,39},{8,16},{9,4... | collective-permute-start | bytes 12582920 | tf_op jit(solution)/shard_map/ppermute | solution.py:46
  33.4 51.7 %collective-permute-start.7 = (bf16[2,256,4096]{2,1,0:T(8,128)(2,1)}, bf16[2,256,4096]{2,1,0:T(8,128)(2,1)}, u32[]{:S(2)}, u32[]{:S(2)}) collective-permute-start(bf16[2,256,4096]{2,1,0:T(8,128)(2,1)} %maximum_maximum_fusion.t_ref.s_ref.refs_0_), channel_id=1, source_target_pairs={{0,24},{1,97},{2,26},{3,99},{4,28},{5,101},{6,30},{7,103},{8,0},{9... | collective-permute-start | bytes 12582920 | tf_op jit(solution)/shard_map/ppermute | solution.py:46
  35.5 59.4 %collective-permute-start.4 = (bf16[596,4096]{1,0:T(8,128)(2,1)}, bf16[596,4096]{1,0:T(8,128)(2,1)}, u32[]{:S(2)}, u32[]{:S(2)}) collective-permute-start(bf16[596,4096]{1,0:T(8,128)(2,1)} %bitcast.11.ta_ref), channel_id=1, source_target_pairs={{0,1},{1,0},{2,3},{3,2},{4,5},{5,4},{6,7},{7,6},{8,9},{9,8},{10,11... | collective-permute-start | bytes 14647304 | tf_op jit(solution)/shard_map/ppermute | solution.py:46
  38.4 56.5 %collective-permute-start.5 = (bf16[596,4096]{1,0:T(8,128)(2,1)}, bf16[596,4096]{1,0:T(8,128)(2,1)}, u32[]{:S(2)}, u32[]{:S(2)}) collective-permute-start(bf16[596,4096]{1,0:T(8,128)(2,1)} %bitcast.12.sa_ref), channel_id=1, source_target_pairs={{0,1},{1,0},{2,3},{3,2},{4,5},{5,4},{6,7},{7,6},{8,9},{9,8},{10,11... | collective-permute-start | bytes 14647304 | tf_op jit(solution)/shard_map/ppermute | solution.py:46
  38.7 52.2 %copy-start.45 = (s32[16]{0:T(128)}, s32[16]{0:T(128)S(1)}, u32[]{:S(2)}) copy-start(s32[16]{0:T(128)S(1)} %select_n.131.place_ref) | copy-start | bytes 196
  85.1 76.2 %collective-permute-start.8 = (bf16[256,4096]{1,0:T(8,128)(2,1)}, bf16[256,4096]{1,0:T(8,128)(2,1)}, u32[]{:S(2)}, u32[]{:S(2)}) collective-permute-start(bf16[256,4096]{1,0:T(8,128)(2,1)} %slice_bitcast_fusion.1), channel_id=1, source_target_pairs={{0,8},{1,33},{2,10},{3,35},{4,12},{5,37},{6,14},{7,39},{8,16},{9,4... | collective-permute-start | bytes 6291464 | tf_op jit(solution)/shard_map/ppermute | solution.py:46
  88.2 72.8 %collective-permute-start.9 = (bf16[256,4096]{1,0:T(8,128)(2,1)}, bf16[256,4096]{1,0:T(8,128)(2,1)S(1)}, u32[]{:S(2)}, u32[]{:S(2)}) collective-permute-start(bf16[256,4096]{1,0:T(8,128)(2,1)} %slice_bitcast_fusion), channel_id=1, source_target_pairs={{0,24},{1,97},{2,26},{3,99},{4,28},{5,101},{6,30},{7,103},{8,0},{9... | collective-permute-start | bytes 6291464 | tf_op jit(solution)/shard_map/ppermute | solution.py:46
  90.9 165.2 %collective-permute-start.20 = (bf16[2,256,4096]{2,1,0:T(8,128)(2,1)}, bf16[2,256,4096]{2,1,0:T(8,128)(2,1)}, u32[]{:S(2)}, u32[]{:S(2)}) collective-permute-start(bf16[2,256,4096]{2,1,0:T(8,128)(2,1)} %maximum_maximum_fusion.t_ref.s_ref.refs_0_), channel_id=1, source_target_pairs={{0,1},{1,0},{2,3},{3,2},{4,5},{5,4},{6,7},{7,6},{8,9},{9,8},{10,11... | collective-permute-start | bytes 12582920 | tf_op jit(solution)/shard_map/ppermute | solution.py:46
  94.8 161.3 %collective-permute-start.21 = (bf16[2,256,4096]{2,1,0:T(8,128)(2,1)}, bf16[2,256,4096]{2,1,0:T(8,128)(2,1)}, u32[]{:S(2)}, u32[]{:S(2)}) collective-permute-start(bf16[2,256,4096]{2,1,0:T(8,128)(2,1)} %collective-permute-done.6.t_ref.s_ref.refs_1_), channel_id=1, source_target_pairs={{0,1},{1,0},{2,3},{3,2},{4,5},{5,4},{6,7},{7,6},{8,9},{9,8},{10,11... | collective-permute-start | bytes 12582920 | tf_op jit(solution)/shard_map/ppermute | solution.py:46
  94.9 161.2 %collective-permute-start.22 = (bf16[2,256,4096]{2,1,0:T(8,128)(2,1)}, bf16[2,256,4096]{2,1,0:T(8,128)(2,1)}, u32[]{:S(2)}, u32[]{:S(2)}) collective-permute-start(bf16[2,256,4096]{2,1,0:T(8,128)(2,1)} %collective-permute-done.7.t_ref.s_ref.refs_2_), channel_id=1, source_target_pairs={{0,1},{1,0},{2,3},{3,2},{4,5},{5,4},{6,7},{7,6},{8,9},{9,8},{10,11... | collective-permute-start | bytes 12582920 | tf_op jit(solution)/shard_map/ppermute | solution.py:46
  161.0 44.8 %copy-start.40 = (s32[2048]{0:T(1024)S(1)}, s32[2048]{0:T(1024)}, u32[]{:S(2)}) copy-start(s32[2048]{0:T(1024)} %param.12) | copy-start | bytes 24580
  161.0 95.1 %collective-permute-start.23 = (bf16[256,4096]{1,0:T(8,128)(2,1)S(1)}, bf16[256,4096]{1,0:T(8,128)(2,1)}, u32[]{:S(2)}, u32[]{:S(2)}) collective-permute-start(bf16[256,4096]{1,0:T(8,128)(2,1)S(1)} %collective-permute-done.9.s_ref.refs_3_), channel_id=1, source_target_pairs={{0,1},{1,0},{2,3},{3,2},{4,5},{5,4},{6,7},{7,6},{8,9},{9,8},{10,11... | collective-permute-start | bytes 6291464 | tf_op jit(solution)/shard_map/ppermute | solution.py:46
  184.9 4.2 %collective-permute-start.10 = (f32[4,16,64]{2,1,0:T(8,128)}, f32[4,16,64]{2,1,0:T(8,128)S(1)}, u32[]{:S(2)}, u32[]{:S(2)}) collective-permute-start(f32[4,16,64]{2,1,0:T(8,128)} %shard_map.90.refs_0_), channel_id=1, source_target_pairs={{0,32},{1,33},{2,34},{3,35},{4,36},{5,37},{6,38},{7,39},{8,40},{9,... | collective-permute-start | bytes 49160 | tf_op jit(solution)/shard_map/ppermute | solution.py:46
  189.1 7.5 %copy-start.35 = (f32[4,16,64]{2,1,0:T(8,128)}, f32[4,16,64]{2,1,0:T(8,128)S(1)}, u32[]{:S(2)}) copy-start(f32[4,16,64]{2,1,0:T(8,128)S(1)} %collective-permute-done.10.refs_1_) | copy-start | bytes 49156
  189.1 3.0 %collective-permute-start.11 = (f32[4,16,64]{2,1,0:T(8,128)}, f32[4,16,64]{2,1,0:T(8,128)S(1)}, u32[]{:S(2)}, u32[]{:S(2)}) collective-permute-start(f32[4,16,64]{2,1,0:T(8,128)} %shard_map.90.refs_0_), channel_id=1, source_target_pairs={{0,96},{1,97},{2,98},{3,99},{4,100},{5,101},{6,102},{7,103},{8,104... | collective-permute-start | bytes 49160 | tf_op jit(solution)/shard_map/ppermute | solution.py:46
  192.1 4.5 %copy-start.37 = (f32[4,16,64]{2,1,0:T(8,128)}, f32[4,16,64]{2,1,0:T(8,128)S(1)}, u32[]{:S(2)}) copy-start(f32[4,16,64]{2,1,0:T(8,128)S(1)} %collective-permute-done.11.refs_2_) | copy-start | bytes 49156
  192.1 4.5 %collective-permute-start.12 = (f32[4,16,64]{2,1,0:T(8,128)}, f32[4,16,64]{2,1,0:T(8,128)S(1)}, u32[]{:S(2)}, u32[]{:S(2)}) collective-permute-start(f32[4,16,64]{2,1,0:T(8,128)} %shard_map.90.refs_0_), channel_id=1, source_target_pairs={{0,64},{1,65},{2,66},{3,67},{4,68},{5,69},{6,70},{7,71},{8,72},{9,... | collective-permute-start | bytes 49160 | tf_op jit(solution)/shard_map/ppermute | solution.py:46
  198.6 4.2 %collective-permute-start.13 = (f32[4,16,64]{2,1,0:T(8,128)}, f32[4,16,64]{2,1,0:T(8,128)S(1)}, u32[]{:S(2)}, u32[]{:S(2)}) collective-permute-start(f32[4,16,64]{2,1,0:T(8,128)} %shard_map.91.refs_0_), channel_id=1, source_target_pairs={{0,8},{1,9},{2,10},{3,11},{4,12},{5,13},{6,14},{7,15},{8,16},{9,17... | collective-permute-start | bytes 49160 | tf_op jit(solution)/shard_map/ppermute | solution.py:46
  202.8 7.5 %copy-start.34 = (f32[4,16,64]{2,1,0:T(8,128)}, f32[4,16,64]{2,1,0:T(8,128)S(1)}, u32[]{:S(2)}) copy-start(f32[4,16,64]{2,1,0:T(8,128)S(1)} %collective-permute-done.13.refs_1_) | copy-start | bytes 49156
  202.8 3.0 %collective-permute-start.14 = (f32[4,16,64]{2,1,0:T(8,128)}, f32[4,16,64]{2,1,0:T(8,128)S(1)}, u32[]{:S(2)}, u32[]{:S(2)}) collective-permute-start(f32[4,16,64]{2,1,0:T(8,128)} %shard_map.91.refs_0_), channel_id=1, source_target_pairs={{0,24},{1,25},{2,26},{3,27},{4,28},{5,29},{6,30},{7,31},{8,0},{9,1... | collective-permute-start | bytes 49160 | tf_op jit(solution)/shard_map/ppermute | solution.py:46
  205.8 4.5 %copy-start.36 = (f32[4,16,64]{2,1,0:T(8,128)}, f32[4,16,64]{2,1,0:T(8,128)S(1)}, u32[]{:S(2)}) copy-start(f32[4,16,64]{2,1,0:T(8,128)S(1)} %collective-permute-done.14.refs_2_) | copy-start | bytes 49156
  205.8 4.5 %collective-permute-start.15 = (f32[4,16,64]{2,1,0:T(8,128)}, f32[4,16,64]{2,1,0:T(8,128)S(1)}, u32[]{:S(2)}, u32[]{:S(2)}) collective-permute-start(f32[4,16,64]{2,1,0:T(8,128)} %shard_map.91.refs_0_), channel_id=1, source_target_pairs={{0,16},{1,17},{2,18},{3,19},{4,20},{5,21},{6,22},{7,23},{8,24},{9,... | collective-permute-start | bytes 49160 | tf_op jit(solution)/shard_map/ppermute | solution.py:46
  212.3 5.3 %collective-permute-start.16 = (f32[4,16,64]{2,1,0:T(8,128)}, f32[4,16,64]{2,1,0:T(8,128)S(1)}, u32[]{:S(2)}, u32[]{:S(2)}) collective-permute-start(f32[4,16,64]{2,1,0:T(8,128)} %shard_map.92.refs_0_), channel_id=1, source_target_pairs={{0,2},{1,3},{2,4},{3,5},{4,6},{5,7},{6,0},{7,1},{8,10},{9,11},{10,... | collective-permute-start | bytes 49160 | tf_op jit(solution)/shard_map/ppermute | solution.py:46
  214.0 11.2 %copy-start.33 = (f32[16,1,64]{2,1,0:T(1,128)}, f32[16,1,64]{2,1,0:T(1,128)S(1)}, u32[]{:S(2)}) copy-start(f32[16,1,64]{2,1,0:T(1,128)S(1)} %constant_dynamic-slice_fusion) | copy-start | bytes 12292
  217.6 7.6 %copy-start.41 = (f32[4,16,64]{2,1,0:T(8,128)}, f32[4,16,64]{2,1,0:T(8,128)S(1)}, u32[]{:S(2)}) copy-start(f32[4,16,64]{2,1,0:T(8,128)S(1)} %collective-permute-done.16.refs_1_) | copy-start | bytes 49156
  217.6 3.0 %collective-permute-start.17 = (f32[4,16,64]{2,1,0:T(8,128)}, f32[4,16,64]{2,1,0:T(8,128)S(1)}, u32[]{:S(2)}, u32[]{:S(2)}) collective-permute-start(f32[4,16,64]{2,1,0:T(8,128)} %shard_map.92.refs_0_), channel_id=1, source_target_pairs={{0,6},{1,7},{2,0},{3,1},{4,2},{5,3},{6,4},{7,5},{8,14},{9,15},{10,... | collective-permute-start | bytes 49160 | tf_op jit(solution)/shard_map/ppermute | solution.py:46
  220.6 4.6 %copy-start.42 = (f32[4,16,64]{2,1,0:T(8,128)}, f32[4,16,64]{2,1,0:T(8,128)S(1)}, u32[]{:S(2)}) copy-start(f32[4,16,64]{2,1,0:T(8,128)S(1)} %collective-permute-done.17.refs_2_) | copy-start | bytes 49156
  220.6 4.6 %collective-permute-start.18 = (f32[4,16,64]{2,1,0:T(8,128)}, f32[4,16,64]{2,1,0:T(8,128)S(1)}, u32[]{:S(2)}, u32[]{:S(2)}) collective-permute-start(f32[4,16,64]{2,1,0:T(8,128)} %shard_map.92.refs_0_), channel_id=1, source_target_pairs={{0,4},{1,5},{2,6},{3,7},{4,0},{5,1},{6,2},{7,3},{8,12},{9,13},{10,... | collective-permute-start | bytes 49160 | tf_op jit(solution)/shard_map/ppermute | solution.py:46
  227.4 19.6 %collective-permute-start.24 = (f32[1,1]{1,0:T(1,128)}, f32[1,1]{1,0:T(1,128)}, u32[]{:S(2)}, u32[]{:S(2)}) collective-permute-start(f32[1,1]{1,0:T(1,128)} %get-tuple-element.45), channel_id=1, source_target_pairs={{0,1},{1,0},{2,3},{3,2},{4,5},{5,4},{6,7},{7,6},{8,9},{9,8},{10,11... | collective-permute-start | bytes 20 | tf_op jit(solution)/shard_map/ppermute | solution.py:46
  238.0 1.1 copy-start.13
  239.0 1.1 copy-start.15
  240.1 1.1 copy-start.21
  241.2 1.1 copy-start.23
  242.3 1.1 copy-start.25
  243.3 1.1 copy-start.27
  245.1 1.9 copy-start.17
  245.1 1.9 copy-start.19
  247.0 9.1 %collective-permute-start.19 = (bf16[596,1024]{1,0:T(8,128)(2,1)}, bf16[596,1024]{1,0:T(8,128)(2,1)}, u32[]{:S(2)}, u32[]{:S(2)}) collective-permute-start(bf16[596,1024]{1,0:T(8,128)(2,1)} %shard_map.95), channel_id=1, source_target_pairs={{0,1},{1,0},{2,3},{3,2},{4,5},{5,4},{6,7},{7,6},{8,9},{9,8},{10,11... | collective-permute-start | bytes 3661832 | tf_op jit(solution)/shard_map/ppermute | solution.py:46
  247.0 1.1 copy-start.1
  248.1 1.1 copy-start.3
  249.1 1.1 copy-start.5
  250.2 1.1 copy-start.7
  (24 other events, 18.7 us)

commit v2 on v1

--- a/solution.py
+++ b/solution.py
@@ -78,65 +78,44 @@
     return nt_all, ns_all, mean, add_all([p[3] for p in parts])
 
 
-def logits_kernel(steps, first_ref, ids_ref, t_ref, s_ref, ta_ref, sa_ref, tb_ref, sb_ref,
-                  oas_ref, oau_ref, obs_ref, obu_ref, st_ref):
-    k = pl.program_id(0)
-    t_hid = t_ref[0] if len(t_ref.shape) == 3 else t_ref[...]
-    s_hid = s_ref[0] if len(s_ref.shape) == 3 else s_ref[...]
-    for head, hid, out in ((sa_ref, s_hid, oas_ref), (ta_ref, t_hid, oau_ref),
-                           (sb_ref, s_hid, obs_ref), (tb_ref, t_hid, obu_ref)):
-        part = nt(head[...], hid)
-
-        @pl.when(k == 0)
-        def _():
-            out[...] = part
-
-        @pl.when(k > 0)
-        def _():
-            out[...] += part
-
-    @pl.when(k == steps - 1)
-    def _():
-        parts = []
-        for i, (so, uo) in enumerate(((oas_ref, oau_ref), (obs_ref, obu_ref))):
-            s, t = so[...], uo[...]
-            rows = lax.broadcasted_iota(jnp.int32, s.shape, 0) + first_ref[i]
-            u, part = stats_of(s, t, rows == ids_ref[...])
-            uo[...] = u
-            parts.append(part)
-        total = join(parts)
-        tokens = total[0].shape[1] // SIDE
-        for q in range(4):
-            for b in range(SIDE):
-                st_ref[b, q:q + 1, :] = total[q][:, b * tokens:(b + 1) * tokens]
-
-
-def logits_call(firsts, ids, stack, heads, t_alone=None, s_alone=None):
-    ta, sa, tb, sb = heads
-    vocab, depth = ta.shape
-    tile = 1024
-    steps = depth // tile
-    if t_alone is None:
-        tokens = stack.shape[1]
-        hids = [stack, stack]
-        hid_specs = [pl.BlockSpec((1, tokens, tile), lambda k, j=j: (j, 0, k)) for j in range(2)]
-    else:
-        tokens = t_alone.shape[0]
-        hids = [t_alone, s_alone]
-        hid_specs = [pl.BlockSpec((tokens, tile), lambda k: (0, k))] * 2
-    head_spec = pl.BlockSpec((vocab, tile), lambda k: (0, k))
-    out = jax.ShapeDtypeStruct((vocab, tokens), F32)
-    whole = pl.BlockSpec((vocab, tokens), lambda k: (0, 0))
-    return pl.pallas_call(
-        functools.partial(logits_kernel, steps),
-        grid=(steps,),
-        in_specs=[pl.BlockSpec(memory_space=pltpu.SMEM), pl.BlockSpec((1, tokens), lambda k: (0, 0))]
-        + hid_specs + [head_spec] * 4,
-        out_specs=[whole] * 4 + [pl.BlockSpec((SIDE, 4, tokens // SIDE), lambda k: (0, 0, 0))],
-        out_shape=[out] * 4 + [jax.ShapeDtypeStruct((SIDE, 4, tokens // SIDE), F32)],
-        compiler_params=pltpu.CompilerParams(vmem_limit_bytes=32 * MIB),
+def logits_kernel(first_ref, ids_ref, t_ref, s_ref, ta_ref, sa_ref, tb_ref, sb_ref, *refs):
+    *_, out_ref, st_ref, held, sems = refs
+    parts, copies = [], []
+    for i, (sh, th) in enumerate(((sa_ref, ta_ref), (sb_ref, tb_ref))):
+        held[2 * i] = nt(sh[...], s_ref[...])
+        held[2 * i + 1] = nt(th[...], t_ref[...])
+        s, t = held[2 * i], held[2 * i + 1]
+        rows = lax.broadcasted_iota(jnp.int32, s.shape, 0) + first_ref[i]
+        u, part = stats_of(s, t, rows == ids_ref[...])
+        held[2 * i + 1] = u
+        parts.append(part)
+        copies.append(pltpu.make_async_copy(held.at[pl.ds(2 * i, 2)], out_ref.at[pl.ds(2 * i, 2)], sems.at[i]))
+        copies[-1].start()
+    total = join(parts)
+    tokens = total[0].shape[1] // SIDE
+    for q in range(4):
+        for b in range(SIDE):
+            st_ref[b, q:q + 1, :] = total[q][:, b * tokens:(b + 1) * tokens]
+    for copy in copies:
+        copy.wait()
+
+
+def logits_call(firsts, ids, t_hid, s_hid, heads, after=()):
+    vocab, depth = heads[0].shape
+    tokens = t_hid.shape[0]
+    vmem = pl.BlockSpec(memory_space=pltpu.VMEM)
+    return pl.pallas_call(
+        logits_kernel,
+        in_specs=[pl.BlockSpec(memory_space=pltpu.SMEM)] + [vmem] * 7 + [pl.BlockSpec(memory_space=pl.ANY)] * len(after),
+        out_specs=[pl.BlockSpec(memory_space=pltpu.HBM), vmem],
+        out_shape=[
+            pltpu.HBM((4, vocab, tokens), F32),
+            jax.ShapeDtypeStruct((SIDE, 4, tokens // SIDE), F32),
+        ],
+        scratch_shapes=[pltpu.VMEM((4, vocab, tokens), F32), pltpu.SemaphoreType.DMA((2,))],
+        compiler_params=pltpu.CompilerParams(vmem_limit_bytes=20 * MIB),
         cost_estimate=pl.CostEstimate(flops=8 * vocab * tokens * depth, bytes_accessed=8 * vocab * depth, transcendentals=0),
-    )(firsts, ids, *hids, ta, sa, tb, sb)
+    )(firsts, ids, t_hid, s_hid, *heads, *after)
 
 
 def order_kernel(place_ref, *refs):
@@ -148,6 +127,9 @@
                 out_ref[q, pl.ds(b, 1), :] = group[i, q:q + 1, :]
 
 
+SMALL = pltpu.CompilerParams(vmem_limit_bytes=4 * MIB)
+
+
 def order_call(place, groups):
     tokens = groups[0].shape[-1]
     return pl.pallas_call(
@@ -155,6 +137,7 @@
         in_specs=[pl.BlockSpec(memory_space=pltpu.SMEM)] + [pl.BlockSpec(memory_space=pltpu.VMEM)] * len(groups),
         out_specs=pl.BlockSpec(memory_space=pltpu.VMEM),
         out_shape=jax.ShapeDtypeStruct((4, SIDE * SIDE, tokens), F32),
+        compiler_params=SMALL,
     )(place, *groups)
 
 
@@ -172,6 +155,7 @@
         in_specs=[vmem] * len(parts),
         out_specs=vmem,
         out_shape=jax.ShapeDtypeStruct(parts[0].shape, F32),
+        compiler_params=SMALL,
     )(*parts)
 
 
@@ -198,32 +182,38 @@
         out_specs=[vmem, vmem],
         out_shape=[jax.ShapeDtypeStruct((SIDE, 4, SIDE * tokens), F32), jax.ShapeDtypeStruct((1, 1), F32)],
         scratch_shapes=[pltpu.VMEM((4, SIDE * SIDE, tokens), F32)],
+        compiler_params=SMALL,
     )(place, factor, weight, *parts)
 
 
-def grad_kernel(first_ref, ids_ref, coef_ref, *refs):
-    *ins, out_ref = refs
+def grad_kernel(part, first_ref, ids_ref, coef_ref, *refs):
+    *ins, out_ref, held, sems = refs
+    copies = [pltpu.make_async_copy(ref.at[pl.ds(2 * part, 2)], held.at[j], sems.at[j]) for j, ref in enumerate(ins)]
+    for copy in copies:
+        copy.start()
+    tokens = held.shape[3]
     for j in range(SIDE):
-        s, u = ins[2 * j][...], ins[2 * j + 1][...]
+        copies[j].wait()
+        s, u = held[j, 0], held[j, 1]
         n_s, factor, shift, pull = (coef_ref[j, q:q + 1, :] for q in range(4))
-        rows = lax.broadcasted_iota(jnp.int32, s.shape, 0) + first_ref[0]
+        rows = lax.broadcasted_iota(jnp.int32, s.shape, 0) + first_ref[part]
         inner = jnp.exp(s - n_s) * (u + shift)
         inner = inner - jnp.where(rows == ids_ref[j:j + 1, :], pull, 0.0)
-        tokens = s.shape[1]
         out_ref[:, j * tokens:(j + 1) * tokens] = (factor * inner).astype(jnp.bfloat16)
 
 
-def grad_call(first_row, ids, coef, logits):
-    vocab, tokens = logits[0].shape
+def grad_call(part, firsts, ids, coef, logits):
+    _, vocab, tokens = logits[0].shape
     vmem = pl.BlockSpec(memory_space=pltpu.VMEM)
     return pl.pallas_call(
-        grad_kernel,
-        in_specs=[pl.BlockSpec(memory_space=pltpu.SMEM)] + [vmem] * (2 + len(logits)),
+        functools.partial(grad_kernel, part),
+        in_specs=[pl.BlockSpec(memory_space=pltpu.SMEM), vmem, vmem] + [pl.BlockSpec(memory_space=pltpu.HBM)] * SIDE,
         out_specs=vmem,
         out_shape=jax.ShapeDtypeStruct((vocab, SIDE * tokens), jnp.bfloat16),
-        compiler_params=pltpu.CompilerParams(vmem_limit_bytes=32 * MIB),
+        scratch_shapes=[pltpu.VMEM((SIDE, 2, vocab, tokens), F32), pltpu.SemaphoreType.DMA((SIDE,))],
+        compiler_params=pltpu.CompilerParams(vmem_limit_bytes=16 * MIB),
         cost_estimate=pl.CostEstimate(flops=10 * vocab * tokens * SIDE, bytes_accessed=10 * vocab * tokens * SIDE, transcendentals=0),
-    )(first_row, ids, coef, *logits)
+    )(firsts, ids, coef, *[pltpu.with_memory_space_constraint(a, pltpu.HBM) for a in logits])
 
 
 def head_kernel(ga_ref, gb_ref, *refs):
@@ -254,9 +244,9 @@
         in_specs=[whole, whole] + specs,
         out_specs=pl.BlockSpec((vocab, tile), lambda i: (0, i)),
         out_shape=jax.ShapeDtypeStruct((vocab, depth), jnp.bfloat16),
-        compiler_params=pltpu.CompilerParams(vmem_limit_bytes=32 * MIB),
+        compiler_params=pltpu.CompilerParams(vmem_limit_bytes=16 * MIB),
         cost_estimate=pl.CostEstimate(flops=4 * vocab * tokens * depth, bytes_accessed=4 * tokens * depth, transcendentals=0),
-    )(ga, gb, *hids)
+    )(ga, gb, *[pltpu.with_memory_space_constraint(a, pltpu.HBM) for a in hids])
 
 
 def local(teacher_hidden, student_hidden, teacher_head, student_head, sampled_ids, valid_mask):
@@ -267,7 +257,6 @@
 
     ta, sa = teacher_head.T, student_head.T
     tb, sb = send(ta, SIBLING), send(sa, SIBLING)
-    heads = (ta, sa, tb, sb)
 
     shift = jnp.array([o % SIDE for o in OFFSETS], jnp.int32)
     one = (jnp.where(core == 0, x, y) + shift) % SIDE
@@ -289,31 +278,37 @@
     own = lax.dynamic_slice_in_dim(jnp.stack([teacher_hidden, student_hidden]), core * half, half, 1)
     low, high = send(own, first(1)), send(own, first(-1))
     far_t, far_s = send(low[0], first(1)), send(high[1], first(-1))
-    far = jnp.stack([far_t, far_s])
-    row = jnp.concatenate([own, low, high, far], axis=1)
-    row_low, row_high = send(row, second(1)), send(row, second(-1))
-    far_t, far_s = send(row_low[0], second(1)), send(row_high[1], second(-1))
-
-    groups = [
-        logits_call(firsts, ids[0:1], row, heads),
-        logits_call(firsts, ids[1:2], row_low, heads),
-        logits_call(firsts, ids[2:3], row_high, heads),
-        logits_call(firsts, ids[3:4], None, heads, far_t, far_s),
-    ]
-    students = [row, row_low, row_high, far_s]
-    others = [send(h, SIBLING) for h in students]
-
-    total = order_call(place, [g[4] for g in groups])
+    far_t, far_s, tb, sb = lax.optimization_barrier((far_t, far_s, tb, sb))
+    heads = (ta, sa, tb, sb)
+    row_t = jnp.concatenate([own[0], low[0], high[0], far_t], axis=0)
+    row_s = jnp.concatenate([own[1], low[1], high[1], far_s], axis=0)
+    low_t, high_s = send(row_t, second(1)), send(row_s, second(-1))
+    high_t, low_s = send(row_t, second(-1)), send(row_s, second(1))
+    group0 = logits_call(firsts, ids[0:1], row_t, row_s, heads)
+    other0 = send(row_s, SIBLING)
+    low_t, high_s, other0, *group0 = lax.optimization_barrier((low_t, high_s, other0, *group0))
+    far_t, far_s = send(low_t, second(1)), send(high_s, second(-1))
+    other1, other2 = send(low_s, SIBLING), send(high_s, SIBLING)
+    group1 = logits_call(firsts, ids[1:2], low_t, low_s, heads)
+    group2 = logits_call(firsts, ids[2:3], high_t, high_s, heads)
+    group3 = logits_call(firsts, ids[3:4], far_t, far_s, heads, (group1[1], group2[1], other1, other2))
+    other3 = send(far_s, SIBLING)
+    groups = [group0, group1, group2, group3]
+    students = [row_s, low_s, high_s, far_s]
+    others = [other0, other1, other2, other3]
+
+    total = order_call(place, [g[1] for g in groups])
     for axis in range(3):
         parts = [total, send(total, along(axis, 1)), send(total, along(axis, -1)), send(total, along(axis, 2))]
         if axis < 2:
             total = join_call(parts)
     coef, kl = finish_call(place, factor, weights, parts)
 
-    away = grad_call(firsts[1:], ids, coef, [a for g in groups for a in g[2:4]])
+    logits = [g[0] for g in groups]
+    away = grad_call(1, firsts, ids, coef, logits)
     arrived = send(away, SIBLING)
+    kept = grad_call(0, firsts, ids, coef, logits)
     kl = kl + send(kl, SIBLING)
-    kept = grad_call(firsts[:1], ids, coef, [a for g in groups for a in g[0:2]])
     head_grad = head_call(kept, arrived, students + others).T
     return head_grad, kl[0, 0] / token_count
 

time: 274 us -> 184 us (0.67)
  waiting for transfers between devices: 93.2 us -> 55.9 us
  local copies, waits for them, and re-layouts: 37.3 us -> 11.3 us
  Pallas kernels: 97.1 us -> 71.4 us
    ppermute x25 -> x27, waiting for transfers between devices: 93.2 us -> 55.9 us  [send(): return lax.ppermute(array, AXES, perm)]
    pallas_call x6, Pallas kernels: 76 us -> 53.7 us  [the longest x4 47.4 us: logits_call(): pl.pallas_call(logits_kernel, in_specs=[pl.BlockSpec(memory_space=pltpu.S...]
    unnamed x94 -> x18, local copies, waits for them, and re-layouts: 29.4 us -> 9.59 us
    squeeze x4 -> x3, local copies, waits for them, and re-layouts: 6.34 us -> 0.21 us  [the longest x2 0.14 us: local(): row_s = jnp.concatenate([own[1], low[1], high[1], far_s], axis=0)]
    pallas_call x2, Pallas kernels: 2.91 us -> 0.09 us  [join_call(): pl.pallas_call(join_kernel, in_specs=[vmem] * len(parts), out_specs=vmem,...]
    ppermute x25 -> x27, starting transfers between devices: 35.2 us -> 36.1 us  [send(): return lax.ppermute(array, AXES, perm)]
  transfers between devices with their start and end apart: 25 -> 27, of which waited for: 13 -> 7; matrix products, arithmetic and copies ran while one was open for 3% -> 3% of each run, Pallas kernels for 30% -> 30%
where the time goes in v2:
time: 184 us; the launch traced here: 183 us
  Pallas kernels  71.4 us (39%)
  waiting for transfers between devices  55.9 us (30%)
  starting transfers between devices  36.1 us (20%)
  local copies, waits for them, and re-layouts  11.3 us (6%)
  between operations  4.69 us (3%)
  other arithmetic  3.8 us (2%)
    ppermute x27, waiting for transfers between devices, send(): return lax.ppermute(array, AXES, perm)  55.9 us
    pallas_call x4, Pallas kernels, logits_call(): pl.pallas_call(logits_kernel, in_specs=[pl.BlockSpec(memory_space=pltpu.S...  47.4 us
    ppermute x27, starting transfers between devices, send(): return lax.ppermute(array, AXES, perm)  36.1 us
    pallas_call x1, Pallas kernels, head_call(): pl.pallas_call(head_kernel, grid=(depth // tile,), in_specs=[whole, whole...  15.8 us
    unnamed x18, local copies, waits for them, and re-layouts  9.59 us
    pallas_call x2, Pallas kernels, grad_call(): pl.pallas_call(functools.partial(grad_kernel, part), in_specs=[pl.BlockSp...  6.37 us
  transfers between devices with their start and end apart: 27, of which 7 were waited for; matrix products, arithmetic and copies ran while one was open for 3% of the time, Pallas kernels for 30%

profile of v2, /device:TPU:1, one launch (start us, length us, event | category | flops | bytes accessed | tf_op | source)
XLA Modules:
  0.0 183.2 jit_solution(4644084877541494462)
XLA Ops:
  0.6 1.5 collective-permute-start.4
  2.1 0.1 collective-permute-start.5
  2.2 1.3 fusion
  3.5 1.4 collective-permute-start
  4.9 1.5 collective-permute-start.1
  6.5 12.4 %collective-permute-done = bf16[2,64,4096]{2,1,0:T(8,128)(2,1)S(1)} collective-permute-done((bf16[2,64,4096]{2,1,0:T(8,128)(2,1)S(1)}, bf16[2,64,4096]{2,1,0:T(8,128)(2,1)S(1)}, u32[]{:S(2)}, u32[]{:S(2)}) %collective-permute-start) | collective-permute-done | bytes 1048608 | tf_op jit(solution)/shard_map/ppermute | solution.py:46
  19.1 2.7 %collective-permute-start.3 = (bf16[64,4096]{1,0:T(8,128)(2,1)S(1)}, bf16[64,4096]{1,0:T(8,128)(2,1)S(1)}, u32[]{:S(2)}, u32[]{:S(2)}) collective-permute-start(bf16[64,4096]{1,0:T(8,128)(2,1)S(1)} %get-tuple-element.51), channel_id=1, source_target_pairs={{0,96},{1,25},{2,98},{3,27},{4,100},{5,29},{6,102},{7,31},{8,104},... | collective-permute-start | bytes 1572872 | tf_op jit(solution)/shard_map/ppermute | solution.py:46
  21.9 6.6 %collective-permute-done.2 = bf16[64,4096]{1,0:T(8,128)(2,1)S(1)} collective-permute-done((bf16[64,4096]{1,0:T(8,128)(2,1)S(1)}, bf16[64,4096]{1,0:T(8,128)(2,1)S(1)}, u32[]{:S(2)}, u32[]{:S(2)}) %collective-permute-start.2) | collective-permute-done | bytes 524320 | tf_op jit(solution)/shard_map/ppermute | solution.py:46
  28.6 0.1 pad_maximum_fusion.1.s_ref.refs_0_
  28.7 2.5 %collective-permute-start.7 = (bf16[256,4096]{1,0:T(8,128)(2,1)S(1)}, bf16[256,4096]{1,0:T(8,128)(2,1)}, u32[]{:S(2)}, u32[]{:S(2)}) collective-permute-start(bf16[256,4096]{1,0:T(8,128)(2,1)S(1)} %pad_maximum_fusion.1.s_ref.refs_0_), channel_id=1, source_target_pairs={{0,24},{1,97},{2,26},{3,99},{4,28},{5,101},{6,30},{7,103},{8,0},{9... | collective-permute-start | bytes 6291464 | tf_op jit(solution)/shard_map/ppermute | solution.py:46
  31.3 2.6 %collective-permute-start.8 = (bf16[256,4096]{1,0:T(8,128)(2,1)S(1)}, bf16[256,4096]{1,0:T(8,128)(2,1)}, u32[]{:S(2)}, u32[]{:S(2)}) collective-permute-start(bf16[256,4096]{1,0:T(8,128)(2,1)S(1)} %pad_maximum_fusion.1.s_ref.refs_0_), channel_id=1, source_target_pairs={{0,1},{1,0},{2,3},{3,2},{4,5},{5,4},{6,7},{7,6},{8,9},{9,8},{10,11... | collective-permute-start | bytes 6291464 | tf_op jit(solution)/shard_map/ppermute | solution.py:46
  33.9 0.4 collective-permute-start.9
  34.3 1.5 pad_maximum_fusion.t_ref
  35.8 0.9 collective-permute-start.6
  37.1 0.6 gather_fusion
  37.9 1.8 collective-permute-start.10
  39.7 2.4 %copy-done = bf16[4096,596]{0,1:T(8,128)(2,1)S(1)} copy-done((bf16[4096,596]{0,1:T(8,128)(2,1)S(1)}, bf16[4096,596]{0,1:T(8,128)(2,1)}, u32[]{:S(2)}) %copy-start) | copy-done | bytes 4882456
  42.1 2.4 %copy-done.2 = bf16[4096,596]{0,1:T(8,128)(2,1)S(1)} copy-done((bf16[4096,596]{0,1:T(8,128)(2,1)S(1)}, bf16[4096,596]{0,1:T(8,128)(2,1)}, u32[]{:S(2)}) %copy-start.2) | copy-done | bytes 4882456
  44.5 11.1 %shard_map.86 = (f32[4,596,256]{2,1,0:T(8,128)}, f32[4,4,64]{2,1,0:T(4,128)S(1)}) custom-call(s32[2]{0:T(128)S(1)} %pad_add_fusion.first_ref, s32[1,256]{1,0:T(1,128)S(1)} %slice.51.ids_ref, bf16[256,4096]{1,0:T(8,128)(2,1)} %pad_maximum_fusion.t_ref, bf16[256,4096]{1,0:T(8,128)(2,1)S(1)} %pad_maximum_fusion.1.s_ref.refs_0_, bf16[596,4096]{1,0:T(8,128)(2,1)S(1)} %bitcast.25, ...), custom_call_target="tpu_custom_call" | custom-call | flops 4999610368 | bytes 19529728 | tf_op jit(solution)/shard_map/pallas_call | solution.py:107
  55.7 27.6 %collective-permute-done.6.t_ref = bf16[256,4096]{1,0:T(8,128)(2,1)} collective-permute-done((bf16[256,4096]{1,0:T(8,128)(2,1)}, bf16[256,4096]{1,0:T(8,128)(2,1)}, u32[]{:S(2)}, u32[]{:S(2)}) %collective-permute-start.6) | collective-permute-done | bytes 2097184 | tf_op jit(solution)/shard_map/ppermute | solution.py:46
  83.2 1.5 collective-permute-start.12
  84.7 1.0 collective-permute-start.13
  86.1 0.6 convert_reduce_fusion
  86.7 2.4 %copy-done.1 = bf16[4096,596]{0,1:T(8,128)(2,1)S(1)} copy-done((bf16[4096,596]{0,1:T(8,128)(2,1)S(1)}, bf16[4096,596]{0,1:T(8,128)(2,1)}, u32[]{:S(2)}) %copy-start.1) | copy-done | bytes 4882456
  89.1 2.4 %copy-done.3 = bf16[4096,596]{0,1:T(8,128)(2,1)S(1)} copy-done((bf16[4096,596]{0,1:T(8,128)(2,1)S(1)}, bf16[4096,596]{0,1:T(8,128)(2,1)}, u32[]{:S(2)}) %copy-start.3) | copy-done | bytes 4882456
  91.4 11.8 %shard_map.87 = (f32[4,596,256]{2,1,0:T(8,128)}, f32[4,4,64]{2,1,0:T(4,128)S(1)}) custom-call(s32[2]{0:T(128)S(1)} %pad_add_fusion.first_ref, s32[1,256]{1,0:T(1,128)S(1)} %slice.53.ids_ref, bf16[256,4096]{1,0:T(8,128)(2,1)} %collective-permute-done.6.t_ref, bf16[256,4096]{1,0:T(8,128)(2,1)} %collective-permute-done.9.s_ref.refs_1_, ...), custom_call_target="tpu_custom_call" | custom-call | flops 4999610368 | bytes 19529728 | tf_op jit(solution)/shard_map/pallas_call | solution.py:107
  103.3 11.8 %shard_map.88 = (f32[4,596,256]{2,1,0:T(8,128)}, f32[4,4,64]{2,1,0:T(4,128)S(1)}) custom-call(s32[2]{0:T(128)S(1)} %pad_add_fusion.first_ref, s32[1,256]{1,0:T(1,128)S(1)} %slice.55.ids_ref, bf16[256,4096]{1,0:T(8,128)(2,1)} %collective-permute-done.10.t_ref, bf16[256,4096]{1,0:T(8,128)(2,1)} %collective-permute-done.7.s_ref.refs_2_, ...), custom_call_target="tpu_custom_call" | custom-call | flops 4999610368 | bytes 19529728 | tf_op jit(solution)/shard_map/pallas_call | solution.py:107
  115.1 0.3 collective-permute-start.25
  115.5 12.5 %shard_map.89 = (f32[4,596,256]{2,1,0:T(8,128)}, f32[4,4,64]{2,1,0:T(4,128)S(1)}) custom-call(s32[2]{0:T(128)S(1)} %pad_add_fusion.first_ref, s32[1,256]{1,0:T(1,128)S(1)} %slice.57.ids_ref, bf16[256,4096]{1,0:T(8,128)(2,1)} %collective-permute-done.11.t_ref, bf16[256,4096]{1,0:T(8,128)(2,1)} %collective-permute-done.12.s_ref.refs_3_, ...), custom_call_target="tpu_custom_call" | custom-call | flops 4999610368 | bytes 19529728 | tf_op jit(solution)/shard_map/pallas_call | solution.py:107
  128.1 0.6 shard_map.90.refs_0_
  128.6 0.5 collective-permute-start.15
  129.1 2.8 %collective-permute-start.16 = (f32[4,16,64]{2,1,0:T(8,128)S(1)}, f32[4,16,64]{2,1,0:T(8,128)S(1)}, u32[]{:S(2)}, u32[]{:S(2)}) collective-permute-start(f32[4,16,64]{2,1,0:T(8,128)S(1)} %shard_map.90.refs_0_), channel_id=1, source_target_pairs={{0,96},{1,97},{2,98},{3,99},{4,100},{5,101},{6,102},{7,103},{8,104... | collective-permute-start | bytes 49160 | tf_op jit(solution)/shard_map/ppermute | solution.py:46
  131.9 1.1 collective-permute-start.17
  133.7 2.4 %collective-permute-done.17.refs_3_ = f32[4,16,64]{2,1,0:T(8,128)S(1)} collective-permute-done((f32[4,16,64]{2,1,0:T(8,128)S(1)}, f32[4,16,64]{2,1,0:T(8,128)S(1)}, u32[]{:S(2)}, u32[]{:S(2)}) %collective-permute-start.17) | collective-permute-done | bytes 16416 | tf_op jit(solution)/shard_map/ppermute | solution.py:46
  136.2 0.3 collective-permute-start.18
  136.5 2.5 %collective-permute-start.19 = (f32[4,16,64]{2,1,0:T(8,128)S(1)}, f32[4,16,64]{2,1,0:T(8,128)S(1)}, u32[]{:S(2)}, u32[]{:S(2)}) collective-permute-start(f32[4,16,64]{2,1,0:T(8,128)S(1)} %shard_map.91.refs_0_), channel_id=1, source_target_pairs={{0,24},{1,25},{2,26},{3,27},{4,28},{5,29},{6,30},{7,31},{8,0},{9,1... | collective-permute-start | bytes 49160 | tf_op jit(solution)/shard_map/ppermute | solution.py:46
  139.0 0.5 collective-permute-start.20
  139.7 0.6 collective-permute-done.18.refs_1_
  140.3 3.2 %collective-permute-done.20.refs_3_ = f32[4,16,64]{2,1,0:T(8,128)S(1)} collective-permute-done((f32[4,16,64]{2,1,0:T(8,128)S(1)}, f32[4,16,64]{2,1,0:T(8,128)S(1)}, u32[]{:S(2)}, u32[]{:S(2)}) %collective-permute-start.20) | collective-permute-done | bytes 16416 | tf_op jit(solution)/shard_map/ppermute | solution.py:46
  143.5 1.7 collective-permute-start.21
  145.2 2.2 %collective-permute-start.22 = (f32[4,16,64]{2,1,0:T(8,128)S(1)}, f32[4,16,64]{2,1,0:T(8,128)S(1)}, u32[]{:S(2)}, u32[]{:S(2)}) collective-permute-start(f32[4,16,64]{2,1,0:T(8,128)S(1)} %shard_map.92.refs_0_), channel_id=1, source_target_pairs={{0,6},{1,7},{2,0},{3,1},{4,2},{5,3},{6,4},{7,5},{8,14},{9,15},{10,... | collective-permute-start | bytes 49160 | tf_op jit(solution)/shard_map/ppermute | solution.py:46
  147.4 1.2 collective-permute-start.23
  148.6 3.0 %collective-permute-done.23.refs_3_ = f32[4,16,64]{2,1,0:T(8,128)S(1)} collective-permute-done((f32[4,16,64]{2,1,0:T(8,128)S(1)}, f32[4,16,64]{2,1,0:T(8,128)S(1)}, u32[]{:S(2)}, u32[]{:S(2)}) %collective-permute-start.23) | collective-permute-done | bytes 16416 | tf_op jit(solution)/shard_map/ppermute | solution.py:46
  151.7 1.2 shard_map.93
  152.9 3.2 %shard_map.95 = bf16[596,1024]{1,0:T(8,128)(2,1)S(1)} custom-call(s32[2]{0:T(128)S(1)} %pad_add_fusion.first_ref, s32[4,256]{1,0:T(4,128)S(1)} %broadcast_select_fusion.1.ids_ref, f32[4,4,256]{2,1,0:T(4,128)S(1)} %get-tuple-element.33.coef_ref, f32[4,596,256]{2,1,0:T(8,128)} %get-tuple-element.34.refs_0_, f32[4,596,256]{2,1,0:T(8,128)} %get-tuple-element.35.refs_1_, ...), custom_call_target="tpu_custom_call" | custom-call | flops 6103040 | bytes 6103040 | tf_op jit(solution)/shard_map/pallas_call | solution.py:208
  156.1 4.9 %collective-permute-start.24 = (bf16[596,1024]{1,0:T(8,128)(2,1)S(1)}, bf16[596,1024]{1,0:T(8,128)(2,1)}, u32[]{:S(2)}, u32[]{:S(2)}) collective-permute-start(bf16[596,1024]{1,0:T(8,128)(2,1)S(1)} %shard_map.95), channel_id=1, source_target_pairs={{0,1},{1,0},{2,3},{3,2},{4,5},{5,4},{6,7},{7,6},{8,9},{9,8},{10,11... | collective-permute-start | bytes 3661832 | tf_op jit(solution)/shard_map/ppermute | solution.py:46
  161.1 3.2 %shard_map.94.ga_ref = bf16[596,1024]{1,0:T(8,128)(2,1)S(1)} custom-call(s32[2]{0:T(128)S(1)} %pad_add_fusion.first_ref, s32[4,256]{1,0:T(4,128)S(1)} %broadcast_select_fusion.1.ids_ref, f32[4,4,256]{2,1,0:T(4,128)S(1)} %get-tuple-element.33.coef_ref, f32[4,596,256]{2,1,0:T(8,128)} %get-tuple-element.34.refs_0_, f32[4,596,256]{2,1,0:T(8,128)} %get-tuple-element.35.refs_1_, ...), custom_call_target="tpu_custom_call" | custom-call | flops 6103040 | bytes 6103040 | tf_op jit(solution)/shard_map/pallas_call | solution.py:208
  166.3 15.8 %shard_map.96 = bf16[596,4096]{1,0:T(8,128)(2,1)} custom-call(bf16[596,1024]{1,0:T(8,128)(2,1)S(1)} %shard_map.94.ga_ref, bf16[596,1024]{1,0:T(8,128)(2,1)} %collective-permute-done.24.gb_ref, bf16[256,4096]{1,0:T(8,128)(2,1)} %copy-done.4, bf16[256,4096]{1,0:T(8,128)(2,1)} %collective-permute-done.9.s_ref.refs_1_, ...), custom_call_target="tpu_custom_call" | custom-call | flops 9999220736 | bytes 16777216 | tf_op jit(solution)/shard_map/pallas_call | solution.py:241
  (67 shorter events, 1.7 us)
Async XLA Ops:
  0.6 27.9 %collective-permute-start.4 = (bf16[596,4096]{1,0:T(8,128)(2,1)}, bf16[596,4096]{1,0:T(8,128)(2,1)}, u32[]{:S(2)}, u32[]{:S(2)}) collective-permute-start(bf16[596,4096]{1,0:T(8,128)(2,1)} %bitcast.24), channel_id=1, source_target_pairs={{0,1},{1,0},{2,3},{3,2},{4,5},{5,4},{6,7},{7,6},{8,9},{9,8},{10,11... | collective-permute-start | bytes 14647304 | tf_op jit(solution)/shard_map/ppermute | solution.py:46
  2.1 26.4 %collective-permute-start.5 = (bf16[596,4096]{1,0:T(8,128)(2,1)}, bf16[596,4096]{1,0:T(8,128)(2,1)}, u32[]{:S(2)}, u32[]{:S(2)}) collective-permute-start(bf16[596,4096]{1,0:T(8,128)(2,1)} %bitcast.29), channel_id=1, source_target_pairs={{0,1},{1,0},{2,3},{3,2},{4,5},{5,4},{6,7},{7,6},{8,9},{9,8},{10,11... | collective-permute-start | bytes 14647304 | tf_op jit(solution)/shard_map/ppermute | solution.py:46
  3.5 15.4 %collective-permute-start = (bf16[2,64,4096]{2,1,0:T(8,128)(2,1)S(1)}, bf16[2,64,4096]{2,1,0:T(8,128)(2,1)S(1)}, u32[]{:S(2)}, u32[]{:S(2)}) collective-permute-start(bf16[2,64,4096]{2,1,0:T(8,128)(2,1)S(1)} %fusion), channel_id=1, source_target_pairs={{0,32},{1,9},{2,34},{3,11},{4,36},{5,13},{6,38},{7,15},{8,40},{9,1... | collective-permute-start | bytes 3145736 | tf_op jit(solution)/shard_map/ppermute | solution.py:46
  4.9 14.1 %collective-permute-start.1 = (bf16[2,64,4096]{2,1,0:T(8,128)(2,1)S(1)}, bf16[2,64,4096]{2,1,0:T(8,128)(2,1)S(1)}, u32[]{:S(2)}, u32[]{:S(2)}) collective-permute-start(bf16[2,64,4096]{2,1,0:T(8,128)(2,1)S(1)} %fusion), channel_id=1, source_target_pairs={{0,96},{1,25},{2,98},{3,27},{4,100},{5,29},{6,102},{7,31},{8,104},... | collective-permute-start | bytes 3145736 | tf_op jit(solution)/shard_map/ppermute | solution.py:46
  18.9 9.6 %collective-permute-start.2 = (bf16[64,4096]{1,0:T(8,128)(2,1)S(1)}, bf16[64,4096]{1,0:T(8,128)(2,1)S(1)}, u32[]{:S(2)}, u32[]{:S(2)}) collective-permute-start(bf16[64,4096]{1,0:T(8,128)(2,1)S(1)} %get-tuple-element.49), channel_id=1, source_target_pairs={{0,32},{1,9},{2,34},{3,11},{4,36},{5,13},{6,38},{7,15},{8,40},{9,1... | collective-permute-start | bytes 1572872 | tf_op jit(solution)/shard_map/ppermute | solution.py:46
  19.1 9.4 %collective-permute-start.3 = (bf16[64,4096]{1,0:T(8,128)(2,1)S(1)}, bf16[64,4096]{1,0:T(8,128)(2,1)S(1)}, u32[]{:S(2)}, u32[]{:S(2)}) collective-permute-start(bf16[64,4096]{1,0:T(8,128)(2,1)S(1)} %get-tuple-element.51), channel_id=1, source_target_pairs={{0,96},{1,25},{2,98},{3,27},{4,100},{5,29},{6,102},{7,31},{8,104},... | collective-permute-start | bytes 1572872 | tf_op jit(solution)/shard_map/ppermute | solution.py:46
  28.7 11.0 %copy-start.4 = (bf16[256,4096]{1,0:T(8,128)(2,1)}, bf16[256,4096]{1,0:T(8,128)(2,1)S(1)}, u32[]{:S(2)}) copy-start(bf16[256,4096]{1,0:T(8,128)(2,1)S(1)} %pad_maximum_fusion.1.s_ref.refs_0_) | copy-start | bytes 6291460
  28.7 26.9 %collective-permute-start.7 = (bf16[256,4096]{1,0:T(8,128)(2,1)S(1)}, bf16[256,4096]{1,0:T(8,128)(2,1)}, u32[]{:S(2)}, u32[]{:S(2)}) collective-permute-start(bf16[256,4096]{1,0:T(8,128)(2,1)S(1)} %pad_maximum_fusion.1.s_ref.refs_0_), channel_id=1, source_target_pairs={{0,24},{1,97},{2,26},{3,99},{4,28},{5,101},{6,30},{7,103},{8,0},{9... | collective-permute-start | bytes 6291464 | tf_op jit(solution)/shard_map/ppermute | solution.py:46
  31.3 24.4 %collective-permute-start.8 = (bf16[256,4096]{1,0:T(8,128)(2,1)S(1)}, bf16[256,4096]{1,0:T(8,128)(2,1)}, u32[]{:S(2)}, u32[]{:S(2)}) collective-permute-start(bf16[256,4096]{1,0:T(8,128)(2,1)S(1)} %pad_maximum_fusion.1.s_ref.refs_0_), channel_id=1, source_target_pairs={{0,1},{1,0},{2,3},{3,2},{4,5},{5,4},{6,7},{7,6},{8,9},{9,8},{10,11... | collective-permute-start | bytes 6291464 | tf_op jit(solution)/shard_map/ppermute | solution.py:46
  33.9 50.9 %collective-permute-start.9 = (bf16[256,4096]{1,0:T(8,128)(2,1)S(1)}, bf16[256,4096]{1,0:T(8,128)(2,1)}, u32[]{:S(2)}, u32[]{:S(2)}) collective-permute-start(bf16[256,4096]{1,0:T(8,128)(2,1)S(1)} %pad_maximum_fusion.1.s_ref.refs_0_), channel_id=1, source_target_pairs={{0,8},{1,33},{2,10},{3,35},{4,12},{5,37},{6,14},{7,39},{8,16},{9,4... | collective-permute-start | bytes 6291464 | tf_op jit(solution)/shard_map/ppermute | solution.py:46
  34.3 2.5 %copy-start.8 = (s32[4]{0:T(128)S(1)}, s32[4]{0:T(128)}, u32[]{:S(2)}) copy-start(s32[4]{0:T(128)} %constant.123.clone) | copy-start | bytes 52
  34.3 2.7 %copy-start.7 = (s32[2048]{0:T(1024)S(1)}, s32[2048]{0:T(1024)}, u32[]{:S(2)}) copy-start(s32[2048]{0:T(1024)} %param.11) | copy-start | bytes 24580
  35.8 47.4 %collective-permute-start.6 = (bf16[256,4096]{1,0:T(8,128)(2,1)}, bf16[256,4096]{1,0:T(8,128)(2,1)}, u32[]{:S(2)}, u32[]{:S(2)}) collective-permute-start(bf16[256,4096]{1,0:T(8,128)(2,1)} %pad_maximum_fusion.t_ref), channel_id=1, source_target_pairs={{0,8},{1,33},{2,10},{3,35},{4,12},{5,37},{6,14},{7,39},{8,16},{9,4... | collective-permute-start | bytes 6291464 | tf_op jit(solution)/shard_map/ppermute | solution.py:46
  37.9 65.3 %collective-permute-start.10 = (bf16[256,4096]{1,0:T(8,128)(2,1)}, bf16[256,4096]{1,0:T(8,128)(2,1)}, u32[]{:S(2)}, u32[]{:S(2)}) collective-permute-start(bf16[256,4096]{1,0:T(8,128)(2,1)} %pad_maximum_fusion.t_ref), channel_id=1, source_target_pairs={{0,24},{1,97},{2,26},{3,99},{4,28},{5,101},{6,30},{7,103},{8,0},{9... | collective-permute-start | bytes 6291464 | tf_op jit(solution)/shard_map/ppermute | solution.py:46
  39.7 2.4 %copy-start = (bf16[4096,596]{0,1:T(8,128)(2,1)S(1)}, bf16[4096,596]{0,1:T(8,128)(2,1)}, u32[]{:S(2)}) copy-start(bf16[4096,596]{0,1:T(8,128)(2,1)} %param.9) | copy-start | bytes 14647300
  42.1 2.4 %copy-start.2 = (bf16[4096,596]{0,1:T(8,128)(2,1)S(1)}, bf16[4096,596]{0,1:T(8,128)(2,1)}, u32[]{:S(2)}) copy-start(bf16[4096,596]{0,1:T(8,128)(2,1)} %param.10) | copy-start | bytes 14647300
  44.5 41.5 %copy-start.6 = (s32[2048]{0:T(1024)S(1)}, s32[2048]{0:T(1024)}, u32[]{:S(2)}) copy-start(s32[2048]{0:T(1024)} %param.12) | copy-start | bytes 24580
  83.2 31.9 %collective-permute-start.12 = (bf16[256,4096]{1,0:T(8,128)(2,1)}, bf16[256,4096]{1,0:T(8,128)(2,1)}, u32[]{:S(2)}, u32[]{:S(2)}) collective-permute-start(bf16[256,4096]{1,0:T(8,128)(2,1)} %collective-permute-done.7.s_ref.refs_2_), channel_id=1, source_target_pairs={{0,24},{1,97},{2,26},{3,99},{4,28},{5,101},{6,30},{7,103},{8,0},{9... | collective-permute-start | bytes 6291464 | tf_op jit(solution)/shard_map/ppermute | solution.py:46
  84.7 30.8 %collective-permute-start.14 = (bf16[256,4096]{1,0:T(8,128)(2,1)}, bf16[256,4096]{1,0:T(8,128)(2,1)}, u32[]{:S(2)}, u32[]{:S(2)}) collective-permute-start(bf16[256,4096]{1,0:T(8,128)(2,1)} %collective-permute-done.7.s_ref.refs_2_), channel_id=1, source_target_pairs={{0,1},{1,0},{2,3},{3,2},{4,5},{5,4},{6,7},{7,6},{8,9},{9,8},{10,11... | collective-permute-start | bytes 6291464 | tf_op jit(solution)/shard_map/ppermute | solution.py:46
  84.7 30.7 %collective-permute-start.11 = (bf16[256,4096]{1,0:T(8,128)(2,1)}, bf16[256,4096]{1,0:T(8,128)(2,1)}, u32[]{:S(2)}, u32[]{:S(2)}) collective-permute-start(bf16[256,4096]{1,0:T(8,128)(2,1)} %collective-permute-done.6.t_ref), channel_id=1, source_target_pairs={{0,8},{1,33},{2,10},{3,35},{4,12},{5,37},{6,14},{7,39},{8,16},{9,4... | collective-permute-start | bytes 6291464 | tf_op jit(solution)/shard_map/ppermute | solution.py:46
  84.7 30.8 %collective-permute-start.13 = (bf16[256,4096]{1,0:T(8,128)(2,1)}, bf16[256,4096]{1,0:T(8,128)(2,1)S(1)}, u32[]{:S(2)}, u32[]{:S(2)}) collective-permute-start(bf16[256,4096]{1,0:T(8,128)(2,1)} %collective-permute-done.9.s_ref.refs_1_), channel_id=1, source_target_pairs={{0,1},{1,0},{2,3},{3,2},{4,5},{5,4},{6,7},{7,6},{8,9},{9,8},{10,11... | collective-permute-start | bytes 6291464 | tf_op jit(solution)/shard_map/ppermute | solution.py:46
  86.7 2.4 %copy-start.1 = (bf16[4096,596]{0,1:T(8,128)(2,1)S(1)}, bf16[4096,596]{0,1:T(8,128)(2,1)}, u32[]{:S(2)}) copy-start(bf16[4096,596]{0,1:T(8,128)(2,1)} %param.9) | copy-start | bytes 14647300
  89.0 2.4 %copy-start.3 = (bf16[4096,596]{0,1:T(8,128)(2,1)S(1)}, bf16[4096,596]{0,1:T(8,128)(2,1)}, u32[]{:S(2)}) copy-start(bf16[4096,596]{0,1:T(8,128)(2,1)} %param.10) | copy-start | bytes 14647300
  115.1 51.1 %collective-permute-start.25 = (bf16[256,4096]{1,0:T(8,128)(2,1)}, bf16[256,4096]{1,0:T(8,128)(2,1)}, u32[]{:S(2)}, u32[]{:S(2)}) collective-permute-start(bf16[256,4096]{1,0:T(8,128)(2,1)} %collective-permute-done.12.s_ref.refs_3_), channel_id=1, source_target_pairs={{0,1},{1,0},{2,3},{3,2},{4,5},{5,4},{6,7},{7,6},{8,9},{9,8},{10,11... | collective-permute-start | bytes 6291464 | tf_op jit(solution)/shard_map/ppermute | solution.py:46
  115.5 12.6 %copy-start.5 = (bf16[256,4096]{1,0:T(8,128)(2,1)}, bf16[256,4096]{1,0:T(8,128)(2,1)S(1)}, u32[]{:S(2)}) copy-start(bf16[256,4096]{1,0:T(8,128)(2,1)S(1)} %collective-permute-done.13.refs_2_.refs_5_) | copy-start | bytes 6291460
  128.6 5.1 %collective-permute-start.15 = (f32[4,16,64]{2,1,0:T(8,128)S(1)}, f32[4,16,64]{2,1,0:T(8,128)S(1)}, u32[]{:S(2)}, u32[]{:S(2)}) collective-permute-start(f32[4,16,64]{2,1,0:T(8,128)S(1)} %shard_map.90.refs_0_), channel_id=1, source_target_pairs={{0,32},{1,33},{2,34},{3,35},{4,36},{5,37},{6,38},{7,39},{8,40},{9,... | collective-permute-start | bytes 49160 | tf_op jit(solution)/shard_map/ppermute | solution.py:46
  129.1 4.6 %collective-permute-start.16 = (f32[4,16,64]{2,1,0:T(8,128)S(1)}, f32[4,16,64]{2,1,0:T(8,128)S(1)}, u32[]{:S(2)}, u32[]{:S(2)}) collective-permute-start(f32[4,16,64]{2,1,0:T(8,128)S(1)} %shard_map.90.refs_0_), channel_id=1, source_target_pairs={{0,96},{1,97},{2,98},{3,99},{4,100},{5,101},{6,102},{7,103},{8,104... | collective-permute-start | bytes 49160 | tf_op jit(solution)/shard_map/ppermute | solution.py:46
  131.9 4.3 %collective-permute-start.17 = (f32[4,16,64]{2,1,0:T(8,128)S(1)}, f32[4,16,64]{2,1,0:T(8,128)S(1)}, u32[]{:S(2)}, u32[]{:S(2)}) collective-permute-start(f32[4,16,64]{2,1,0:T(8,128)S(1)} %shard_map.90.refs_0_), channel_id=1, source_target_pairs={{0,64},{1,65},{2,66},{3,67},{4,68},{5,69},{6,70},{7,71},{8,72},{9,... | collective-permute-start | bytes 49160 | tf_op jit(solution)/shard_map/ppermute | solution.py:46
  136.2 4.0 %collective-permute-start.18 = (f32[4,16,64]{2,1,0:T(8,128)S(1)}, f32[4,16,64]{2,1,0:T(8,128)S(1)}, u32[]{:S(2)}, u32[]{:S(2)}) collective-permute-start(f32[4,16,64]{2,1,0:T(8,128)S(1)} %shard_map.91.refs_0_), channel_id=1, source_target_pairs={{0,8},{1,9},{2,10},{3,11},{4,12},{5,13},{6,14},{7,15},{8,16},{9,17... | collective-permute-start | bytes 49160 | tf_op jit(solution)/shard_map/ppermute | solution.py:46
  136.5 3.8 %collective-permute-start.19 = (f32[4,16,64]{2,1,0:T(8,128)S(1)}, f32[4,16,64]{2,1,0:T(8,128)S(1)}, u32[]{:S(2)}, u32[]{:S(2)}) collective-permute-start(f32[4,16,64]{2,1,0:T(8,128)S(1)} %shard_map.91.refs_0_), channel_id=1, source_target_pairs={{0,24},{1,25},{2,26},{3,27},{4,28},{5,29},{6,30},{7,31},{8,0},{9,1... | collective-permute-start | bytes 49160 | tf_op jit(solution)/shard_map/ppermute | solution.py:46
  139.0 4.5 %collective-permute-start.20 = (f32[4,16,64]{2,1,0:T(8,128)S(1)}, f32[4,16,64]{2,1,0:T(8,128)S(1)}, u32[]{:S(2)}, u32[]{:S(2)}) collective-permute-start(f32[4,16,64]{2,1,0:T(8,128)S(1)} %shard_map.91.refs_0_), channel_id=1, source_target_pairs={{0,16},{1,17},{2,18},{3,19},{4,20},{5,21},{6,22},{7,23},{8,24},{9,... | collective-permute-start | bytes 49160 | tf_op jit(solution)/shard_map/ppermute | solution.py:46
  143.5 5.1 %collective-permute-start.21 = (f32[4,16,64]{2,1,0:T(8,128)S(1)}, f32[4,16,64]{2,1,0:T(8,128)S(1)}, u32[]{:S(2)}, u32[]{:S(2)}) collective-permute-start(f32[4,16,64]{2,1,0:T(8,128)S(1)} %shard_map.92.refs_0_), channel_id=1, source_target_pairs={{0,2},{1,3},{2,4},{3,5},{4,6},{5,7},{6,0},{7,1},{8,10},{9,11},{10,... | collective-permute-start | bytes 49160 | tf_op jit(solution)/shard_map/ppermute | solution.py:46
  145.2 3.5 %collective-permute-start.22 = (f32[4,16,64]{2,1,0:T(8,128)S(1)}, f32[4,16,64]{2,1,0:T(8,128)S(1)}, u32[]{:S(2)}, u32[]{:S(2)}) collective-permute-start(f32[4,16,64]{2,1,0:T(8,128)S(1)} %shard_map.92.refs_0_), channel_id=1, source_target_pairs={{0,6},{1,7},{2,0},{3,1},{4,2},{5,3},{6,4},{7,5},{8,14},{9,15},{10,... | collective-permute-start | bytes 49160 | tf_op jit(solution)/shard_map/ppermute | solution.py:46
  147.4 4.3 %collective-permute-start.23 = (f32[4,16,64]{2,1,0:T(8,128)S(1)}, f32[4,16,64]{2,1,0:T(8,128)S(1)}, u32[]{:S(2)}, u32[]{:S(2)}) collective-permute-start(f32[4,16,64]{2,1,0:T(8,128)S(1)} %shard_map.92.refs_0_), channel_id=1, source_target_pairs={{0,4},{1,5},{2,6},{3,7},{4,0},{5,1},{6,2},{7,3},{8,12},{9,13},{10,... | collective-permute-start | bytes 49160 | tf_op jit(solution)/shard_map/ppermute | solution.py:46
  156.1 10.2 %collective-permute-start.24 = (bf16[596,1024]{1,0:T(8,128)(2,1)S(1)}, bf16[596,1024]{1,0:T(8,128)(2,1)}, u32[]{:S(2)}, u32[]{:S(2)}) collective-permute-start(bf16[596,1024]{1,0:T(8,128)(2,1)S(1)} %shard_map.95), channel_id=1, source_target_pairs={{0,1},{1,0},{2,3},{3,2},{4,5},{5,4},{6,7},{7,6},{8,9},{9,8},{10,11... | collective-permute-start | bytes 3661832 | tf_op jit(solution)/shard_map/ppermute | solution.py:46
  161.0 3.3 %collective-permute-start.26 = (f32[1,1]{1,0:T(1,128)}, f32[1,1]{1,0:T(1,128)}, u32[]{:S(2)}, u32[]{:S(2)}) collective-permute-start(f32[1,1]{1,0:T(1,128)} %get-tuple-element.39), channel_id=1, source_target_pairs={{0,1},{1,0},{2,3},{3,2},{4,5},{5,4},{6,7},{7,6},{8,9},{9,8},{10,11... | collective-permute-start | bytes 20 | tf_op jit(solution)/shard_map/ppermute | solution.py:46

commit v3 on v2

v3 whole, which is shorter than its diff:
```python
import functools

import jax
import jax.numpy as jnp
from jax import lax
from jax.experimental import pallas as pl
from jax.experimental.pallas import tpu as pltpu
from jax.sharding import PartitionSpec as P

LOSS_SCALE = 64.0
SAMPLED_WEIGHT = 0.0625
SIDE = 4
AXES = ("dp", "tensor")
OFFSETS = (0, -1, 1, 2)
F32 = jnp.float32
MIB = 1 << 20


def flat(x, y, z, c):
    return (((x % SIDE) * SIDE + y % SIDE) * SIDE + z % SIDE) * 2 + c


def pairs(step):
    return [
        (flat(x, y, z, c), flat(*step(x, y, z, c)))
        for x in range(SIDE) for y in range(SIDE) for z in range(SIDE) for c in range(2)
    ]


def first(d):
    return pairs(lambda x, y, z, c: (x + d * (1 - c), y + d * c, z, c))


def second(d):
    return pairs(lambda x, y, z, c: (x + d * c, y + d * (1 - c), z, c))


def along(axis, d):
    return pairs(lambda x, y, z, c: (x + d * (axis == 0), y + d * (axis == 1), z + d * (axis == 2), c))


def z_pair():
    return pairs(lambda x, y, z, c: (x, y, z + 1 - 2 * c, c))


SIBLING = pairs(lambda x, y, z, c: (x, y, z, 1 - c))


def send(array, perm):
    return lax.ppermute(array, AXES, perm)


def nt(a, b):
    return lax.dot_general(a, b, (((1,), (1,)), ((), ())), preferred_element_type=F32)


PAD = -1e30


def stats_of(held, i, first, ids):
    rows, tokens = held.shape[1:]
    step = 40

    def chunk(j, r):
        return held[j, pl.ds(pl.multiple_of(r * step, 8), step), :].reshape(step // 8, 8, tokens)

    def tops(r, carry):
        ms, mt = carry
        return jnp.maximum(ms, jnp.max(chunk(2 * i, r), axis=0)), jnp.maximum(mt, jnp.max(chunk(2 * i + 1, r), axis=0))

    low = jnp.full((8, tokens), PAD, F32)
    ms, mt = lax.fori_loop(0, rows // step, tops, (low, low))
    ms, mt = jnp.max(ms, axis=0, keepdims=True), jnp.max(mt, axis=0, keepdims=True)
    at = lax.broadcasted_iota(jnp.int32, (step, tokens), 0).reshape(step // 8, 8, tokens)
    wanted = ids - first

    def sums(r, carry):
        s, t = chunk(2 * i, r), chunk(2 * i + 1, r)
        u = s - t
        es = jnp.exp(s - ms)
        et = jnp.exp(t - mt)
        picked = jnp.where(at == wanted - r * step, u, 0.0)
        return tuple(c + jnp.sum(v, axis=0) for c, v in zip(carry, (es, et, es * u, picked)))

    nil = jnp.zeros((8, tokens), F32)
    zs, zt, mean, picked = (
        jnp.sum(v, axis=0, keepdims=True) for v in lax.fori_loop(0, rows // step, sums, (nil,) * 4))
    return mt + jnp.log(zt), ms + jnp.log(zs), mean / zs, picked


def add_all(values):
    if len(values) == 4:
        return (values[0] + values[3]) + (values[1] + values[2])
    return sum(values[1:], values[0])


def join(parts):
    def lse(values):
        top = functools.reduce(jnp.maximum, values)
        return top + jnp.log(add_all([jnp.exp(v - top) for v in values]))
    nt_all = lse([p[0] for p in parts])
    ns_all = lse([p[1] for p in parts])
    mean = add_all([jnp.exp(p[1] - ns_all) * p[2] for p in parts])
    return nt_all, ns_all, mean, add_all([p[3] for p in parts])


def logits_kernel(shape, scalar_ref, ids_ref, *refs):
    n = len(shape)
    count = sum(len(kind) for group in shape for kind in group)
    pieces, heads, refs = list(refs[:count]), refs[count:count + 4], refs[count + 4:]
    hidden = [[[pieces.pop(0) for _ in kind] for kind in group] for group in shape]
    *outs, student_ref = refs[-7 - 2 * n:-6]
    hid, head, held, in_sems, head_sems, out_sems = refs[-6:]
    vocab, rows = head.shape[1], held.shape[2]
    common, width = hidden[0][0][0].shape[-1], hidden[0][1][0].shape[-1]
    at = (0, pl.multiple_of(common + scalar_ref[2] * width, width), pl.multiple_of(common + (1 - scalar_ref[2]) * width, width))

    def fetch(g, kind, j):
        found = hidden[g][kind]
        source = found[j] if len(found) == 2 else found[0].at[(j,) if len(found[0].shape) == 3 else (g, j)]
        return pltpu.make_async_copy(source, hid.at[g, j, :, pl.ds(at[kind], source.shape[-1])], in_sems.at[g, kind, j])

    def fetch_head(h, lo, hi, sem):
        return pltpu.make_async_copy(heads[h].at[:, lo:hi], head.at[h, :, lo:hi], head_sems.at[sem])

    depth = hid.shape[3]
    early = [fetch_head(0, 0, common, 4)] + [fetch(g, 0, 1) for g in range(n)]
    late = [fetch_head(0, common, depth, 0)] + [fetch(g, kind, 1) for g in range(n) for kind in (1, 2)]
    teacher = [fetch_head(1, 0, depth, 1)] + [fetch(g, kind, 0) for g in range(n) for kind in (0, 1, 2)]
    sibling = [[fetch_head(2, 0, depth, 2)], [fetch_head(3, 0, depth, 3)]]

    def start(copies):
        for copy in copies:
            copy.start()

    def wait(copies):
        for copy in copies:
            copy.wait()

    start(early)
    start(late)
    wait(early)
    start(teacher)
    for g in range(n):
        held[g, 0, :vocab, :] = nt(head[0, :, :common], hid[g, 1, :, :common])
    wait(late)
    start(sibling[0])
    for g in range(n):
        held[g, 0, :vocab, :] += nt(head[0, :, common:], hid[g, 1, :, common:])
    wait(teacher)
    start(sibling[1])
    kept = [
        pltpu.make_async_copy(hid.at[g, 1], student_ref.at[pl.ds(g * hid.shape[2], hid.shape[2])], out_sems.at[g, 2])
        for g in range(n)
    ]
    start(kept)
    for g in range(n):
        held[g, 1, :vocab, :] = nt(head[1], hid[g, 0])
    parts, stored = [[] for _ in range(n)], []

    def finish(i):
        for g in range(n):
            held[g, 2 * i:2 * i + 2, vocab:, :] = jnp.full((2, rows - vocab, held.shape[3]), PAD, F32)
            stored.append(pltpu.make_async_copy(
                held.at[g, pl.ds(2 * i, 2)], outs[2 * g].at[pl.ds(2 * i, 2)], out_sems.at[g, i]))
            stored[-1].start()
            parts[g].append(stats_of(held.at[g], i, scalar_ref[i], ids_ref[g:g + 1, :]))

    finish(0)
    for i in range(2):
        wait(sibling[i])
        for g in range(n):
            held[g, 2 + i, :vocab, :] = nt(head[2 + i], hid[g, 1 - i])
    finish(1)
    for g in range(n):
        total = join(parts[g])
        tokens = total[0].shape[1] // SIDE
        for q in range(4):
            for b in range(SIDE):
                outs[2 * g + 1][b, q:q + 1, :] = total[q][:, b * tokens:(b + 1) * tokens]
    wait(kept)
    wait(stored)


def logits_call(scalars, ids, groups, heads, after=()):
    vocab, depth = heads[0].shape
    n, tokens = ids.shape
    rows = -(-vocab // 40) * 40
    vmem, hbm = pl.BlockSpec(memory_space=pltpu.VMEM), pl.BlockSpec(memory_space=pl.ANY)
    pieces = [a for group in groups for kind in group for a in kind]
    shape = [[[None] * len(kind) for kind in group] for group in groups]
    out = pl.pallas_call(
        functools.partial(logits_kernel, shape),
        in_specs=[pl.BlockSpec(memory_space=pltpu.SMEM), vmem] + [hbm] * (len(pieces) + 4 + len(after)),
        out_specs=[pl.BlockSpec(memory_space=pltpu.HBM), vmem] * n + [pl.BlockSpec(memory_space=pltpu.HBM)],
        out_shape=[
            pltpu.HBM((4, rows, tokens), F32),
            jax.ShapeDtypeStruct((SIDE, 4, tokens // SIDE), F32),
        ] * n + [pltpu.HBM((n * tokens, depth), jnp.bfloat16)],
        scratch_shapes=[
            pltpu.VMEM((n, 2, tokens, depth), jnp.bfloat16),
            pltpu.VMEM((4, vocab, depth), jnp.bfloat16),
            pltpu.VMEM((n, 4, rows, tokens), F32),
            pltpu.SemaphoreType.DMA((n, 3, 2)),
            pltpu.SemaphoreType.DMA((5,)),
            pltpu.SemaphoreType.DMA((n, 3)),
        ],
        compiler_params=pltpu.CompilerParams(vmem_limit_bytes=(26 + 9 * n) * MIB),
        cost_estimate=pl.CostEstimate(flops=8 * n * vocab * tokens * depth, bytes_accessed=8 * vocab * depth, transcendentals=0),
    )(scalars, ids, *pieces, *in_hbm(heads), *after)
    return *[out[2 * g:2 * g + 2] for g in range(n)], out[-1]


def order_kernel(place_ref, *refs):
    *groups, out_ref = refs
    for j, group in enumerate(groups):
        for i in range(SIDE):
            b = place_ref[j * SIDE + i]
            for q in range(4):
                out_ref[q, pl.ds(b, 1), :] = group[i, q:q + 1, :]


SMALL = pltpu.CompilerParams(vmem_limit_bytes=4 * MIB)


def order_call(place, groups):
    tokens = groups[0].shape[-1]
    return pl.pallas_call(
        order_kernel,
        in_specs=[pl.BlockSpec(memory_space=pltpu.SMEM)] + [pl.BlockSpec(memory_space=pltpu.VMEM)] * len(groups),
        out_specs=pl.BlockSpec(memory_space=pltpu.VMEM),
        out_shape=jax.ShapeDtypeStruct((4, SIDE * SIDE, tokens), F32),
        compiler_params=SMALL,
    )(place, *groups)


def join_kernel(*refs):
    *ins, out_ref = refs
    total = join([[r[q] for q in range(4)] for r in ins])
    for q in range(4):
        out_ref[q] = total[q]


def join_call(parts):
    vmem = pl.BlockSpec(memory_space=pltpu.VMEM)
    return pl.pallas_call(
        join_kernel,
        in_specs=[vmem] * len(parts),
        out_specs=vmem,
        out_shape=jax.ShapeDtypeStruct(parts[0].shape, F32),
        compiler_params=SMALL,
    )(*parts)


def finish_kernel(place_ref, factor_ref, weight_ref, *refs):
    *ins, coef_ref, kl_ref, rows_ref = refs
    n_t, n_s, mean, picked = join([[r[q] for q in range(4)] for r in ins])
    kl_ref[...] = jnp.sum(weight_ref[...] * (mean + n_t - n_s), keepdims=True)
    pull = SAMPLED_WEIGHT * -(picked + n_t - n_s)
    for q, value in enumerate((n_s, factor_ref[...], pull - mean, pull)):
        rows_ref[q] = value
    tokens = n_s.shape[1]
    for j in range(SIDE):
        for q in range(4):
            for i in range(SIDE):
                coef_ref[j, q:q + 1, i * tokens:(i + 1) * tokens] = rows_ref[q, pl.ds(place_ref[j * SIDE + i], 1), :]


def finish_call(place, factor, weight, parts):
    vmem = pl.BlockSpec(memory_space=pltpu.VMEM)
    tokens = factor.shape[1]
    return pl.pallas_call(
        finish_kernel,
        in_specs=[pl.BlockSpec(memory_space=pltpu.SMEM)] + [vmem] * (2 + len(parts)),
        out_specs=[vmem, vmem],
        out_shape=[jax.ShapeDtypeStruct((SIDE, 4, SIDE * tokens), F32), jax.ShapeDtypeStruct((1, 1), F32)],
        scratch_shapes=[pltpu.VMEM((4, SIDE * SIDE, tokens), F32)],
        compiler_params=SMALL,
    )(place, factor, weight, *parts)


def grad_kernel(part, scalar_ref, ids_ref, coef_ref, *refs):
    *ins, out_ref, held, sems = refs
    vocab = out_ref.shape[0]
    copies = [pltpu.make_async_copy(ref.at[pl.ds(2 * part, 2)], held.at[j], sems.at[j]) for j, ref in enumerate(ins)]
    for copy in copies:
        copy.start()
    tokens = held.shape[3]
    for j in range(SIDE):
        copies[j].wait()
        s, t = held[j, 0], held[j, 1]
        n_s, factor, shift, pull = (coef_ref[j, q:q + 1, :] for q in range(4))
        rows = lax.broadcasted_iota(jnp.int32, s.shape, 0)
        inner = jnp.exp(s - n_s) * (s - t + shift)
        inner = inner - jnp.where(rows == ids_ref[j:j + 1, :] - scalar_ref[part], pull, 0.0)
        out_ref[:, j * tokens:(j + 1) * tokens] = (factor * inner).astype(jnp.bfloat16)[:vocab]


def in_hbm(arrays):
    return [pltpu.with_memory_space_constraint(a, pltpu.HBM) for a in arrays]


def grad_call(part, scalars, ids, coef, logits, vocab):
    _, rows, tokens = logits[0].shape
    vmem, hbm = pl.BlockSpec(memory_space=pltpu.VMEM), pl.BlockSpec(memory_space=pltpu.HBM)
    return pl.pallas_call(
        functools.partial(grad_kernel, part),
        in_specs=[pl.BlockSpec(memory_space=pltpu.SMEM), vmem, vmem] + [hbm] * SIDE,
        out_specs=vmem,
        out_shape=jax.ShapeDtypeStruct((vocab, SIDE * tokens), jnp.bfloat16),
        scratch_shapes=[pltpu.VMEM((SIDE, 2, rows, tokens), F32), pltpu.SemaphoreType.DMA((SIDE,))],
        compiler_params=pltpu.CompilerParams(vmem_limit_bytes=16 * MIB),
        cost_estimate=pl.CostEstimate(flops=10 * vocab * tokens * SIDE, bytes_accessed=10 * vocab * tokens * SIDE, transcendentals=0),
    )(scalars, ids, coef, *in_hbm(logits))


def head_kernel(ga_ref, gb_ref, *refs):
    *hids, out_ref = refs
    half = len(hids) // 2
    total = None
    for g, group in ((ga_ref, hids[:half]), (gb_ref, hids[half:])):
        rows = jnp.concatenate([r[...] for r in group], axis=0)
        part = jnp.dot(g[...], rows, preferred_element_type=F32)
        total = part if total is None else total + part
    out_ref[...] = total.astype(jnp.bfloat16)


def head_call(ga, gb, hids):
    vocab, tokens = ga.shape
    depth = hids[0].shape[-1]
    tile = 1024
    whole = pl.BlockSpec((vocab, tokens), lambda i: (0, 0))
    return pl.pallas_call(
        head_kernel,
        grid=(depth // tile,),
        in_specs=[whole, whole] + [pl.BlockSpec((h.shape[0], tile), lambda i: (0, i)) for h in hids],
        out_specs=pl.BlockSpec((vocab, tile), lambda i: (0, i)),
        out_shape=jax.ShapeDtypeStruct((vocab, depth), jnp.bfloat16),
        compiler_params=pltpu.CompilerParams(vmem_limit_bytes=44 * MIB),
        cost_estimate=pl.CostEstimate(flops=4 * vocab * tokens * depth, bytes_accessed=4 * tokens * depth, transcendentals=0),
    )(ga, gb, *in_hbm(hids))


def local(teacher_hidden, student_hidden, teacher_head, student_head, sampled_ids, valid_mask):
    dp, tensor = lax.axis_index("dp"), lax.axis_index("tensor")
    x, y, core = dp // SIDE, dp % SIDE, tensor % 2
    half = teacher_hidden.shape[0] // 2
    vocab = teacher_head.shape[1]

    ta, sa = teacher_head.T, student_head.T
    tb, sb = send(ta, SIBLING), send(sa, SIBLING)

    shift = jnp.array([o % SIDE for o in OFFSETS], jnp.int32)
    one = (jnp.where(core == 0, x, y) + shift) % SIDE
    two = (jnp.where(core == 0, y, x) + shift) % SIDE
    place = jnp.where(core == 0, one[None, :] * SIDE + two[:, None], two[:, None] * SIDE + one[None, :]).reshape(-1)

    def mine(a):
        return lax.dynamic_index_in_dim(a.reshape(SIDE * SIDE, 2, half), core, 1, keepdims=False)

    ids = jnp.take(mine(sampled_ids), place, axis=0).reshape(SIDE, SIDE * half)
    all_weights = valid_mask.astype(F32)
    token_count = jnp.sum(all_weights)
    weights = mine(all_weights)
    factor = LOSS_SCALE * weights / jnp.sqrt(token_count)
    row_of = flat(x, y, tensor // 2, core) * vocab
    other_of = flat(x, y, tensor // 2, 1 - core) * vocab
    parity = (tensor // 2) % 2
    scalars = jnp.stack([row_of, other_of, parity])

    depth = teacher_hidden.shape[1]
    common, width = depth // 2, depth // 4
    own = lax.dynamic_slice_in_dim(jnp.stack([teacher_hidden, student_hidden]), core * half, half, 1)
    own_x = lax.dynamic_slice_in_dim(own, common + parity * width, width, 2)
    own = jnp.concatenate([own[:, :, :common], own_x], axis=2)
    low, high = send(own, first(1)), send(own, first(-1))
    far_t, far_s = send(low[0], first(1)), send(high[1], first(-1))
    far_t, far_s, tb, sb = lax.optimization_barrier((far_t, far_s, tb, sb))
    heads = (sa, ta, sb, tb)
    row = [own, low, high, jnp.stack([far_t, far_s])]
    row_x = jnp.concatenate([a[:, :, common:] for a in row], axis=1)
    row_c = jnp.concatenate([a[:, :, :common] for a in row], axis=1)
    low_x, high_x = send(row_x, second(1)), send(row_x, second(-1))
    row_y = send(row_x, z_pair())
    low_c, high_c = send(row_c, second(1)), send(row_c, second(-1))
    low_x, high_x, row_y = lax.optimization_barrier((low_x, high_x, row_y))
    far_xt, far_xs = send(low_x[0], second(1)), send(high_x[1], second(-1))
    both_y = send(jnp.stack([low_x, high_x]), z_pair())
    group0, student0 = logits_call(scalars, ids[0:1], [((row_c,), (row_x,), (row_y,))], heads)
    low_c, high_c, both_y, far_xt, far_xs, student0, *group0 = lax.optimization_barrier(
        (low_c, high_c, both_y, far_xt, far_xs, student0, *group0))
    on_t, on_s = low_c[0], high_c[1]
    far_ct, far_cs = send(on_t, second(1)), send(on_s, second(-1))
    far_yt, far_ys = send(far_xt, z_pair()), send(far_xs, z_pair())
    other0 = send(student0, SIBLING)
    group1, group2, student1 = logits_call(scalars, ids[1:3], [
        ((low_c,), (low_x,), (both_y,)), ((high_c,), (high_x,), (both_y,))], heads, (other0,))
    far_ct, far_cs, far_yt, far_ys, student1 = lax.optimization_barrier((far_ct, far_cs, far_yt, far_ys, student1))
    other1 = send(student1, SIBLING)
    group3, student2 = logits_call(scalars, ids[3:4], [((far_ct, far_cs), (far_xt, far_xs), (far_yt, far_ys))], heads, (group1[1],))
    groups = [group0, group1, group2, group3]
    others = [other0, other1, send(student2, SIBLING)]

    total = order_call(place, [g[1] for g in groups])
    for axis in range(3):
        parts = [total, send(total, along(axis, 1)), send(total, along(axis, -1)), send(total, along(axis, 2))]
        if axis < 2:
            total = join_call(parts)
    coef, kl = finish_call(place, factor, weights, parts)

    logits = [g[0] for g in groups]
    away = grad_call(1, scalars, ids, coef, logits, vocab)
    arrived = send(away, SIBLING)
    kept = grad_call(0, scalars, ids, coef, logits, vocab)
    kl = kl + send(kl, SIBLING)
    head_grad = head_call(kept, arrived, [student0, student1, student2] + others).T
    return head_grad, kl[0, 0] / token_count


def solution(mesh):
    placed = (
        P("dp", None),
        P("dp", None),
        P(None, AXES),
        P(None, AXES),
        P(),
        P(),
    )
    return jax.shard_map(
        local,
        mesh=mesh,
        in_specs=placed,
        out_specs=(P(None, AXES), P()),
        check_vma=False,
    )
```

time: 184 us -> 175 us (0.951)
  waiting for transfers between devices: 55.9 us -> 33.7 us
  starting transfers between devices: 36.1 us -> 46.4 us
  other arithmetic: 3.8 us -> 6.57 us
    ppermute x27 -> x32, waiting for transfers between devices: 55.9 us -> 33.7 us  [send(): return lax.ppermute(array, AXES, perm)]
    ppermute x27 -> x32, starting transfers between devices: 36.1 us -> 46.4 us  [send(): return lax.ppermute(array, AXES, perm)]
    unnamed x18 -> x14, local copies, waits for them, and re-layouts: 9.59 us -> 0.03 us
    squeeze x3 -> x6, local copies, waits for them, and re-layouts: 0.21 us -> 8.39 us  [the longest x2 4.62 us: local(): on_t, on_s = (low_c[0], high_c[1])]
    another operation x1 -> x3, other arithmetic: 0.07 us -> 3.18 us  [the longest x1 3.05 us: local(): both_y = send(jnp.stack([low_x, high_x]), z_pair())]
    pallas_call x4 -> x3, Pallas kernels: 47.4 us -> 48.9 us  [logits_call(): pl.pallas_call(functools.partial(logits_kernel, shape), in_specs=[pl.Bloc...]
  transfers between devices with their start and end apart: 27 -> 32, of which waited for: 7 -> 10; matrix products, arithmetic and copies ran while one was open for 3% -> 9% of each run, Pallas kernels for 30% -> 33%
where the time goes in v3:
time: 175 us
  Pallas kernels  72.5 us (41%)
  starting transfers between devices  46.4 us (27%)
  waiting for transfers between devices  33.7 us (19%)
  local copies, waits for them, and re-layouts  10.8 us (6%)
  other arithmetic  6.57 us (4%)
  between operations  4.68 us (3%)
    pallas_call x3, Pallas kernels, logits_call(): pl.pallas_call(functools.partial(logits_kernel, shape), in_specs=[pl.Bloc...  48.9 us
    ppermute x32, starting transfers between devices, send(): return lax.ppermute(array, AXES, perm)  46.4 us
    ppermute x32, waiting for transfers between devices, send(): return lax.ppermute(array, AXES, perm)  33.7 us
    pallas_call x1, Pallas kernels, head_call(): pl.pallas_call(head_kernel, grid=(depth // tile,), in_specs=[whole, whole...  15.3 us
    pallas_call x2, Pallas kernels, grad_call(): pl.pallas_call(functools.partial(grad_kernel, part), in_specs=[pl.BlockSp...  6.41 us
    squeeze x2, local copies, waits for them, and re-layouts, local(): on_t, on_s = (low_c[0], high_c[1])  4.62 us
    squeeze x2, local copies, waits for them, and re-layouts, local(): far_xt, far_xs = (send(low_x[0], second(1)), send(high_x[1], second(-1)))  3.72 us
  transfers between devices with their start and end apart: 32, of which 10 were waited for; matrix products, arithmetic and copies ran while one was open for 9% of the time, Pallas kernels for 33%

profile of v3, /device:TPU:1, one launch (start us, length us, event | category | flops | bytes accessed | tf_op | source)
XLA Modules:
  0.0 174.7 jit_solution(2655315896886463889)
XLA Ops:
  0.6 1.5 collective-permute-start.4
  2.2 1.1 fusion.3
  3.5 1.4 collective-permute-start
  5.0 1.5 collective-permute-start.1
  6.5 9.6 %collective-permute-done = bf16[2,64,3072]{2,1,0:T(8,128)(2,1)S(1)} collective-permute-done((bf16[2,64,3072]{2,1,0:T(8,128)(2,1)S(1)}, bf16[2,64,3072]{2,1,0:T(8,128)(2,1)S(1)}, u32[]{:S(2)}, u32[]{:S(2)}) %collective-permute-start) | collective-permute-done | bytes 786464 | tf_op jit(solution)/shard_map/ppermute | solution.py:50
  16.3 2.7 %collective-permute-start.3 = (bf16[64,3072]{1,0:T(8,128)(2,1)S(1)}, bf16[64,3072]{1,0:T(8,128)(2,1)S(1)}, u32[]{:S(2)}, u32[]{:S(2)}) collective-permute-start(bf16[64,3072]{1,0:T(8,128)(2,1)S(1)} %slice_bitcast_fusion.4), channel_id=1, source_target_pairs={{0,96},{1,25},{2,98},{3,27},{4,100},{5,29},{6,102},{7,31},{8,104},... | collective-permute-start | bytes 1179656 | tf_op jit(solution)/shard_map/ppermute | solution.py:50
  19.1 5.3 %collective-permute-done.2 = bf16[64,3072]{1,0:T(8,128)(2,1)S(1)} collective-permute-done((bf16[64,3072]{1,0:T(8,128)(2,1)S(1)}, bf16[64,3072]{1,0:T(8,128)(2,1)S(1)}, u32[]{:S(2)}, u32[]{:S(2)}) %collective-permute-start.2) | collective-permute-done | bytes 393248 | tf_op jit(solution)/shard_map/ppermute | solution.py:50
  24.5 3.8 %collective-permute-start.10 = (bf16[2,256,1024]{2,1,0:T(8,128)(2,1)S(1)}, bf16[2,256,1024]{2,1,0:T(8,128)(2,1)}, u32[]{:S(2)}, u32[]{:S(2)}) collective-permute-start(bf16[2,256,1024]{2,1,0:T(8,128)(2,1)S(1)} %fusion.refs_1_), channel_id=1, source_target_pairs={{0,2},{1,7},{2,4},{3,1},{4,6},{5,3},{6,0},{7,5},{8,10},{9,15},{10,... | collective-permute-start | bytes 3145736 | tf_op jit(solution)/shard_map/ppermute | solution.py:50
  28.3 0.6 collective-permute-start.8
  28.9 2.1 %collective-permute-start.9 = (bf16[2,256,1024]{2,1,0:T(8,128)(2,1)S(1)}, bf16[2,256,1024]{2,1,0:T(8,128)(2,1)}, u32[]{:S(2)}, u32[]{:S(2)}) collective-permute-start(bf16[2,256,1024]{2,1,0:T(8,128)(2,1)S(1)} %fusion.refs_1_), channel_id=1, source_target_pairs={{0,24},{1,97},{2,26},{3,99},{4,28},{5,101},{6,30},{7,103},{8,0},{9... | collective-permute-start | bytes 3145736 | tf_op jit(solution)/shard_map/ppermute | solution.py:50
  31.4 0.9 slice-done
  32.3 1.3 pad_maximum_fusion.refs_0_
  33.7 2.7 %collective-permute-start.7 = (bf16[2,256,2048]{2,1,0:T(8,128)(2,1)S(1)}, bf16[2,256,2048]{2,1,0:T(8,128)(2,1)}, u32[]{:S(2)}, u32[]{:S(2)}) collective-permute-start(bf16[2,256,2048]{2,1,0:T(8,128)(2,1)S(1)} %pad_maximum_fusion.refs_0_), channel_id=1, source_target_pairs={{0,24},{1,97},{2,26},{3,99},{4,28},{5,101},{6,30},{7,103},{8,0},{9... | collective-permute-start | bytes 6291464 | tf_op jit(solution)/shard_map/ppermute | solution.py:50
  36.4 3.6 %collective-permute-done.10.refs_2_ = bf16[2,256,1024]{2,1,0:T(8,128)(2,1)} collective-permute-done((bf16[2,256,1024]{2,1,0:T(8,128)(2,1)S(1)}, bf16[2,256,1024]{2,1,0:T(8,128)(2,1)}, u32[]{:S(2)}, u32[]{:S(2)}) %collective-permute-start.10) | collective-permute-done | bytes 1048608 | tf_op jit(solution)/shard_map/ppermute | solution.py:50
  40.0 3.5 %collective-permute-done.8.refs_1_ = bf16[2,256,1024]{2,1,0:T(8,128)(2,1)} collective-permute-done((bf16[2,256,1024]{2,1,0:T(8,128)(2,1)S(1)}, bf16[2,256,1024]{2,1,0:T(8,128)(2,1)}, u32[]{:S(2)}, u32[]{:S(2)}) %collective-permute-start.8) | collective-permute-done | bytes 1048608 | tf_op jit(solution)/shard_map/ppermute | solution.py:50
  43.5 3.1 %pad_maximum_fusion.1 = bf16[2,2,256,1024]{3,2,1,0:T(8,128)(2,1)} fusion(bf16[1,2,256,1024]{3,2,1,0:T(8,128)(2,1)} %bitcast.15, bf16[1,2,256,1024]{3,2,1,0:T(8,128)(2,1)} %bitcast.14), kind=kLoop, calls=%fused_computation.6 | loop fusion | flops 1048576 | bytes 4194304 | tf_op jit(solution)/shard_map/stack | solution.py:388
  46.8 0.6 gather_fusion
  47.4 1.9 %slice_bitcast_fusion.3 = bf16[256,1024]{1,0:T(8,128)(2,1)} fusion(bf16[2,256,1024]{2,1,0:T(8,128)(2,1)} %collective-permute-done.8.refs_1_), kind=kLoop, calls=%fused_computation.17 | loop fusion | bytes 1048576 | tf_op jit(solution)/shard_map/squeeze | solution.py:387
  49.3 0.7 collective-permute-start.12
  49.9 1.9 %slice_bitcast_fusion.2 = bf16[256,1024]{1,0:T(8,128)(2,1)} fusion(bf16[2,256,1024]{2,1,0:T(8,128)(2,1)} %collective-permute-done.9.refs_4_), kind=kLoop, calls=%fused_computation.16 | loop fusion | bytes 1048576 | tf_op jit(solution)/shard_map/squeeze | solution.py:387
  51.8 2.0 %collective-permute-start.13 = (bf16[256,1024]{1,0:T(8,128)(2,1)}, bf16[256,1024]{1,0:T(8,128)(2,1)}, u32[]{:S(2)}, u32[]{:S(2)}) collective-permute-start(bf16[256,1024]{1,0:T(8,128)(2,1)} %slice_bitcast_fusion.2), channel_id=1, source_target_pairs={{0,24},{1,97},{2,26},{3,99},{4,28},{5,101},{6,30},{7,103},{8,0},{9... | collective-permute-start | bytes 1572872 | tf_op jit(solution)/shard_map/ppermute | solution.py:50
  54.0 15.3 %shard_map.86 = (f32[4,600,256]{2,1,0:T(8,128)}, f32[4,4,64]{2,1,0:T(4,128)S(1)}, bf16[256,4096]{1,0:T(8,128)(2,1)}) custom-call(s32[3]{0:T(128)S(1)} %pad_add_fusion.scalar_ref, s32[1,256]{1,0:T(1,128)S(1)} %slice.69.ids_ref, bf16[2,256,2048]{2,1,0:T(8,128)(2,1)S(1)} %pad_maximum_fusion.refs_0_, bf16[2,256,1024]{2,1,0:T(8,128)(2,1)S(1)} %fusion.refs_1_, ...), custom_call_target="tpu_custom_call" | custom-call | flops 4999610368 | bytes 19529728 | tf_op jit(solution)/shard_map/pallas_call | solution.py:192
  69.3 2.3 %collective-permute-done.12.refs_2_ = bf16[256,1024]{1,0:T(8,128)(2,1)} collective-permute-done((bf16[256,1024]{1,0:T(8,128)(2,1)}, bf16[256,1024]{1,0:T(8,128)(2,1)}, u32[]{:S(2)}, u32[]{:S(2)}) %collective-permute-start.12) | collective-permute-done | bytes 524320 | tf_op jit(solution)/shard_map/ppermute | solution.py:50
  72.1 3.5 %collective-permute-start.14 = (bf16[256,4096]{1,0:T(8,128)(2,1)}, bf16[256,4096]{1,0:T(8,128)(2,1)}, u32[]{:S(2)}, u32[]{:S(2)}) collective-permute-start(bf16[256,4096]{1,0:T(8,128)(2,1)} %get-tuple-element.49.refs_0_), channel_id=1, source_target_pairs={{0,1},{1,0},{2,3},{3,2},{4,5},{5,4},{6,7},{7,6},{8,9},{9,8},{10,11... | collective-permute-start | bytes 6291464 | tf_op jit(solution)/shard_map/ppermute | solution.py:50
  75.6 2.3 %slice_bitcast_fusion.1 = bf16[256,2048]{1,0:T(8,128)(2,1)} fusion(bf16[2,256,2048]{2,1,0:T(8,128)(2,1)} %collective-permute-done.6.refs_0_), kind=kLoop, calls=%fused_computation.10 | loop fusion | bytes 2097152 | tf_op jit(solution)/shard_map/squeeze | solution.py:392
  78.3 2.3 %slice_bitcast_fusion = bf16[256,2048]{1,0:T(8,128)(2,1)} fusion(bf16[2,256,2048]{2,1,0:T(8,128)(2,1)} %collective-permute-done.7.refs_3_), kind=kLoop, calls=%fused_computation.9 | loop fusion | bytes 2097152 | tf_op jit(solution)/shard_map/squeeze | solution.py:392
  80.6 2.7 %collective-permute-start.16 = (bf16[256,2048]{1,0:T(8,128)(2,1)}, bf16[256,2048]{1,0:T(8,128)(2,1)S(1)}, u32[]{:S(2)}, u32[]{:S(2)}) collective-permute-start(bf16[256,2048]{1,0:T(8,128)(2,1)} %slice_bitcast_fusion), channel_id=1, source_target_pairs={{0,24},{1,97},{2,26},{3,99},{4,28},{5,101},{6,30},{7,103},{8,0},{9... | collective-permute-start | bytes 3145736 | tf_op jit(solution)/shard_map/ppermute | solution.py:50
  83.4 0.7 collective-permute-start.17
  84.1 1.7 collective-permute-start.18
  85.8 18.3 %shard_map.87 = (f32[4,600,256]{2,1,0:T(8,128)}, f32[4,4,64]{2,1,0:T(4,128)S(1)}, f32[4,600,256]{2,1,0:T(8,128)}, f32[4,4,64]{2,1,0:T(4,128)S(1)}, bf16[512,4096]{1,0:T(8,128)(2,1)}) custom-call(s32[3]{0:T(128)S(1)} %pad_add_fusion.scalar_ref, s32[2,256]{1,0:T(2,128)S(1)} %slice.71.ids_ref, bf16[2,256,2048]{2,1,0:T(8,128)(2,1)} %collective-permute-done.6.refs_0_, ...), custom_call_target="tpu_custom_call" | custom-call | flops 9999220736 | bytes 19529728 | tf_op jit(solution)/shard_map/pallas_call | solution.py:192
  104.6 15.3 %shard_map.88 = (f32[4,600,256]{2,1,0:T(8,128)}, f32[4,4,64]{2,1,0:T(4,128)S(1)}, bf16[256,4096]{1,0:T(8,128)(2,1)}) custom-call(s32[3]{0:T(128)S(1)} %pad_add_fusion.scalar_ref, s32[1,256]{1,0:T(1,128)S(1)} %slice.73.ids_ref, bf16[256,2048]{1,0:T(8,128)(2,1)S(1)} %collective-permute-done.15.refs_0_, bf16[256,2048]{1,0:T(8,128)(2,1)S(1)} %collective-permute-done.16.refs_1_, ...), custom_call_target="tpu_custom_call" | custom-call | flops 4999610368 | bytes 19529728 | tf_op jit(solution)/shard_map/pallas_call | solution.py:192
  120.5 0.6 convert_reduce_fusion
  121.1 0.6 shard_map.89.refs_0_
  121.8 2.8 %collective-permute-start.20 = (f32[4,16,64]{2,1,0:T(8,128)S(1)}, f32[4,16,64]{2,1,0:T(8,128)S(1)}, u32[]{:S(2)}, u32[]{:S(2)}) collective-permute-start(f32[4,16,64]{2,1,0:T(8,128)S(1)} %shard_map.89.refs_0_), channel_id=1, source_target_pairs={{0,96},{1,97},{2,98},{3,99},{4,100},{5,101},{6,102},{7,103},{8,104... | collective-permute-start | bytes 49160 | tf_op jit(solution)/shard_map/ppermute | solution.py:50
  124.5 1.1 collective-permute-start.21
  126.4 2.4 %collective-permute-done.21.refs_3_ = f32[4,16,64]{2,1,0:T(8,128)S(1)} collective-permute-done((f32[4,16,64]{2,1,0:T(8,128)S(1)}, f32[4,16,64]{2,1,0:T(8,128)S(1)}, u32[]{:S(2)}, u32[]{:S(2)}) %collective-permute-start.21) | collective-permute-done | bytes 16416 | tf_op jit(solution)/shard_map/ppermute | solution.py:50
  128.9 1.2 collective-permute-start.22
  130.1 1.5 collective-permute-start.23
  131.6 1.3 collective-permute-start.24
  133.1 2.9 %collective-permute-done.24.refs_3_ = f32[4,16,64]{2,1,0:T(8,128)S(1)} collective-permute-done((f32[4,16,64]{2,1,0:T(8,128)S(1)}, f32[4,16,64]{2,1,0:T(8,128)S(1)}, u32[]{:S(2)}, u32[]{:S(2)}) %collective-permute-start.24) | collective-permute-done | bytes 16416 | tf_op jit(solution)/shard_map/ppermute | solution.py:50
  136.1 2.7 %collective-permute-start.26 = (f32[4,16,64]{2,1,0:T(8,128)S(1)}, f32[4,16,64]{2,1,0:T(8,128)S(1)}, u32[]{:S(2)}, u32[]{:S(2)}) collective-permute-start(f32[4,16,64]{2,1,0:T(8,128)S(1)} %shard_map.91.refs_0_), channel_id=1, source_target_pairs={{0,6},{1,7},{2,0},{3,1},{4,2},{5,3},{6,4},{7,5},{8,14},{9,15},{10,... | collective-permute-start | bytes 49160 | tf_op jit(solution)/shard_map/ppermute | solution.py:50
  138.8 0.7 collective-permute-start.27
  140.1 3.0 %collective-permute-done.27.refs_3_ = f32[4,16,64]{2,1,0:T(8,128)S(1)} collective-permute-done((f32[4,16,64]{2,1,0:T(8,128)S(1)}, f32[4,16,64]{2,1,0:T(8,128)S(1)}, u32[]{:S(2)}, u32[]{:S(2)}) %collective-permute-start.27) | collective-permute-done | bytes 16416 | tf_op jit(solution)/shard_map/ppermute | solution.py:50
  143.1 1.2 shard_map.92
  144.3 3.2 %shard_map.94 = bf16[596,1024]{1,0:T(8,128)(2,1)S(1)} custom-call(s32[3]{0:T(128)S(1)} %pad_add_fusion.scalar_ref, s32[4,256]{1,0:T(4,128)S(1)} %broadcast_select_fusion.1.ids_ref, f32[4,4,256]{2,1,0:T(4,128)S(1)} %get-tuple-element.60.coef_ref, f32[4,600,256]{2,1,0:T(8,128)} %get-tuple-element.61.refs_0_, f32[4,600,256]{2,1,0:T(8,128)} %get-tuple-element.62.refs_1_, ...), custom_call_target="tpu_custom_call" | custom-call | flops 6103040 | bytes 6103040 | tf_op jit(solution)/shard_map/pallas_call | solution.py:306
  147.5 5.3 %collective-permute-start.28 = (bf16[596,1024]{1,0:T(8,128)(2,1)S(1)}, bf16[596,1024]{1,0:T(8,128)(2,1)}, u32[]{:S(2)}, u32[]{:S(2)}) collective-permute-start(bf16[596,1024]{1,0:T(8,128)(2,1)S(1)} %shard_map.94), channel_id=1, source_target_pairs={{0,1},{1,0},{2,3},{3,2},{4,5},{5,4},{6,7},{7,6},{8,9},{9,8},{10,11... | collective-permute-start | bytes 3661832 | tf_op jit(solution)/shard_map/ppermute | solution.py:50
  153.2 3.2 %shard_map.93.ga_ref = bf16[596,1024]{1,0:T(8,128)(2,1)S(1)} custom-call(s32[3]{0:T(128)S(1)} %pad_add_fusion.scalar_ref, s32[4,256]{1,0:T(4,128)S(1)} %broadcast_select_fusion.1.ids_ref, f32[4,4,256]{2,1,0:T(4,128)S(1)} %get-tuple-element.60.coef_ref, f32[4,600,256]{2,1,0:T(8,128)} %get-tuple-element.61.refs_0_, f32[4,600,256]{2,1,0:T(8,128)} %get-tuple-element.62.refs_1_, ...), custom_call_target="tpu_custom_call" | custom-call | flops 6103040 | bytes 6103040 | tf_op jit(solution)/shard_map/pallas_call | solution.py:306
  158.3 15.3 %shard_map.95 = bf16[596,4096]{1,0:T(8,128)(2,1)} custom-call(bf16[596,1024]{1,0:T(8,128)(2,1)S(1)} %shard_map.93.ga_ref, bf16[596,1024]{1,0:T(8,128)(2,1)} %collective-permute-done.28.gb_ref, bf16[256,4096]{1,0:T(8,128)(2,1)} %get-tuple-element.49.refs_0_, bf16[512,4096]{1,0:T(8,128)(2,1)} %get-tuple-element.65.refs_1_, ...), custom_call_target="tpu_custom_call" | custom-call | flops 9999220736 | bytes 16777216 | tf_op jit(solution)/shard_map/pallas_call | solution.py:333
  (84 shorter events, 4.9 us)
Async XLA Ops:
  0.6 2.8 %copy-start.1 = (bf16[128,4096]{1,0:T(8,128)(2,1)S(1)}, bf16[128,4096]{1,0:T(8,128)(2,1)}, u32[]{:S(2)}) copy-start(bf16[128,4096]{1,0:T(8,128)(2,1)} %param.7) | copy-start | bytes 3145732
  0.6 2.8 %copy-start.2 = (bf16[128,4096]{1,0:T(8,128)(2,1)S(1)}, bf16[128,4096]{1,0:T(8,128)(2,1)}, u32[]{:S(2)}) copy-start(bf16[128,4096]{1,0:T(8,128)(2,1)} %param.8) | copy-start | bytes 3145732
  0.6 23.7 %collective-permute-start.4 = (bf16[596,4096]{1,0:T(8,128)(2,1)}, bf16[596,4096]{1,0:T(8,128)(2,1)}, u32[]{:S(2)}, u32[]{:S(2)}) collective-permute-start(bf16[596,4096]{1,0:T(8,128)(2,1)} %bitcast.35), channel_id=1, source_target_pairs={{0,1},{1,0},{2,3},{3,2},{4,5},{5,4},{6,7},{7,6},{8,9},{9,8},{10,11... | collective-permute-start | bytes 14647304 | tf_op jit(solution)/shard_map/ppermute | solution.py:50
  2.2 22.2 %collective-permute-start.5 = (bf16[596,4096]{1,0:T(8,128)(2,1)}, bf16[596,4096]{1,0:T(8,128)(2,1)}, u32[]{:S(2)}, u32[]{:S(2)}) collective-permute-start(bf16[596,4096]{1,0:T(8,128)(2,1)} %bitcast.31), channel_id=1, source_target_pairs={{0,1},{1,0},{2,3},{3,2},{4,5},{5,4},{6,7},{7,6},{8,9},{9,8},{10,11... | collective-permute-start | bytes 14647304 | tf_op jit(solution)/shard_map/ppermute | solution.py:50
  3.5 15.6 %copy-start = (bf16[2,64,2048]{2,1,0:T(8,128)(2,1)}, bf16[2,64,2048]{2,1,0:T(8,128)(2,1)S(1)}, u32[]{:S(2)}) copy-start(bf16[2,64,2048]{2,1,0:T(8,128)(2,1)S(1)} %fusion.2) | copy-start | bytes 1572868
  3.5 12.6 %collective-permute-start = (bf16[2,64,3072]{2,1,0:T(8,128)(2,1)S(1)}, bf16[2,64,3072]{2,1,0:T(8,128)(2,1)S(1)}, u32[]{:S(2)}, u32[]{:S(2)}) collective-permute-start(bf16[2,64,3072]{2,1,0:T(8,128)(2,1)S(1)} %pad_maximum_fusion.3), channel_id=1, source_target_pairs={{0,32},{1,9},{2,34},{3,11},{4,36},{5,13},{6,38},{7,15},{8,40},{9,1... | collective-permute-start | bytes 2359304 | tf_op jit(solution)/shard_map/ppermute | solution.py:50
  5.0 11.3 %collective-permute-start.1 = (bf16[2,64,3072]{2,1,0:T(8,128)(2,1)S(1)}, bf16[2,64,3072]{2,1,0:T(8,128)(2,1)S(1)}, u32[]{:S(2)}, u32[]{:S(2)}) collective-permute-start(bf16[2,64,3072]{2,1,0:T(8,128)(2,1)S(1)} %pad_maximum_fusion.3), channel_id=1, source_target_pairs={{0,96},{1,25},{2,98},{3,27},{4,100},{5,29},{6,102},{7,31},{8,104},... | collective-permute-start | bytes 2359304 | tf_op jit(solution)/shard_map/ppermute | solution.py:50
  16.1 15.2 %copy-start.3 = (bf16[2,64,3072]{2,1,0:T(8,128)(2,1)}, bf16[2,64,3072]{2,1,0:T(8,128)(2,1)S(1)}, u32[]{:S(2)}) copy-start(bf16[2,64,3072]{2,1,0:T(8,128)(2,1)S(1)} %collective-permute-done) | copy-start | bytes 2359300
  16.1 14.8 %copy-start.6 = (s32[4]{0:T(128)S(1)}, s32[4]{0:T(128)}, u32[]{:S(2)}) copy-start(s32[4]{0:T(128)} %constant.152.clone) | copy-start | bytes 52
  16.1 15.1 %copy-start.5 = (s32[2048]{0:T(1024)S(1)}, s32[2048]{0:T(1024)}, u32[]{:S(2)}) copy-start(s32[2048]{0:T(1024)} %param.11) | copy-start | bytes 24580
  16.2 8.2 %collective-permute-start.2 = (bf16[64,3072]{1,0:T(8,128)(2,1)S(1)}, bf16[64,3072]{1,0:T(8,128)(2,1)S(1)}, u32[]{:S(2)}, u32[]{:S(2)}) collective-permute-start(bf16[64,3072]{1,0:T(8,128)(2,1)S(1)} %slice_bitcast_fusion.5), channel_id=1, source_target_pairs={{0,32},{1,9},{2,34},{3,11},{4,36},{5,13},{6,38},{7,15},{8,40},{9,1... | collective-permute-start | bytes 1179656 | tf_op jit(solution)/shard_map/ppermute | solution.py:50
  16.3 8.1 %collective-permute-start.3 = (bf16[64,3072]{1,0:T(8,128)(2,1)S(1)}, bf16[64,3072]{1,0:T(8,128)(2,1)S(1)}, u32[]{:S(2)}, u32[]{:S(2)}) collective-permute-start(bf16[64,3072]{1,0:T(8,128)(2,1)S(1)} %slice_bitcast_fusion.4), channel_id=1, source_target_pairs={{0,96},{1,25},{2,98},{3,27},{4,100},{5,29},{6,102},{7,31},{8,104},... | collective-permute-start | bytes 1179656 | tf_op jit(solution)/shard_map/ppermute | solution.py:50
  24.5 15.6 %collective-permute-start.10 = (bf16[2,256,1024]{2,1,0:T(8,128)(2,1)S(1)}, bf16[2,256,1024]{2,1,0:T(8,128)(2,1)}, u32[]{:S(2)}, u32[]{:S(2)}) collective-permute-start(bf16[2,256,1024]{2,1,0:T(8,128)(2,1)S(1)} %fusion.refs_1_), channel_id=1, source_target_pairs={{0,2},{1,7},{2,4},{3,1},{4,6},{5,3},{6,0},{7,5},{8,10},{9,15},{10,... | collective-permute-start | bytes 3145736 | tf_op jit(solution)/shard_map/ppermute | solution.py:50
  28.3 15.3 %collective-permute-start.8 = (bf16[2,256,1024]{2,1,0:T(8,128)(2,1)S(1)}, bf16[2,256,1024]{2,1,0:T(8,128)(2,1)}, u32[]{:S(2)}, u32[]{:S(2)}) collective-permute-start(bf16[2,256,1024]{2,1,0:T(8,128)(2,1)S(1)} %fusion.refs_1_), channel_id=1, source_target_pairs={{0,8},{1,33},{2,10},{3,35},{4,12},{5,37},{6,14},{7,39},{8,16},{9,4... | collective-permute-start | bytes 3145736 | tf_op jit(solution)/shard_map/ppermute | solution.py:50
  28.9 14.6 %collective-permute-start.9 = (bf16[2,256,1024]{2,1,0:T(8,128)(2,1)S(1)}, bf16[2,256,1024]{2,1,0:T(8,128)(2,1)}, u32[]{:S(2)}, u32[]{:S(2)}) collective-permute-start(bf16[2,256,1024]{2,1,0:T(8,128)(2,1)S(1)} %fusion.refs_1_), channel_id=1, source_target_pairs={{0,24},{1,97},{2,26},{3,99},{4,28},{5,101},{6,30},{7,103},{8,0},{9... | collective-permute-start | bytes 3145736 | tf_op jit(solution)/shard_map/ppermute | solution.py:50
  31.3 1.0 slice-start
  33.6 38.0 %collective-permute-start.6 = (bf16[2,256,2048]{2,1,0:T(8,128)(2,1)S(1)}, bf16[2,256,2048]{2,1,0:T(8,128)(2,1)}, u32[]{:S(2)}, u32[]{:S(2)}) collective-permute-start(bf16[2,256,2048]{2,1,0:T(8,128)(2,1)S(1)} %pad_maximum_fusion.refs_0_), channel_id=1, source_target_pairs={{0,8},{1,33},{2,10},{3,35},{4,12},{5,37},{6,14},{7,39},{8,16},{9,4... | collective-permute-start | bytes 6291464 | tf_op jit(solution)/shard_map/ppermute | solution.py:50
  33.7 37.9 %collective-permute-start.7 = (bf16[2,256,2048]{2,1,0:T(8,128)(2,1)S(1)}, bf16[2,256,2048]{2,1,0:T(8,128)(2,1)}, u32[]{:S(2)}, u32[]{:S(2)}) collective-permute-start(bf16[2,256,2048]{2,1,0:T(8,128)(2,1)S(1)} %pad_maximum_fusion.refs_0_), channel_id=1, source_target_pairs={{0,24},{1,97},{2,26},{3,99},{4,28},{5,101},{6,30},{7,103},{8,0},{9... | collective-permute-start | bytes 6291464 | tf_op jit(solution)/shard_map/ppermute | solution.py:50
  46.6 25.5 %collective-permute-start.11 = (bf16[2,2,256,1024]{3,2,1,0:T(8,128)(2,1)}, bf16[2,2,256,1024]{3,2,1,0:T(8,128)(2,1)}, u32[]{:S(2)}, u32[]{:S(2)}) collective-permute-start(bf16[2,2,256,1024]{3,2,1,0:T(8,128)(2,1)} %pad_maximum_fusion.1), channel_id=1, source_target_pairs={{0,2},{1,7},{2,4},{3,1},{4,6},{5,3},{6,0},{7,5},{8,10},{9,15},{10,... | collective-permute-start | bytes 6291464 | tf_op jit(solution)/shard_map/ppermute | solution.py:50
  49.3 22.3 %collective-permute-start.12 = (bf16[256,1024]{1,0:T(8,128)(2,1)}, bf16[256,1024]{1,0:T(8,128)(2,1)}, u32[]{:S(2)}, u32[]{:S(2)}) collective-permute-start(bf16[256,1024]{1,0:T(8,128)(2,1)} %slice_bitcast_fusion.3), channel_id=1, source_target_pairs={{0,8},{1,33},{2,10},{3,35},{4,12},{5,37},{6,14},{7,39},{8,16},{9,4... | collective-permute-start | bytes 1572872 | tf_op jit(solution)/shard_map/ppermute | solution.py:50
  51.8 19.8 %collective-permute-start.13 = (bf16[256,1024]{1,0:T(8,128)(2,1)}, bf16[256,1024]{1,0:T(8,128)(2,1)}, u32[]{:S(2)}, u32[]{:S(2)}) collective-permute-start(bf16[256,1024]{1,0:T(8,128)(2,1)} %slice_bitcast_fusion.2), channel_id=1, source_target_pairs={{0,24},{1,97},{2,26},{3,99},{4,28},{5,101},{6,30},{7,103},{8,0},{9... | collective-permute-start | bytes 1572872 | tf_op jit(solution)/shard_map/ppermute | solution.py:50
  72.1 13.7 %collective-permute-start.14 = (bf16[256,4096]{1,0:T(8,128)(2,1)}, bf16[256,4096]{1,0:T(8,128)(2,1)}, u32[]{:S(2)}, u32[]{:S(2)}) collective-permute-start(bf16[256,4096]{1,0:T(8,128)(2,1)} %get-tuple-element.49.refs_0_), channel_id=1, source_target_pairs={{0,1},{1,0},{2,3},{3,2},{4,5},{5,4},{6,7},{7,6},{8,9},{9,8},{10,11... | collective-permute-start | bytes 6291464 | tf_op jit(solution)/shard_map/ppermute | solution.py:50
  77.9 26.1 %collective-permute-start.15 = (bf16[256,2048]{1,0:T(8,128)(2,1)}, bf16[256,2048]{1,0:T(8,128)(2,1)S(1)}, u32[]{:S(2)}, u32[]{:S(2)}) collective-permute-start(bf16[256,2048]{1,0:T(8,128)(2,1)} %slice_bitcast_fusion.1), channel_id=1, source_target_pairs={{0,8},{1,33},{2,10},{3,35},{4,12},{5,37},{6,14},{7,39},{8,16},{9,4... | collective-permute-start | bytes 3145736 | tf_op jit(solution)/shard_map/ppermute | solution.py:50
  80.6 23.5 %collective-permute-start.16 = (bf16[256,2048]{1,0:T(8,128)(2,1)}, bf16[256,2048]{1,0:T(8,128)(2,1)S(1)}, u32[]{:S(2)}, u32[]{:S(2)}) collective-permute-start(bf16[256,2048]{1,0:T(8,128)(2,1)} %slice_bitcast_fusion), channel_id=1, source_target_pairs={{0,24},{1,97},{2,26},{3,99},{4,28},{5,101},{6,30},{7,103},{8,0},{9... | collective-permute-start | bytes 3145736 | tf_op jit(solution)/shard_map/ppermute | solution.py:50
  83.4 20.7 %collective-permute-start.17 = (bf16[256,1024]{1,0:T(8,128)(2,1)}, bf16[256,1024]{1,0:T(8,128)(2,1)S(1)}, u32[]{:S(2)}, u32[]{:S(2)}) collective-permute-start(bf16[256,1024]{1,0:T(8,128)(2,1)} %collective-permute-done.12.refs_2_), channel_id=1, source_target_pairs={{0,2},{1,7},{2,4},{3,1},{4,6},{5,3},{6,0},{7,5},{8,10},{9,15},{10,... | collective-permute-start | bytes 1572872 | tf_op jit(solution)/shard_map/ppermute | solution.py:50
  84.1 20.0 %collective-permute-start.18 = (bf16[256,1024]{1,0:T(8,128)(2,1)}, bf16[256,1024]{1,0:T(8,128)(2,1)S(1)}, u32[]{:S(2)}, u32[]{:S(2)}) collective-permute-start(bf16[256,1024]{1,0:T(8,128)(2,1)} %collective-permute-done.13.refs_3_), channel_id=1, source_target_pairs={{0,2},{1,7},{2,4},{3,1},{4,6},{5,3},{6,0},{7,5},{8,10},{9,15},{10,... | collective-permute-start | bytes 1572872 | tf_op jit(solution)/shard_map/ppermute | solution.py:50
  104.1 54.2 %collective-permute-start.29 = (bf16[512,4096]{1,0:T(8,128)(2,1)}, bf16[512,4096]{1,0:T(8,128)(2,1)}, u32[]{:S(2)}, u32[]{:S(2)}) collective-permute-start(bf16[512,4096]{1,0:T(8,128)(2,1)} %get-tuple-element.65.refs_1_), channel_id=1, source_target_pairs={{0,1},{1,0},{2,3},{3,2},{4,5},{5,4},{6,7},{7,6},{8,9},{9,8},{10,11... | collective-permute-start | bytes 12582920 | tf_op jit(solution)/shard_map/ppermute | solution.py:50
  104.6 15.8 %copy-start.4 = (s32[2048]{0:T(1024)S(1)}, s32[2048]{0:T(1024)}, u32[]{:S(2)}) copy-start(s32[2048]{0:T(1024)} %param.12) | copy-start | bytes 24580
  120.0 38.3 %collective-permute-start.30 = (bf16[256,4096]{1,0:T(8,128)(2,1)}, bf16[256,4096]{1,0:T(8,128)(2,1)}, u32[]{:S(2)}, u32[]{:S(2)}) collective-permute-start(bf16[256,4096]{1,0:T(8,128)(2,1)} %get-tuple-element.66.refs_2_), channel_id=1, source_target_pairs={{0,1},{1,0},{2,3},{3,2},{4,5},{5,4},{6,7},{7,6},{8,9},{9,8},{10,11... | collective-permute-start | bytes 6291464 | tf_op jit(solution)/shard_map/ppermute | solution.py:50
  121.7 4.7 %collective-permute-start.19 = (f32[4,16,64]{2,1,0:T(8,128)S(1)}, f32[4,16,64]{2,1,0:T(8,128)S(1)}, u32[]{:S(2)}, u32[]{:S(2)}) collective-permute-start(f32[4,16,64]{2,1,0:T(8,128)S(1)} %shard_map.89.refs_0_), channel_id=1, source_target_pairs={{0,32},{1,33},{2,34},{3,35},{4,36},{5,37},{6,38},{7,39},{8,40},{9,... | collective-permute-start | bytes 49160 | tf_op jit(solution)/shard_map/ppermute | solution.py:50
  121.8 4.6 %collective-permute-start.20 = (f32[4,16,64]{2,1,0:T(8,128)S(1)}, f32[4,16,64]{2,1,0:T(8,128)S(1)}, u32[]{:S(2)}, u32[]{:S(2)}) collective-permute-start(f32[4,16,64]{2,1,0:T(8,128)S(1)} %shard_map.89.refs_0_), channel_id=1, source_target_pairs={{0,96},{1,97},{2,98},{3,99},{4,100},{5,101},{6,102},{7,103},{8,104... | collective-permute-start | bytes 49160 | tf_op jit(solution)/shard_map/ppermute | solution.py:50
  124.5 4.3 %collective-permute-start.21 = (f32[4,16,64]{2,1,0:T(8,128)S(1)}, f32[4,16,64]{2,1,0:T(8,128)S(1)}, u32[]{:S(2)}, u32[]{:S(2)}) collective-permute-start(f32[4,16,64]{2,1,0:T(8,128)S(1)} %shard_map.89.refs_0_), channel_id=1, source_target_pairs={{0,64},{1,65},{2,66},{3,67},{4,68},{5,69},{6,70},{7,71},{8,72},{9,... | collective-permute-start | bytes 49160 | tf_op jit(solution)/shard_map/ppermute | solution.py:50
  128.9 4.3 %collective-permute-start.22 = (f32[4,16,64]{2,1,0:T(8,128)S(1)}, f32[4,16,64]{2,1,0:T(8,128)S(1)}, u32[]{:S(2)}, u32[]{:S(2)}) collective-permute-start(f32[4,16,64]{2,1,0:T(8,128)S(1)} %shard_map.90.refs_0_), channel_id=1, source_target_pairs={{0,8},{1,9},{2,10},{3,11},{4,12},{5,13},{6,14},{7,15},{8,16},{9,17... | collective-permute-start | bytes 49160 | tf_op jit(solution)/shard_map/ppermute | solution.py:50
  130.1 3.0 %collective-permute-start.23 = (f32[4,16,64]{2,1,0:T(8,128)S(1)}, f32[4,16,64]{2,1,0:T(8,128)S(1)}, u32[]{:S(2)}, u32[]{:S(2)}) collective-permute-start(f32[4,16,64]{2,1,0:T(8,128)S(1)} %shard_map.90.refs_0_), channel_id=1, source_target_pairs={{0,24},{1,25},{2,26},{3,27},{4,28},{5,29},{6,30},{7,31},{8,0},{9,1... | collective-permute-start | bytes 49160 | tf_op jit(solution)/shard_map/ppermute | solution.py:50
  131.6 4.4 %collective-permute-start.24 = (f32[4,16,64]{2,1,0:T(8,128)S(1)}, f32[4,16,64]{2,1,0:T(8,128)S(1)}, u32[]{:S(2)}, u32[]{:S(2)}) collective-permute-start(f32[4,16,64]{2,1,0:T(8,128)S(1)} %shard_map.90.refs_0_), channel_id=1, source_target_pairs={{0,16},{1,17},{2,18},{3,19},{4,20},{5,21},{6,22},{7,23},{8,24},{9,... | collective-permute-start | bytes 49160 | tf_op jit(solution)/shard_map/ppermute | solution.py:50
  136.1 4.0 %collective-permute-start.25 = (f32[4,16,64]{2,1,0:T(8,128)S(1)}, f32[4,16,64]{2,1,0:T(8,128)S(1)}, u32[]{:S(2)}, u32[]{:S(2)}) collective-permute-start(f32[4,16,64]{2,1,0:T(8,128)S(1)} %shard_map.91.refs_0_), channel_id=1, source_target_pairs={{0,2},{1,3},{2,4},{3,5},{4,6},{5,7},{6,0},{7,1},{8,10},{9,11},{10,... | collective-permute-start | bytes 49160 | tf_op jit(solution)/shard_map/ppermute | solution.py:50
  136.1 4.0 %collective-permute-start.26 = (f32[4,16,64]{2,1,0:T(8,128)S(1)}, f32[4,16,64]{2,1,0:T(8,128)S(1)}, u32[]{:S(2)}, u32[]{:S(2)}) collective-permute-start(f32[4,16,64]{2,1,0:T(8,128)S(1)} %shard_map.91.refs_0_), channel_id=1, source_target_pairs={{0,6},{1,7},{2,0},{3,1},{4,2},{5,3},{6,4},{7,5},{8,14},{9,15},{10,... | collective-permute-start | bytes 49160 | tf_op jit(solution)/shard_map/ppermute | solution.py:50
  138.8 4.3 %collective-permute-start.27 = (f32[4,16,64]{2,1,0:T(8,128)S(1)}, f32[4,16,64]{2,1,0:T(8,128)S(1)}, u32[]{:S(2)}, u32[]{:S(2)}) collective-permute-start(f32[4,16,64]{2,1,0:T(8,128)S(1)} %shard_map.91.refs_0_), channel_id=1, source_target_pairs={{0,4},{1,5},{2,6},{3,7},{4,0},{5,1},{6,2},{7,3},{8,12},{9,13},{10,... | collective-permute-start | bytes 49160 | tf_op jit(solution)/shard_map/ppermute | solution.py:50
  147.5 10.7 %collective-permute-start.28 = (bf16[596,1024]{1,0:T(8,128)(2,1)S(1)}, bf16[596,1024]{1,0:T(8,128)(2,1)}, u32[]{:S(2)}, u32[]{:S(2)}) collective-permute-start(bf16[596,1024]{1,0:T(8,128)(2,1)S(1)} %shard_map.94), channel_id=1, source_target_pairs={{0,1},{1,0},{2,3},{3,2},{4,5},{5,4},{6,7},{7,6},{8,9},{9,8},{10,11... | collective-permute-start | bytes 3661832 | tf_op jit(solution)/shard_map/ppermute | solution.py:50
  152.8 3.6 %collective-permute-start.31 = (f32[1,1]{1,0:T(1,128)}, f32[1,1]{1,0:T(1,128)}, u32[]{:S(2)}, u32[]{:S(2)}) collective-permute-start(f32[1,1]{1,0:T(1,128)} %get-tuple-element.67), channel_id=1, source_target_pairs={{0,1},{1,0},{2,3},{3,2},{4,5},{5,4},{6,7},{7,6},{8,9},{9,8},{10,11... | collective-permute-start | bytes 20 | tf_op jit(solution)/shard_map/ppermute | solution.py:50

commit v4 on v3

--- a/solution.py
+++ b/solution.py
@@ -104,7 +104,7 @@
     return nt_all, ns_all, mean, add_all([p[3] for p in parts])
 
 
-def logits_kernel(shape, scalar_ref, ids_ref, *refs):
+def logits_kernel(shape, places, scalar_ref, ids_ref, *refs):
     n = len(shape)
     count = sum(len(kind) for group in shape for kind in group)
     pieces, heads, refs = list(refs[:count]), refs[count:count + 4], refs[count + 4:]
@@ -117,7 +117,7 @@
 
     def fetch(g, kind, j):
         found = hidden[g][kind]
-        source = found[j] if len(found) == 2 else found[0].at[(j,) if len(found[0].shape) == 3 else (g, j)]
+        source = found[j] if len(found) == 2 else found[0].at[(j,) if len(found[0].shape) == 3 else (places[g], j)]
         return pltpu.make_async_copy(source, hid.at[g, j, :, pl.ds(at[kind], source.shape[-1])], in_sems.at[g, kind, j])
 
     def fetch_head(h, lo, hi, sem):
@@ -182,7 +182,7 @@
     wait(stored)
 
 
-def logits_call(scalars, ids, groups, heads, after=()):
+def logits_call(scalars, ids, groups, heads, places):
     vocab, depth = heads[0].shape
     n, tokens = ids.shape
     rows = -(-vocab // 40) * 40
@@ -190,8 +190,8 @@
     pieces = [a for group in groups for kind in group for a in kind]
     shape = [[[None] * len(kind) for kind in group] for group in groups]
     out = pl.pallas_call(
-        functools.partial(logits_kernel, shape),
-        in_specs=[pl.BlockSpec(memory_space=pltpu.SMEM), vmem] + [hbm] * (len(pieces) + 4 + len(after)),
+        functools.partial(logits_kernel, shape, places),
+        in_specs=[pl.BlockSpec(memory_space=pltpu.SMEM), vmem] + [hbm] * (len(pieces) + 4),
         out_specs=[pl.BlockSpec(memory_space=pltpu.HBM), vmem] * n + [pl.BlockSpec(memory_space=pltpu.HBM)],
         out_shape=[
             pltpu.HBM((4, rows, tokens), F32),
@@ -207,7 +207,7 @@
         ],
         compiler_params=pltpu.CompilerParams(vmem_limit_bytes=(26 + 9 * n) * MIB),
         cost_estimate=pl.CostEstimate(flops=8 * n * vocab * tokens * depth, bytes_accessed=8 * vocab * depth, transcendentals=0),
-    )(scalars, ids, *pieces, *in_hbm(heads), *after)
+    )(scalars, ids, *pieces, *in_hbm(heads))
     return *[out[2 * g:2 * g + 2] for g in range(n)], out[-1]
 
 
@@ -252,9 +252,29 @@
     )(*parts)
 
 
-def finish_kernel(place_ref, factor_ref, weight_ref, *refs):
-    *ins, coef_ref, kl_ref, rows_ref = refs
-    n_t, n_s, mean, picked = join([[r[q] for q in range(4)] for r in ins])
+def reads_of(part, ins, held, sems):
+    return [pltpu.make_async_copy(ref.at[pl.ds(2 * part, 2)], held.at[j], sems.at[j]) for j, ref in enumerate(ins)]
+
+
+def write_grads(part, reads, held, scalar_ref, ids_ref, coef_ref, out_ref):
+    vocab, tokens = out_ref.shape[0], held.shape[3]
+    for j in range(SIDE):
+        reads[j].wait()
+        s, t = held[j, 0], held[j, 1]
+        n_s, factor, shift, pull = (coef_ref[j, q:q + 1, :] for q in range(4))
+        rows = lax.broadcasted_iota(jnp.int32, s.shape, 0)
+        inner = jnp.exp(s - n_s) * (s - t + shift)
+        inner = inner - jnp.where(rows == ids_ref[j:j + 1, :] - scalar_ref[part], pull, 0.0)
+        out_ref[:, j * tokens:(j + 1) * tokens] = (factor * inner).astype(jnp.bfloat16)[:vocab]
+
+
+def finish_kernel(place_ref, scalar_ref, factor_ref, weight_ref, ids_ref, *refs):
+    parts, logits = refs[:SIDE], refs[SIDE:2 * SIDE]
+    coef_ref, kl_ref, out_ref, rows_ref, held, sems = refs[2 * SIDE:]
+    reads = reads_of(1, logits, held, sems)
+    for read in reads:
+        read.start()
+    n_t, n_s, mean, picked = join([[r[q] for q in range(4)] for r in parts])
     kl_ref[...] = jnp.sum(weight_ref[...] * (mean + n_t - n_s), keepdims=True)
     pull = SAMPLED_WEIGHT * -(picked + n_t - n_s)
     for q, value in enumerate((n_s, factor_ref[...], pull - mean, pull)):
@@ -264,36 +284,36 @@
         for q in range(4):
             for i in range(SIDE):
                 coef_ref[j, q:q + 1, i * tokens:(i + 1) * tokens] = rows_ref[q, pl.ds(place_ref[j * SIDE + i], 1), :]
-
-
-def finish_call(place, factor, weight, parts):
-    vmem = pl.BlockSpec(memory_space=pltpu.VMEM)
-    tokens = factor.shape[1]
+    write_grads(1, reads, held, scalar_ref, ids_ref, coef_ref, out_ref)
+
+
+def finish_call(place, scalars, factor, weight, ids, parts, logits, vocab):
+    smem, vmem, hbm = (pl.BlockSpec(memory_space=m) for m in (pltpu.SMEM, pltpu.VMEM, pltpu.HBM))
+    tokens, rows = factor.shape[1], logits[0].shape[1]
     return pl.pallas_call(
         finish_kernel,
-        in_specs=[pl.BlockSpec(memory_space=pltpu.SMEM)] + [vmem] * (2 + len(parts)),
-        out_specs=[vmem, vmem],
-        out_shape=[jax.ShapeDtypeStruct((SIDE, 4, SIDE * tokens), F32), jax.ShapeDtypeStruct((1, 1), F32)],
-        scratch_shapes=[pltpu.VMEM((4, SIDE * SIDE, tokens), F32)],
-        compiler_params=SMALL,
-    )(place, factor, weight, *parts)
+        in_specs=[smem, smem] + [vmem] * (3 + len(parts)) + [hbm] * len(logits),
+        out_specs=[vmem, vmem, vmem],
+        out_shape=[
+            jax.ShapeDtypeStruct((SIDE, 4, SIDE * tokens), F32),
+            jax.ShapeDtypeStruct((1, 1), F32),
+            jax.ShapeDtypeStruct((vocab, SIDE * SIDE * tokens), jnp.bfloat16),
+        ],
+        scratch_shapes=[
+            pltpu.VMEM((4, SIDE * SIDE, tokens), F32),
+            pltpu.VMEM((SIDE, 2, rows, SIDE * tokens), F32),
+            pltpu.SemaphoreType.DMA((SIDE,)),
+        ],
+        compiler_params=pltpu.CompilerParams(vmem_limit_bytes=16 * MIB),
+    )(place, scalars, factor, weight, ids, *parts, *in_hbm(logits))
 
 
 def grad_kernel(part, scalar_ref, ids_ref, coef_ref, *refs):
     *ins, out_ref, held, sems = refs
-    vocab = out_ref.shape[0]
-    copies = [pltpu.make_async_copy(ref.at[pl.ds(2 * part, 2)], held.at[j], sems.at[j]) for j, ref in enumerate(ins)]
-    for copy in copies:
-        copy.start()
-    tokens = held.shape[3]
-    for j in range(SIDE):
-        copies[j].wait()
-        s, t = held[j, 0], held[j, 1]
-        n_s, factor, shift, pull = (coef_ref[j, q:q + 1, :] for q in range(4))
-        rows = lax.broadcasted_iota(jnp.int32, s.shape, 0)
-        inner = jnp.exp(s - n_s) * (s - t + shift)
-        inner = inner - jnp.where(rows == ids_ref[j:j + 1, :] - scalar_ref[part], pull, 0.0)
-        out_ref[:, j * tokens:(j + 1) * tokens] = (factor * inner).astype(jnp.bfloat16)[:vocab]
+    reads = reads_of(part, ins, held, sems)
+    for read in reads:
+        read.start()
+    write_grads(part, reads, held, scalar_ref, ids_ref, coef_ref, out_ref)
 
 
 def in_hbm(arrays):
@@ -314,8 +334,13 @@
     )(scalars, ids, coef, *in_hbm(logits))
 
 
-def head_kernel(ga_ref, gb_ref, *refs):
-    *hids, out_ref = refs
+def head_kernel(kla_ref, klb_ref, ga_ref, gb_ref, *refs):
+    *hids, out_ref, kl_ref = refs
+
+    @pl.when(pl.program_id(0) == 0)
+    def _():
+        kl_ref[...] = kla_ref[...] + klb_ref[...]
+
     half = len(hids) // 2
     total = None
     for g, group in ((ga_ref, hids[:half]), (gb_ref, hids[half:])):
@@ -325,20 +350,21 @@
     out_ref[...] = total.astype(jnp.bfloat16)
 
 
-def head_call(ga, gb, hids):
+def head_call(kls, ga, gb, hids):
     vocab, tokens = ga.shape
     depth = hids[0].shape[-1]
     tile = 1024
     whole = pl.BlockSpec((vocab, tokens), lambda i: (0, 0))
+    one = pl.BlockSpec((1, 1), lambda i: (0, 0))
     return pl.pallas_call(
         head_kernel,
         grid=(depth // tile,),
-        in_specs=[whole, whole] + [pl.BlockSpec((h.shape[0], tile), lambda i: (0, i)) for h in hids],
-        out_specs=pl.BlockSpec((vocab, tile), lambda i: (0, i)),
-        out_shape=jax.ShapeDtypeStruct((vocab, depth), jnp.bfloat16),
+        in_specs=[one, one, whole, whole] + [pl.BlockSpec((h.shape[0], tile), lambda i: (0, i)) for h in hids],
+        out_specs=[pl.BlockSpec((vocab, tile), lambda i: (0, i)), one],
+        out_shape=[jax.ShapeDtypeStruct((vocab, depth), jnp.bfloat16), jax.ShapeDtypeStruct((1, 1), F32)],
         compiler_params=pltpu.CompilerParams(vmem_limit_bytes=44 * MIB),
         cost_estimate=pl.CostEstimate(flops=4 * vocab * tokens * depth, bytes_accessed=4 * tokens * depth, transcendentals=0),
-    )(ga, gb, *in_hbm(hids))
+    )(*kls, ga, gb, *in_hbm(hids))
 
 
 def local(teacher_hidden, student_hidden, teacher_head, student_head, sampled_ids, valid_mask):
@@ -363,6 +389,7 @@
     token_count = jnp.sum(all_weights)
     weights = mine(all_weights)
     factor = LOSS_SCALE * weights / jnp.sqrt(token_count)
+    weights = weights / token_count
     row_of = flat(x, y, tensor // 2, core) * vocab
     other_of = flat(x, y, tensor // 2, 1 - core) * vocab
     parity = (tensor // 2) % 2
@@ -379,6 +406,7 @@
     heads = (sa, ta, sb, tb)
     row = [own, low, high, jnp.stack([far_t, far_s])]
     row_x = jnp.concatenate([a[:, :, common:] for a in row], axis=1)
+    row_x, *row = lax.optimization_barrier((row_x, *row))
     row_c = jnp.concatenate([a[:, :, :common] for a in row], axis=1)
     low_x, high_x = send(row_x, second(1)), send(row_x, second(-1))
     row_y = send(row_x, z_pair())
@@ -386,35 +414,33 @@
     low_x, high_x, row_y = lax.optimization_barrier((low_x, high_x, row_y))
     far_xt, far_xs = send(low_x[0], second(1)), send(high_x[1], second(-1))
     both_y = send(jnp.stack([low_x, high_x]), z_pair())
-    group0, student0 = logits_call(scalars, ids[0:1], [((row_c,), (row_x,), (row_y,))], heads)
-    low_c, high_c, both_y, far_xt, far_xs, student0, *group0 = lax.optimization_barrier(
-        (low_c, high_c, both_y, far_xt, far_xs, student0, *group0))
+    low_c, high_c, far_xt, far_xs = lax.optimization_barrier((low_c, high_c, far_xt, far_xs))
     on_t, on_s = low_c[0], high_c[1]
     far_ct, far_cs = send(on_t, second(1)), send(on_s, second(-1))
+    both_y, on_t, on_s = lax.optimization_barrier((both_y, on_t, on_s))
     far_yt, far_ys = send(far_xt, z_pair()), send(far_xs, z_pair())
+    group0, group1, student0 = logits_call(
+        scalars, ids[0:2], [((row_c,), (row_x,), (row_y,)), ((low_c,), (low_x,), (both_y,))], heads, (0, 0))
+    far_ct, far_cs, far_yt, far_ys, student0 = lax.optimization_barrier((far_ct, far_cs, far_yt, far_ys, student0))
     other0 = send(student0, SIBLING)
-    group1, group2, student1 = logits_call(scalars, ids[1:3], [
-        ((low_c,), (low_x,), (both_y,)), ((high_c,), (high_x,), (both_y,))], heads, (other0,))
-    far_ct, far_cs, far_yt, far_ys, student1 = lax.optimization_barrier((far_ct, far_cs, far_yt, far_ys, student1))
-    other1 = send(student1, SIBLING)
-    group3, student2 = logits_call(scalars, ids[3:4], [((far_ct, far_cs), (far_xt, far_xs), (far_yt, far_ys))], heads, (group1[1],))
+    group2, group3, student1 = logits_call(
+        scalars, ids[2:4],
+        [((high_c,), (high_x,), (both_y,)), ((far_ct, far_cs), (far_xt, far_xs), (far_yt, far_ys))], heads, (1, 0))
     groups = [group0, group1, group2, group3]
-    others = [other0, other1, send(student2, SIBLING)]
+    others = [other0, send(student1, SIBLING)]
 
     total = order_call(place, [g[1] for g in groups])
     for axis in range(3):
         parts = [total, send(total, along(axis, 1)), send(total, along(axis, -1)), send(total, along(axis, 2))]
         if axis < 2:
             total = join_call(parts)
-    coef, kl = finish_call(place, factor, weights, parts)
-
     logits = [g[0] for g in groups]
-    away = grad_call(1, scalars, ids, coef, logits, vocab)
+    coef, kl, away = finish_call(place, scalars, factor, weights, ids, parts, logits, vocab)
     arrived = send(away, SIBLING)
+    other_kl = send(kl, SIBLING)
     kept = grad_call(0, scalars, ids, coef, logits, vocab)
-    kl = kl + send(kl, SIBLING)
-    head_grad = head_call(kept, arrived, [student0, student1, student2] + others).T
-    return head_grad, kl[0, 0] / token_count
+    head_grad, kl = head_call((kl, other_kl), kept, arrived, [student0, student1] + others)
+    return head_grad.T, kl.reshape(())
 
 
 def solution(mesh):

time: 175 us -> 168 us (0.960)
  Pallas kernels: 72.5 us -> 57.9 us
  waiting for transfers between devices: 33.7 us -> 46.2 us
  local copies, waits for them, and re-layouts: 10.8 us -> 5.83 us
  starting transfers between devices: 46.4 us -> 49.7 us
  between operations: 4.68 us -> 1.74 us
    ppermute x32 -> x31, waiting for transfers between devices: 33.7 us -> 46.2 us  [send(): return lax.ppermute(array, AXES, perm)]
    pallas_call x5 -> x4, Pallas kernels: 65.5 us -> 54 us  [the longest x2 34.8 us: logits_call(): pl.pallas_call(functools.partial(logits_kernel, shape, places), in_specs=...]
    ppermute x32 -> x31, starting transfers between devices: 46.4 us -> 49.7 us  [send(): return lax.ppermute(array, AXES, perm)]
    pallas_call x2 -> x1, Pallas kernels: 6.41 us -> 3.2 us  [grad_call(): pl.pallas_call(functools.partial(grad_kernel, part), in_specs=[pl.BlockSp...]
    squeeze x2, local copies, waits for them, and re-layouts: 3.72 us -> 1.67 us  [local(): far_xt, far_xs = (send(low_x[0], second(1)), send(high_x[1], second(-1)))]
    squeeze x2, local copies, waits for them, and re-layouts: 4.62 us -> 2.65 us  [local(): on_t, on_s = (low_c[0], high_c[1])]
  transfers between devices with their start and end apart: 32 -> 31, of which waited for: 10 -> 12; matrix products, arithmetic and copies ran while one was open for 9% -> 7% of each run, Pallas kernels for 33% -> 15%
where the time goes in v4:
time: 168 us; the launch traced here: 167 us
  Pallas kernels  57.9 us (34%)
  starting transfers between devices  49.7 us (30%)
  waiting for transfers between devices  46.2 us (28%)
  other arithmetic  5.99 us (4%)
  local copies, waits for them, and re-layouts  5.83 us (3%)
  between operations  1.74 us (1%)
    ppermute x31, starting transfers between devices, send(): return lax.ppermute(array, AXES, perm)  49.7 us
    ppermute x31, waiting for transfers between devices, send(): return lax.ppermute(array, AXES, perm)  46.2 us
    pallas_call x2, Pallas kernels, logits_call(): pl.pallas_call(functools.partial(logits_kernel, shape, places), in_specs=...  34.8 us
    pallas_call x1, Pallas kernels, head_call(): pl.pallas_call(head_kernel, grid=(depth // tile,), in_specs=[one, one, wh...  15.6 us
    pallas_call x1, Pallas kernels, finish_call(): pl.pallas_call(finish_kernel, in_specs=[smem, smem] + [vmem] * (3 + len(p...  3.64 us
  transfers between devices with their start and end apart: 31, of which 12 were waited for; matrix products, arithmetic and copies ran while one was open for 7% of the time, Pallas kernels for 15%

profile of v4, /device:TPU:1, one launch (start us, length us, event | category | flops | bytes accessed | tf_op | source)
XLA Modules:
  0.0 167.3 jit_solution(8522224190702968875)
XLA Ops:
  0.6 1.5 collective-permute-start.4
  2.2 1.1 fusion.1
  3.5 1.4 collective-permute-start
  5.0 2.2 %collective-permute-start.1 = (bf16[2,64,3072]{2,1,0:T(8,128)(2,1)S(1)}, bf16[2,64,3072]{2,1,0:T(8,128)(2,1)S(1)}, u32[]{:S(2)}, u32[]{:S(2)}) collective-permute-start(bf16[2,64,3072]{2,1,0:T(8,128)(2,1)S(1)} %pad_maximum_fusion.4), channel_id=1, source_target_pairs={{0,96},{1,25},{2,98},{3,27},{4,100},{5,29},{6,102},{7,31},{8,104},... | collective-permute-start | bytes 2359304 | tf_op jit(solution)/shard_map/ppermute | solution.py:50
  7.2 8.9 %collective-permute-done = bf16[2,64,3072]{2,1,0:T(8,128)(2,1)S(1)} collective-permute-done((bf16[2,64,3072]{2,1,0:T(8,128)(2,1)S(1)}, bf16[2,64,3072]{2,1,0:T(8,128)(2,1)S(1)}, u32[]{:S(2)}, u32[]{:S(2)}) %collective-permute-start) | collective-permute-done | bytes 786464 | tf_op jit(solution)/shard_map/ppermute | solution.py:50
  16.3 3.4 %collective-permute-start.3 = (bf16[64,3072]{1,0:T(8,128)(2,1)S(1)}, bf16[64,3072]{1,0:T(8,128)(2,1)S(1)}, u32[]{:S(2)}, u32[]{:S(2)}) collective-permute-start(bf16[64,3072]{1,0:T(8,128)(2,1)S(1)} %slice_bitcast_fusion.4), channel_id=1, source_target_pairs={{0,96},{1,25},{2,98},{3,27},{4,100},{5,29},{6,102},{7,31},{8,104},... | collective-permute-start | bytes 1179656 | tf_op jit(solution)/shard_map/ppermute | solution.py:50
  19.7 4.6 %collective-permute-done.2 = bf16[64,3072]{1,0:T(8,128)(2,1)S(1)} collective-permute-done((bf16[64,3072]{1,0:T(8,128)(2,1)S(1)}, bf16[64,3072]{1,0:T(8,128)(2,1)S(1)}, u32[]{:S(2)}, u32[]{:S(2)}) %collective-permute-start.2) | collective-permute-done | bytes 393248 | tf_op jit(solution)/shard_map/ppermute | solution.py:50
  24.6 1.0 collective-permute-start.6
  25.6 1.8 %collective-permute-start.7 = (bf16[2,256,1024]{2,1,0:T(8,128)(2,1)S(1)}, bf16[2,256,1024]{2,1,0:T(8,128)(2,1)S(1)}, u32[]{:S(2)}, u32[]{:S(2)}) collective-permute-start(bf16[2,256,1024]{2,1,0:T(8,128)(2,1)S(1)} %pad_maximum_fusion.2.refs_1_), channel_id=1, source_target_pairs={{0,24},{1,97},{2,26},{3,99},{4,28},{5,101},{6,30},{7,103},{8,0},{9... | collective-permute-start | bytes 3145736 | tf_op jit(solution)/shard_map/ppermute | solution.py:50
  27.4 3.7 %collective-permute-start.8 = (bf16[2,256,1024]{2,1,0:T(8,128)(2,1)S(1)}, bf16[2,256,1024]{2,1,0:T(8,128)(2,1)}, u32[]{:S(2)}, u32[]{:S(2)}) collective-permute-start(bf16[2,256,1024]{2,1,0:T(8,128)(2,1)S(1)} %pad_maximum_fusion.2.refs_1_), channel_id=1, source_target_pairs={{0,2},{1,7},{2,4},{3,1},{4,6},{5,3},{6,0},{7,5},{8,10},{9,15},{10,... | collective-permute-start | bytes 3145736 | tf_op jit(solution)/shard_map/ppermute | solution.py:50
  31.3 1.6 pad_maximum_fusion.refs_0_
  32.8 1.3 collective-permute-start.10
  34.7 5.3 %collective-permute-done.6.refs_4_ = bf16[2,256,1024]{2,1,0:T(8,128)(2,1)S(1)} collective-permute-done((bf16[2,256,1024]{2,1,0:T(8,128)(2,1)S(1)}, bf16[2,256,1024]{2,1,0:T(8,128)(2,1)S(1)}, u32[]{:S(2)}, u32[]{:S(2)}) %collective-permute-start.6) | collective-permute-done | bytes 1048608 | tf_op jit(solution)/shard_map/ppermute | solution.py:50
  40.0 2.9 %collective-permute-done.8.refs_2_ = bf16[2,256,1024]{2,1,0:T(8,128)(2,1)} collective-permute-done((bf16[2,256,1024]{2,1,0:T(8,128)(2,1)S(1)}, bf16[2,256,1024]{2,1,0:T(8,128)(2,1)}, u32[]{:S(2)}, u32[]{:S(2)}) %collective-permute-start.8) | collective-permute-done | bytes 1048608 | tf_op jit(solution)/shard_map/ppermute | solution.py:50
  42.9 1.5 pad_maximum_fusion.1
  44.4 3.5 %collective-permute-start.13 = (bf16[2,2,256,1024]{3,2,1,0:T(8,128)(2,1)}, bf16[2,2,256,1024]{3,2,1,0:T(8,128)(2,1)}, u32[]{:S(2)}, u32[]{:S(2)}) collective-permute-start(bf16[2,2,256,1024]{3,2,1,0:T(8,128)(2,1)} %pad_maximum_fusion.1), channel_id=1, source_target_pairs={{0,2},{1,7},{2,4},{3,1},{4,6},{5,3},{6,0},{7,5},{8,10},{9,15},{10,... | collective-permute-start | bytes 6291464 | tf_op jit(solution)/shard_map/ppermute | solution.py:50
  47.9 0.8 slice_bitcast_fusion.3
  48.7 0.8 slice_bitcast_fusion.2
  49.6 2.7 %collective-permute-start.12 = (bf16[256,1024]{1,0:T(8,128)(2,1)}, bf16[256,1024]{1,0:T(8,128)(2,1)}, u32[]{:S(2)}, u32[]{:S(2)}) collective-permute-start(bf16[256,1024]{1,0:T(8,128)(2,1)} %slice_bitcast_fusion.2), channel_id=1, source_target_pairs={{0,24},{1,97},{2,26},{3,99},{4,28},{5,101},{6,30},{7,103},{8,0},{9... | collective-permute-start | bytes 1572872 | tf_op jit(solution)/shard_map/ppermute | solution.py:50
  52.2 0.6 gather_fusion
  53.0 15.0 %collective-permute-done.11.refs_5_ = bf16[256,1024]{1,0:T(8,128)(2,1)} collective-permute-done((bf16[256,1024]{1,0:T(8,128)(2,1)}, bf16[256,1024]{1,0:T(8,128)(2,1)}, u32[]{:S(2)}, u32[]{:S(2)}) %collective-permute-start.11) | collective-permute-done | bytes 524320 | tf_op jit(solution)/shard_map/ppermute | solution.py:50
  68.1 1.3 slice_bitcast_fusion.1
  69.4 1.0 collective-permute-start.14
  70.4 1.3 slice_bitcast_fusion
  71.7 1.8 %collective-permute-start.15 = (bf16[256,2048]{1,0:T(8,128)(2,1)S(1)}, bf16[256,2048]{1,0:T(8,128)(2,1)S(1)}, u32[]{:S(2)}, u32[]{:S(2)}) collective-permute-start(bf16[256,2048]{1,0:T(8,128)(2,1)S(1)} %slice_bitcast_fusion), channel_id=1, source_target_pairs={{0,24},{1,97},{2,26},{3,99},{4,28},{5,101},{6,30},{7,103},{8,0},{9... | collective-permute-start | bytes 3145736 | tf_op jit(solution)/shard_map/ppermute | solution.py:50
  73.6 3.7 %collective-permute-start.16 = (bf16[256,1024]{1,0:T(8,128)(2,1)}, bf16[256,1024]{1,0:T(8,128)(2,1)S(1)}, u32[]{:S(2)}, u32[]{:S(2)}) collective-permute-start(bf16[256,1024]{1,0:T(8,128)(2,1)} %collective-permute-done.11.refs_5_), channel_id=1, source_target_pairs={{0,2},{1,7},{2,4},{3,1},{4,6},{5,3},{6,0},{7,5},{8,10},{9,15},{10,... | collective-permute-start | bytes 1572872 | tf_op jit(solution)/shard_map/ppermute | solution.py:50
  77.4 0.3 collective-permute-start.17
  77.6 17.6 %shard_map.86 = (f32[4,600,256]{2,1,0:T(8,128)}, f32[4,4,64]{2,1,0:T(4,128)S(1)}, f32[4,600,256]{2,1,0:T(8,128)}, f32[4,4,64]{2,1,0:T(4,128)S(1)}, bf16[512,4096]{1,0:T(8,128)(2,1)}) custom-call(s32[3]{0:T(128)S(1)} %pad_add_fusion.scalar_ref, s32[2,256]{1,0:T(2,128)S(1)} %slice.55.ids_ref, bf16[2,256,2048]{2,1,0:T(8,128)(2,1)} %pad_maximum_fusion.refs_0_, ...), custom_call_target="tpu_custom_call" | custom-call | flops 9999220736 | bytes 19529728 | tf_op jit(solution)/shard_map/pallas_call | solution.py:192
  95.3 17.3 %shard_map.87 = (f32[4,600,256]{2,1,0:T(8,128)}, f32[4,4,64]{2,1,0:T(4,128)S(1)}, f32[4,600,256]{2,1,0:T(8,128)}, f32[4,4,64]{2,1,0:T(4,128)S(1)}, bf16[512,4096]{1,0:T(8,128)(2,1)}) custom-call(s32[3]{0:T(128)S(1)} %pad_add_fusion.scalar_ref, s32[2,256]{1,0:T(2,128)S(1)} %slice.71.ids_ref, bf16[2,256,2048]{2,1,0:T(8,128)(2,1)} %collective-permute-done.10.refs_0_, ...), custom_call_target="tpu_custom_call" | custom-call | flops 9999220736 | bytes 19529728 | tf_op jit(solution)/shard_map/pallas_call | solution.py:192
  112.5 3.8 %collective-permute-start.30 = (bf16[512,4096]{1,0:T(8,128)(2,1)}, bf16[512,4096]{1,0:T(8,128)(2,1)}, u32[]{:S(2)}, u32[]{:S(2)}) collective-permute-start(bf16[512,4096]{1,0:T(8,128)(2,1)} %get-tuple-element.73.refs_1_), channel_id=1, source_target_pairs={{0,1},{1,0},{2,3},{3,2},{4,5},{5,4},{6,7},{7,6},{8,9},{9,8},{10,11... | collective-permute-start | bytes 12582920 | tf_op jit(solution)/shard_map/ppermute | solution.py:50
  116.5 0.6 convert_reduce_fusion
  117.1 0.6 shard_map.88.refs_0_
  117.6 0.4 collective-permute-start.18
  118.1 3.0 %collective-permute-start.19 = (f32[4,16,64]{2,1,0:T(8,128)S(1)}, f32[4,16,64]{2,1,0:T(8,128)S(1)}, u32[]{:S(2)}, u32[]{:S(2)}) collective-permute-start(f32[4,16,64]{2,1,0:T(8,128)S(1)} %shard_map.88.refs_0_), channel_id=1, source_target_pairs={{0,96},{1,97},{2,98},{3,99},{4,100},{5,101},{6,102},{7,103},{8,104... | collective-permute-start | bytes 49160 | tf_op jit(solution)/shard_map/ppermute | solution.py:50
  121.0 1.1 collective-permute-start.20
  122.9 2.4 %collective-permute-done.20.refs_3_ = f32[4,16,64]{2,1,0:T(8,128)S(1)} collective-permute-done((f32[4,16,64]{2,1,0:T(8,128)S(1)}, f32[4,16,64]{2,1,0:T(8,128)S(1)}, u32[]{:S(2)}, u32[]{:S(2)}) %collective-permute-start.20) | collective-permute-done | bytes 16416 | tf_op jit(solution)/shard_map/ppermute | solution.py:50
  125.5 2.6 %collective-permute-start.22 = (f32[4,16,64]{2,1,0:T(8,128)S(1)}, f32[4,16,64]{2,1,0:T(8,128)S(1)}, u32[]{:S(2)}, u32[]{:S(2)}) collective-permute-start(f32[4,16,64]{2,1,0:T(8,128)S(1)} %shard_map.89.refs_0_), channel_id=1, source_target_pairs={{0,24},{1,25},{2,26},{3,27},{4,28},{5,29},{6,30},{7,31},{8,0},{9,1... | collective-permute-start | bytes 49160 | tf_op jit(solution)/shard_map/ppermute | solution.py:50
  128.3 0.6 divide_bitcast_fusion
  129.4 3.0 %collective-permute-done.23.refs_3_ = f32[4,16,64]{2,1,0:T(8,128)S(1)} collective-permute-done((f32[4,16,64]{2,1,0:T(8,128)S(1)}, f32[4,16,64]{2,1,0:T(8,128)S(1)}, u32[]{:S(2)}, u32[]{:S(2)}) %collective-permute-start.23) | collective-permute-done | bytes 16416 | tf_op jit(solution)/shard_map/ppermute | solution.py:50
  132.4 1.4 collective-permute-start.24
  133.8 1.4 collective-permute-start.25
  135.2 0.5 collective-permute-start.26
  135.7 0.8 collective-permute-done.24.refs_1_
  136.6 2.9 %collective-permute-done.26.refs_3_ = f32[4,16,64]{2,1,0:T(8,128)S(1)} collective-permute-done((f32[4,16,64]{2,1,0:T(8,128)S(1)}, f32[4,16,64]{2,1,0:T(8,128)S(1)}, u32[]{:S(2)}, u32[]{:S(2)}) %collective-permute-start.26) | collective-permute-done | bytes 16416 | tf_op jit(solution)/shard_map/ppermute | solution.py:50
  139.4 3.6 %shard_map.91 = (f32[4,4,256]{2,1,0:T(4,128)S(1)}, f32[1,1]{1,0:T(1,128)}, bf16[596,1024]{1,0:T(8,128)(2,1)S(1)}) custom-call(s32[16]{0:T(128)S(1)} %select_n.134.place_ref, s32[3]{0:T(128)S(1)} %pad_add_fusion.scalar_ref, f32[16,64]{1,0:T(8,128)S(1)} %get-tuple-element.85.factor_ref, f32[16,64]{1,0:T(8,128)S(1)} %get-tuple-element.84.weight_ref, ...), custom_call_target="tpu_custom_call" | custom-call | tf_op jit(solution)/shard_map/pallas_call | solution.py:293
  143.1 5.3 %collective-permute-start.28 = (bf16[596,1024]{1,0:T(8,128)(2,1)S(1)}, bf16[596,1024]{1,0:T(8,128)(2,1)S(1)}, u32[]{:S(2)}, u32[]{:S(2)}) collective-permute-start(bf16[596,1024]{1,0:T(8,128)(2,1)S(1)} %get-tuple-element.71), channel_id=1, source_target_pairs={{0,1},{1,0},{2,3},{3,2},{4,5},{5,4},{6,7},{7,6},{8,9},{9,8},{10,11... | collective-permute-start | bytes 3661832 | tf_op jit(solution)/shard_map/ppermute | solution.py:50
  148.5 3.2 %shard_map.92.ga_ref = bf16[596,1024]{1,0:T(8,128)(2,1)S(1)} custom-call(s32[3]{0:T(128)S(1)} %pad_add_fusion.scalar_ref, s32[4,256]{1,0:T(4,128)S(1)} %broadcast_select_fusion.1.ids_ref, f32[4,4,256]{2,1,0:T(4,128)S(1)} %get-tuple-element.70.coef_ref, f32[4,600,256]{2,1,0:T(8,128)} %get-tuple-element.65.refs_4_.refs_0_, ...), custom_call_target="tpu_custom_call" | custom-call | flops 6103040 | bytes 6103040 | tf_op jit(solution)/shard_map/pallas_call | solution.py:326
  151.8 15.6 %shard_map.93 = (bf16[596,4096]{1,0:T(8,128)(2,1)}, f32[1,1]{1,0:T(1,128)}) custom-call(f32[1,1]{1,0:T(1,128)} %get-tuple-element.69.kla_ref, f32[1,1]{1,0:T(1,128)} %collective-permute-done.27.klb_ref, bf16[596,1024]{1,0:T(8,128)(2,1)S(1)} %shard_map.92.ga_ref, bf16[596,1024]{1,0:T(8,128)(2,1)S(1)} %collective-permute-done.28.gb_ref, ...), custom_call_target="tpu_custom_call" | custom-call | flops 9999220736 | bytes 16777216 | tf_op jit(solution)/shard_map/pallas_call | solution.py:359
  (86 shorter events, 2.9 us)
Async XLA Ops:
  0.6 2.8 %copy-start = (bf16[128,4096]{1,0:T(8,128)(2,1)S(1)}, bf16[128,4096]{1,0:T(8,128)(2,1)}, u32[]{:S(2)}) copy-start(bf16[128,4096]{1,0:T(8,128)(2,1)} %param.7) | copy-start | bytes 3145732
  0.6 2.8 %copy-start.1 = (bf16[128,4096]{1,0:T(8,128)(2,1)S(1)}, bf16[128,4096]{1,0:T(8,128)(2,1)}, u32[]{:S(2)}) copy-start(bf16[128,4096]{1,0:T(8,128)(2,1)} %param.8) | copy-start | bytes 3145732
  0.6 23.7 %collective-permute-start.4 = (bf16[596,4096]{1,0:T(8,128)(2,1)}, bf16[596,4096]{1,0:T(8,128)(2,1)}, u32[]{:S(2)}, u32[]{:S(2)}) collective-permute-start(bf16[596,4096]{1,0:T(8,128)(2,1)} %bitcast.48), channel_id=1, source_target_pairs={{0,1},{1,0},{2,3},{3,2},{4,5},{5,4},{6,7},{7,6},{8,9},{9,8},{10,11... | collective-permute-start | bytes 14647304 | tf_op jit(solution)/shard_map/ppermute | solution.py:50
  2.2 22.2 %collective-permute-start.5 = (bf16[596,4096]{1,0:T(8,128)(2,1)}, bf16[596,4096]{1,0:T(8,128)(2,1)}, u32[]{:S(2)}, u32[]{:S(2)}) collective-permute-start(bf16[596,4096]{1,0:T(8,128)(2,1)} %bitcast.45), channel_id=1, source_target_pairs={{0,1},{1,0},{2,3},{3,2},{4,5},{5,4},{6,7},{7,6},{8,9},{9,8},{10,11... | collective-permute-start | bytes 14647304 | tf_op jit(solution)/shard_map/ppermute | solution.py:50
  3.5 1.5 copy-start.2
  3.5 12.6 %collective-permute-start = (bf16[2,64,3072]{2,1,0:T(8,128)(2,1)S(1)}, bf16[2,64,3072]{2,1,0:T(8,128)(2,1)S(1)}, u32[]{:S(2)}, u32[]{:S(2)}) collective-permute-start(bf16[2,64,3072]{2,1,0:T(8,128)(2,1)S(1)} %pad_maximum_fusion.4), channel_id=1, source_target_pairs={{0,32},{1,9},{2,34},{3,11},{4,36},{5,13},{6,38},{7,15},{8,40},{9,1... | collective-permute-start | bytes 2359304 | tf_op jit(solution)/shard_map/ppermute | solution.py:50
  5.0 11.2 %collective-permute-start.1 = (bf16[2,64,3072]{2,1,0:T(8,128)(2,1)S(1)}, bf16[2,64,3072]{2,1,0:T(8,128)(2,1)S(1)}, u32[]{:S(2)}, u32[]{:S(2)}) collective-permute-start(bf16[2,64,3072]{2,1,0:T(8,128)(2,1)S(1)} %pad_maximum_fusion.4), channel_id=1, source_target_pairs={{0,96},{1,25},{2,98},{3,27},{4,100},{5,29},{6,102},{7,31},{8,104},... | collective-permute-start | bytes 2359304 | tf_op jit(solution)/shard_map/ppermute | solution.py:50
  16.1 8.4 %copy-start.4 = (bf16[2,64,3072]{2,1,0:T(8,128)(2,1)}, bf16[2,64,3072]{2,1,0:T(8,128)(2,1)S(1)}, u32[]{:S(2)}) copy-start(bf16[2,64,3072]{2,1,0:T(8,128)(2,1)S(1)} %collective-permute-done) | copy-start | bytes 2359300
  16.1 8.2 %collective-permute-start.2 = (bf16[64,3072]{1,0:T(8,128)(2,1)S(1)}, bf16[64,3072]{1,0:T(8,128)(2,1)S(1)}, u32[]{:S(2)}, u32[]{:S(2)}) collective-permute-start(bf16[64,3072]{1,0:T(8,128)(2,1)S(1)} %slice_bitcast_fusion.5), channel_id=1, source_target_pairs={{0,32},{1,9},{2,34},{3,11},{4,36},{5,13},{6,38},{7,15},{8,40},{9,1... | collective-permute-start | bytes 1179656 | tf_op jit(solution)/shard_map/ppermute | solution.py:50
  16.2 8.3 %copy-start.5 = (bf16[2,64,3072]{2,1,0:T(8,128)(2,1)}, bf16[2,64,3072]{2,1,0:T(8,128)(2,1)S(1)}, u32[]{:S(2)}) copy-start(bf16[2,64,3072]{2,1,0:T(8,128)(2,1)S(1)} %collective-permute-done.1) | copy-start | bytes 2359300
  16.3 8.1 %collective-permute-start.3 = (bf16[64,3072]{1,0:T(8,128)(2,1)S(1)}, bf16[64,3072]{1,0:T(8,128)(2,1)S(1)}, u32[]{:S(2)}, u32[]{:S(2)}) collective-permute-start(bf16[64,3072]{1,0:T(8,128)(2,1)S(1)} %slice_bitcast_fusion.4), channel_id=1, source_target_pairs={{0,96},{1,25},{2,98},{3,27},{4,100},{5,29},{6,102},{7,31},{8,104},... | collective-permute-start | bytes 1179656 | tf_op jit(solution)/shard_map/ppermute | solution.py:50
  24.4 6.7 %copy-start.3 = (bf16[2,64,3072]{2,1,0:T(8,128)(2,1)S(1)}, bf16[2,64,3072]{2,1,0:T(8,128)(2,1)}, u32[]{:S(2)}) copy-start(bf16[2,64,3072]{2,1,0:T(8,128)(2,1)} %copy-done.2) | copy-start | bytes 2359300
  24.6 6.6 %slice-start = ((bf16[2,64,3072]{2,1,0:T(8,128)(2,1)}), bf16[2,64,2048]{2,1,0:T(8,128)(2,1)S(1)}, s32[]{:S(2)}) async-start(bf16[2,64,3072]{2,1,0:T(8,128)(2,1)} %copy-done.4), calls=%async_computation | async-start | bytes 1048576 | tf_op jit(solution)/shard_map/slice | solution.py:410
  24.6 6.6 %slice-start.1 = ((bf16[2,64,3072]{2,1,0:T(8,128)(2,1)}), bf16[2,64,2048]{2,1,0:T(8,128)(2,1)S(1)}, s32[]{:S(2)}) async-start(bf16[2,64,3072]{2,1,0:T(8,128)(2,1)} %copy-done.5), calls=%async_computation.1 | async-start | bytes 1048576 | tf_op jit(solution)/shard_map/slice | solution.py:410
  24.6 15.3 %collective-permute-start.6 = (bf16[2,256,1024]{2,1,0:T(8,128)(2,1)S(1)}, bf16[2,256,1024]{2,1,0:T(8,128)(2,1)S(1)}, u32[]{:S(2)}, u32[]{:S(2)}) collective-permute-start(bf16[2,256,1024]{2,1,0:T(8,128)(2,1)S(1)} %pad_maximum_fusion.2.refs_1_), channel_id=1, source_target_pairs={{0,8},{1,33},{2,10},{3,35},{4,12},{5,37},{6,14},{7,39},{8,16},{9,4... | collective-permute-start | bytes 3145736 | tf_op jit(solution)/shard_map/ppermute | solution.py:50
  25.6 14.3 %collective-permute-start.7 = (bf16[2,256,1024]{2,1,0:T(8,128)(2,1)S(1)}, bf16[2,256,1024]{2,1,0:T(8,128)(2,1)S(1)}, u32[]{:S(2)}, u32[]{:S(2)}) collective-permute-start(bf16[2,256,1024]{2,1,0:T(8,128)(2,1)S(1)} %pad_maximum_fusion.2.refs_1_), channel_id=1, source_target_pairs={{0,24},{1,97},{2,26},{3,99},{4,28},{5,101},{6,30},{7,103},{8,0},{9... | collective-permute-start | bytes 3145736 | tf_op jit(solution)/shard_map/ppermute | solution.py:50
  27.4 15.5 %collective-permute-start.8 = (bf16[2,256,1024]{2,1,0:T(8,128)(2,1)S(1)}, bf16[2,256,1024]{2,1,0:T(8,128)(2,1)}, u32[]{:S(2)}, u32[]{:S(2)}) collective-permute-start(bf16[2,256,1024]{2,1,0:T(8,128)(2,1)S(1)} %pad_maximum_fusion.2.refs_1_), channel_id=1, source_target_pairs={{0,2},{1,7},{2,4},{3,1},{4,6},{5,3},{6,0},{7,5},{8,10},{9,15},{10,... | collective-permute-start | bytes 3145736 | tf_op jit(solution)/shard_map/ppermute | solution.py:50
  31.2 3.0 %copy-start.8 = (s32[4]{0:T(128)S(1)}, s32[4]{0:T(128)}, u32[]{:S(2)}) copy-start(s32[4]{0:T(128)} %constant.152.clone) | copy-start | bytes 52
  31.2 3.3 %copy-start.7 = (s32[2048]{0:T(1024)S(1)}, s32[2048]{0:T(1024)}, u32[]{:S(2)}) copy-start(s32[2048]{0:T(1024)} %param.11) | copy-start | bytes 24580
  32.8 35.3 %collective-permute-start.10 = (bf16[2,256,2048]{2,1,0:T(8,128)(2,1)}, bf16[2,256,2048]{2,1,0:T(8,128)(2,1)}, u32[]{:S(2)}, u32[]{:S(2)}) collective-permute-start(bf16[2,256,2048]{2,1,0:T(8,128)(2,1)} %pad_maximum_fusion.refs_0_), channel_id=1, source_target_pairs={{0,24},{1,97},{2,26},{3,99},{4,28},{5,101},{6,30},{7,103},{8,0},{9... | collective-permute-start | bytes 6291464 | tf_op jit(solution)/shard_map/ppermute | solution.py:50
  34.1 34.0 %collective-permute-start.9 = (bf16[2,256,2048]{2,1,0:T(8,128)(2,1)}, bf16[2,256,2048]{2,1,0:T(8,128)(2,1)}, u32[]{:S(2)}, u32[]{:S(2)}) collective-permute-start(bf16[2,256,2048]{2,1,0:T(8,128)(2,1)} %pad_maximum_fusion.refs_0_), channel_id=1, source_target_pairs={{0,8},{1,33},{2,10},{3,35},{4,12},{5,37},{6,14},{7,39},{8,16},{9,4... | collective-permute-start | bytes 6291464 | tf_op jit(solution)/shard_map/ppermute | solution.py:50
  44.4 33.3 %collective-permute-start.13 = (bf16[2,2,256,1024]{3,2,1,0:T(8,128)(2,1)}, bf16[2,2,256,1024]{3,2,1,0:T(8,128)(2,1)}, u32[]{:S(2)}, u32[]{:S(2)}) collective-permute-start(bf16[2,2,256,1024]{3,2,1,0:T(8,128)(2,1)} %pad_maximum_fusion.1), channel_id=1, source_target_pairs={{0,2},{1,7},{2,4},{3,1},{4,6},{5,3},{6,0},{7,5},{8,10},{9,15},{10,... | collective-permute-start | bytes 6291464 | tf_op jit(solution)/shard_map/ppermute | solution.py:50
  48.7 19.3 %collective-permute-start.11 = (bf16[256,1024]{1,0:T(8,128)(2,1)}, bf16[256,1024]{1,0:T(8,128)(2,1)}, u32[]{:S(2)}, u32[]{:S(2)}) collective-permute-start(bf16[256,1024]{1,0:T(8,128)(2,1)} %slice_bitcast_fusion.3), channel_id=1, source_target_pairs={{0,8},{1,33},{2,10},{3,35},{4,12},{5,37},{6,14},{7,39},{8,16},{9,4... | collective-permute-start | bytes 1572872 | tf_op jit(solution)/shard_map/ppermute | solution.py:50
  49.6 18.5 %collective-permute-start.12 = (bf16[256,1024]{1,0:T(8,128)(2,1)}, bf16[256,1024]{1,0:T(8,128)(2,1)}, u32[]{:S(2)}, u32[]{:S(2)}) collective-permute-start(bf16[256,1024]{1,0:T(8,128)(2,1)} %slice_bitcast_fusion.2), channel_id=1, source_target_pairs={{0,24},{1,97},{2,26},{3,99},{4,28},{5,101},{6,30},{7,103},{8,0},{9... | collective-permute-start | bytes 1572872 | tf_op jit(solution)/shard_map/ppermute | solution.py:50
  69.4 25.8 %collective-permute-start.14 = (bf16[256,2048]{1,0:T(8,128)(2,1)S(1)}, bf16[256,2048]{1,0:T(8,128)(2,1)S(1)}, u32[]{:S(2)}, u32[]{:S(2)}) collective-permute-start(bf16[256,2048]{1,0:T(8,128)(2,1)S(1)} %slice_bitcast_fusion.1), channel_id=1, source_target_pairs={{0,8},{1,33},{2,10},{3,35},{4,12},{5,37},{6,14},{7,39},{8,16},{9,4... | collective-permute-start | bytes 3145736 | tf_op jit(solution)/shard_map/ppermute | solution.py:50
  71.7 23.5 %collective-permute-start.15 = (bf16[256,2048]{1,0:T(8,128)(2,1)S(1)}, bf16[256,2048]{1,0:T(8,128)(2,1)S(1)}, u32[]{:S(2)}, u32[]{:S(2)}) collective-permute-start(bf16[256,2048]{1,0:T(8,128)(2,1)S(1)} %slice_bitcast_fusion), channel_id=1, source_target_pairs={{0,24},{1,97},{2,26},{3,99},{4,28},{5,101},{6,30},{7,103},{8,0},{9... | collective-permute-start | bytes 3145736 | tf_op jit(solution)/shard_map/ppermute | solution.py:50
  73.6 21.6 %collective-permute-start.16 = (bf16[256,1024]{1,0:T(8,128)(2,1)}, bf16[256,1024]{1,0:T(8,128)(2,1)S(1)}, u32[]{:S(2)}, u32[]{:S(2)}) collective-permute-start(bf16[256,1024]{1,0:T(8,128)(2,1)} %collective-permute-done.11.refs_5_), channel_id=1, source_target_pairs={{0,2},{1,7},{2,4},{3,1},{4,6},{5,3},{6,0},{7,5},{8,10},{9,15},{10,... | collective-permute-start | bytes 1572872 | tf_op jit(solution)/shard_map/ppermute | solution.py:50
  77.4 17.8 %collective-permute-start.17 = (bf16[256,1024]{1,0:T(8,128)(2,1)}, bf16[256,1024]{1,0:T(8,128)(2,1)S(1)}, u32[]{:S(2)}, u32[]{:S(2)}) collective-permute-start(bf16[256,1024]{1,0:T(8,128)(2,1)} %collective-permute-done.12.refs_6_), channel_id=1, source_target_pairs={{0,2},{1,7},{2,4},{3,1},{4,6},{5,3},{6,0},{7,5},{8,10},{9,15},{10,... | collective-permute-start | bytes 1572872 | tf_op jit(solution)/shard_map/ppermute | solution.py:50
  95.3 21.1 %copy-start.6 = (s32[2048]{0:T(1024)S(1)}, s32[2048]{0:T(1024)}, u32[]{:S(2)}) copy-start(s32[2048]{0:T(1024)} %param.12) | copy-start | bytes 24580
  112.5 39.2 %collective-permute-start.30 = (bf16[512,4096]{1,0:T(8,128)(2,1)}, bf16[512,4096]{1,0:T(8,128)(2,1)}, u32[]{:S(2)}, u32[]{:S(2)}) collective-permute-start(bf16[512,4096]{1,0:T(8,128)(2,1)} %get-tuple-element.73.refs_1_), channel_id=1, source_target_pairs={{0,1},{1,0},{2,3},{3,2},{4,5},{5,4},{6,7},{7,6},{8,9},{9,8},{10,11... | collective-permute-start | bytes 12582920 | tf_op jit(solution)/shard_map/ppermute | solution.py:50
  116.3 35.5 %collective-permute-start.29 = (bf16[512,4096]{1,0:T(8,128)(2,1)}, bf16[512,4096]{1,0:T(8,128)(2,1)}, u32[]{:S(2)}, u32[]{:S(2)}) collective-permute-start(bf16[512,4096]{1,0:T(8,128)(2,1)} %get-tuple-element.72.refs_0_), channel_id=1, source_target_pairs={{0,1},{1,0},{2,3},{3,2},{4,5},{5,4},{6,7},{7,6},{8,9},{9,8},{10,11... | collective-permute-start | bytes 12582920 | tf_op jit(solution)/shard_map/ppermute | solution.py:50
  117.6 5.2 %collective-permute-start.18 = (f32[4,16,64]{2,1,0:T(8,128)S(1)}, f32[4,16,64]{2,1,0:T(8,128)S(1)}, u32[]{:S(2)}, u32[]{:S(2)}) collective-permute-start(f32[4,16,64]{2,1,0:T(8,128)S(1)} %shard_map.88.refs_0_), channel_id=1, source_target_pairs={{0,32},{1,33},{2,34},{3,35},{4,36},{5,37},{6,38},{7,39},{8,40},{9,... | collective-permute-start | bytes 49160 | tf_op jit(solution)/shard_map/ppermute | solution.py:50
  118.1 4.8 %collective-permute-start.19 = (f32[4,16,64]{2,1,0:T(8,128)S(1)}, f32[4,16,64]{2,1,0:T(8,128)S(1)}, u32[]{:S(2)}, u32[]{:S(2)}) collective-permute-start(f32[4,16,64]{2,1,0:T(8,128)S(1)} %shard_map.88.refs_0_), channel_id=1, source_target_pairs={{0,96},{1,97},{2,98},{3,99},{4,100},{5,101},{6,102},{7,103},{8,104... | collective-permute-start | bytes 49160 | tf_op jit(solution)/shard_map/ppermute | solution.py:50
  121.0 4.3 %collective-permute-start.20 = (f32[4,16,64]{2,1,0:T(8,128)S(1)}, f32[4,16,64]{2,1,0:T(8,128)S(1)}, u32[]{:S(2)}, u32[]{:S(2)}) collective-permute-start(f32[4,16,64]{2,1,0:T(8,128)S(1)} %shard_map.88.refs_0_), channel_id=1, source_target_pairs={{0,64},{1,65},{2,66},{3,67},{4,68},{5,69},{6,70},{7,71},{8,72},{9,... | collective-permute-start | bytes 49160 | tf_op jit(solution)/shard_map/ppermute | solution.py:50
  125.4 4.0 %collective-permute-start.21 = (f32[4,16,64]{2,1,0:T(8,128)S(1)}, f32[4,16,64]{2,1,0:T(8,128)S(1)}, u32[]{:S(2)}, u32[]{:S(2)}) collective-permute-start(f32[4,16,64]{2,1,0:T(8,128)S(1)} %shard_map.89.refs_0_), channel_id=1, source_target_pairs={{0,8},{1,9},{2,10},{3,11},{4,12},{5,13},{6,14},{7,15},{8,16},{9,17... | collective-permute-start | bytes 49160 | tf_op jit(solution)/shard_map/ppermute | solution.py:50
  125.5 3.9 %collective-permute-start.22 = (f32[4,16,64]{2,1,0:T(8,128)S(1)}, f32[4,16,64]{2,1,0:T(8,128)S(1)}, u32[]{:S(2)}, u32[]{:S(2)}) collective-permute-start(f32[4,16,64]{2,1,0:T(8,128)S(1)} %shard_map.89.refs_0_), channel_id=1, source_target_pairs={{0,24},{1,25},{2,26},{3,27},{4,28},{5,29},{6,30},{7,31},{8,0},{9,1... | collective-permute-start | bytes 49160 | tf_op jit(solution)/shard_map/ppermute | solution.py:50
  128.1 4.3 %collective-permute-start.23 = (f32[4,16,64]{2,1,0:T(8,128)S(1)}, f32[4,16,64]{2,1,0:T(8,128)S(1)}, u32[]{:S(2)}, u32[]{:S(2)}) collective-permute-start(f32[4,16,64]{2,1,0:T(8,128)S(1)} %shard_map.89.refs_0_), channel_id=1, source_target_pairs={{0,16},{1,17},{2,18},{3,19},{4,20},{5,21},{6,22},{7,23},{8,24},{9,... | collective-permute-start | bytes 49160 | tf_op jit(solution)/shard_map/ppermute | solution.py:50
  132.4 4.0 %collective-permute-start.24 = (f32[4,16,64]{2,1,0:T(8,128)S(1)}, f32[4,16,64]{2,1,0:T(8,128)S(1)}, u32[]{:S(2)}, u32[]{:S(2)}) collective-permute-start(f32[4,16,64]{2,1,0:T(8,128)S(1)} %shard_map.90.refs_0_), channel_id=1, source_target_pairs={{0,2},{1,3},{2,4},{3,5},{4,6},{5,7},{6,0},{7,1},{8,10},{9,11},{10,... | collective-permute-start | bytes 49160 | tf_op jit(solution)/shard_map/ppermute | solution.py:50
  133.8 2.8 %collective-permute-start.25 = (f32[4,16,64]{2,1,0:T(8,128)S(1)}, f32[4,16,64]{2,1,0:T(8,128)S(1)}, u32[]{:S(2)}, u32[]{:S(2)}) collective-permute-start(f32[4,16,64]{2,1,0:T(8,128)S(1)} %shard_map.90.refs_0_), channel_id=1, source_target_pairs={{0,6},{1,7},{2,0},{3,1},{4,2},{5,3},{6,4},{7,5},{8,14},{9,15},{10,... | collective-permute-start | bytes 49160 | tf_op jit(solution)/shard_map/ppermute | solution.py:50
  135.2 4.3 %collective-permute-start.26 = (f32[4,16,64]{2,1,0:T(8,128)S(1)}, f32[4,16,64]{2,1,0:T(8,128)S(1)}, u32[]{:S(2)}, u32[]{:S(2)}) collective-permute-start(f32[4,16,64]{2,1,0:T(8,128)S(1)} %shard_map.90.refs_0_), channel_id=1, source_target_pairs={{0,4},{1,5},{2,6},{3,7},{4,0},{5,1},{6,2},{7,3},{8,12},{9,13},{10,... | collective-permute-start | bytes 49160 | tf_op jit(solution)/shard_map/ppermute | solution.py:50
  143.1 8.7 %collective-permute-start.28 = (bf16[596,1024]{1,0:T(8,128)(2,1)S(1)}, bf16[596,1024]{1,0:T(8,128)(2,1)S(1)}, u32[]{:S(2)}, u32[]{:S(2)}) collective-permute-start(bf16[596,1024]{1,0:T(8,128)(2,1)S(1)} %get-tuple-element.71), channel_id=1, source_target_pairs={{0,1},{1,0},{2,3},{3,2},{4,5},{5,4},{6,7},{7,6},{8,9},{9,8},{10,11... | collective-permute-start | bytes 3661832 | tf_op jit(solution)/shard_map/ppermute | solution.py:50
  148.4 3.3 %collective-permute-start.27 = (f32[1,1]{1,0:T(1,128)}, f32[1,1]{1,0:T(1,128)}, u32[]{:S(2)}, u32[]{:S(2)}) collective-permute-start(f32[1,1]{1,0:T(1,128)} %get-tuple-element.69.kla_ref), channel_id=1, source_target_pairs={{0,1},{1,0},{2,3},{3,2},{4,5},{5,4},{6,7},{7,6},{8,9},{9,8},{10,11... | collective-permute-start | bytes 20 | tf_op jit(solution)/shard_map/ppermute | solution.py:50

commit v5 on v4

--- a/solution.py
+++ b/solution.py
@@ -418,14 +418,14 @@
     on_t, on_s = low_c[0], high_c[1]
     far_ct, far_cs = send(on_t, second(1)), send(on_s, second(-1))
     both_y, on_t, on_s = lax.optimization_barrier((both_y, on_t, on_s))
-    far_yt, far_ys = send(far_xt, z_pair()), send(far_xs, z_pair())
+    far_y = send(jnp.stack([far_xt, far_xs]), z_pair())
     group0, group1, student0 = logits_call(
         scalars, ids[0:2], [((row_c,), (row_x,), (row_y,)), ((low_c,), (low_x,), (both_y,))], heads, (0, 0))
-    far_ct, far_cs, far_yt, far_ys, student0 = lax.optimization_barrier((far_ct, far_cs, far_yt, far_ys, student0))
+    far_ct, far_cs, far_y, student0 = lax.optimization_barrier((far_ct, far_cs, far_y, student0))
     other0 = send(student0, SIBLING)
     group2, group3, student1 = logits_call(
         scalars, ids[2:4],
-        [((high_c,), (high_x,), (both_y,)), ((far_ct, far_cs), (far_xt, far_xs), (far_yt, far_ys))], heads, (1, 0))
+        [((high_c,), (high_x,), (both_y,)), ((far_ct, far_cs), (far_xt, far_xs), (far_y,))], heads, (1, 0))
     groups = [group0, group1, group2, group3]
     others = [other0, send(student1, SIBLING)]
 

time: 168 us -> 167 us (level)
    ppermute x31 -> x30, waiting for transfers between devices: 46.2 us -> 44.6 us  [send(): return lax.ppermute(array, AXES, perm)]
    ppermute x31 -> x30, starting transfers between devices: 49.7 us -> 49.6 us  [send(): return lax.ppermute(array, AXES, perm)]
  transfers between devices with their start and end apart: 31 -> 30, of which waited for: 12 -> 10; matrix products, arithmetic and copies ran while one was open for 7% -> 8% of each run, Pallas kernels for 15% -> 15%
where the time goes in v5:
time: 167 us
  Pallas kernels  57.9 us (35%)
  starting transfers between devices  49.6 us (30%)
  waiting for transfers between devices  44.6 us (27%)
  other arithmetic  7.29 us (4%)
  local copies, waits for them, and re-layouts  5.84 us (3%)
  between operations  1.74 us (1%)
    ppermute x30, starting transfers between devices, send(): return lax.ppermute(array, AXES, perm)  49.6 us
    ppermute x30, waiting for transfers between devices, send(): return lax.ppermute(array, AXES, perm)  44.6 us
    pallas_call x2, Pallas kernels, logits_call(): pl.pallas_call(functools.partial(logits_kernel, shape, places), in_specs=...  34.8 us
    pallas_call x1, Pallas kernels, head_call(): pl.pallas_call(head_kernel, grid=(depth // tile,), in_specs=[one, one, wh...  15.6 us
    pallas_call x1, Pallas kernels, finish_call(): pl.pallas_call(finish_kernel, in_specs=[smem, smem] + [vmem] * (3 + len(p...  3.6 us
  transfers between devices with their start and end apart: 30, of which 10 were waited for; matrix products, arithmetic and copies ran while one was open for 8% of the time, Pallas kernels for 15%

profile of v5, /device:TPU:1, one launch (start us, length us, event | category | flops | bytes accessed | tf_op | source)
XLA Modules:
  0.0 166.9 jit_solution(8136228779205964630)
XLA Ops:
  0.6 1.5 collective-permute-start.4
  2.2 1.1 fusion.1
  3.5 1.4 collective-permute-start
  5.0 2.2 %collective-permute-start.1 = (bf16[2,64,3072]{2,1,0:T(8,128)(2,1)S(1)}, bf16[2,64,3072]{2,1,0:T(8,128)(2,1)S(1)}, u32[]{:S(2)}, u32[]{:S(2)}) collective-permute-start(bf16[2,64,3072]{2,1,0:T(8,128)(2,1)S(1)} %pad_maximum_fusion.5), channel_id=1, source_target_pairs={{0,96},{1,25},{2,98},{3,27},{4,100},{5,29},{6,102},{7,31},{8,104},... | collective-permute-start | bytes 2359304 | tf_op jit(solution)/shard_map/ppermute | solution.py:50
  7.2 8.9 %collective-permute-done = bf16[2,64,3072]{2,1,0:T(8,128)(2,1)S(1)} collective-permute-done((bf16[2,64,3072]{2,1,0:T(8,128)(2,1)S(1)}, bf16[2,64,3072]{2,1,0:T(8,128)(2,1)S(1)}, u32[]{:S(2)}, u32[]{:S(2)}) %collective-permute-start) | collective-permute-done | bytes 786464 | tf_op jit(solution)/shard_map/ppermute | solution.py:50
  16.3 3.4 %collective-permute-start.3 = (bf16[64,3072]{1,0:T(8,128)(2,1)S(1)}, bf16[64,3072]{1,0:T(8,128)(2,1)S(1)}, u32[]{:S(2)}, u32[]{:S(2)}) collective-permute-start(bf16[64,3072]{1,0:T(8,128)(2,1)S(1)} %slice_bitcast_fusion.4), channel_id=1, source_target_pairs={{0,96},{1,25},{2,98},{3,27},{4,100},{5,29},{6,102},{7,31},{8,104},... | collective-permute-start | bytes 1179656 | tf_op jit(solution)/shard_map/ppermute | solution.py:50
  19.7 4.6 %collective-permute-done.2 = bf16[64,3072]{1,0:T(8,128)(2,1)S(1)} collective-permute-done((bf16[64,3072]{1,0:T(8,128)(2,1)S(1)}, bf16[64,3072]{1,0:T(8,128)(2,1)S(1)}, u32[]{:S(2)}, u32[]{:S(2)}) %collective-permute-start.2) | collective-permute-done | bytes 393248 | tf_op jit(solution)/shard_map/ppermute | solution.py:50
  24.6 1.0 collective-permute-start.6
  25.6 1.8 %collective-permute-start.7 = (bf16[2,256,1024]{2,1,0:T(8,128)(2,1)S(1)}, bf16[2,256,1024]{2,1,0:T(8,128)(2,1)S(1)}, u32[]{:S(2)}, u32[]{:S(2)}) collective-permute-start(bf16[2,256,1024]{2,1,0:T(8,128)(2,1)S(1)} %pad_maximum_fusion.2.refs_1_), channel_id=1, source_target_pairs={{0,24},{1,97},{2,26},{3,99},{4,28},{5,101},{6,30},{7,103},{8,0},{9... | collective-permute-start | bytes 3145736 | tf_op jit(solution)/shard_map/ppermute | solution.py:50
  27.4 3.7 %collective-permute-start.8 = (bf16[2,256,1024]{2,1,0:T(8,128)(2,1)S(1)}, bf16[2,256,1024]{2,1,0:T(8,128)(2,1)}, u32[]{:S(2)}, u32[]{:S(2)}) collective-permute-start(bf16[2,256,1024]{2,1,0:T(8,128)(2,1)S(1)} %pad_maximum_fusion.2.refs_1_), channel_id=1, source_target_pairs={{0,2},{1,7},{2,4},{3,1},{4,6},{5,3},{6,0},{7,5},{8,10},{9,15},{10,... | collective-permute-start | bytes 3145736 | tf_op jit(solution)/shard_map/ppermute | solution.py:50
  31.3 1.6 pad_maximum_fusion.refs_0_
  32.8 1.3 collective-permute-start.10
  34.7 5.3 %collective-permute-done.6.refs_4_ = bf16[2,256,1024]{2,1,0:T(8,128)(2,1)S(1)} collective-permute-done((bf16[2,256,1024]{2,1,0:T(8,128)(2,1)S(1)}, bf16[2,256,1024]{2,1,0:T(8,128)(2,1)S(1)}, u32[]{:S(2)}, u32[]{:S(2)}) %collective-permute-start.6) | collective-permute-done | bytes 1048608 | tf_op jit(solution)/shard_map/ppermute | solution.py:50
  40.0 2.9 %collective-permute-done.8.refs_2_ = bf16[2,256,1024]{2,1,0:T(8,128)(2,1)} collective-permute-done((bf16[2,256,1024]{2,1,0:T(8,128)(2,1)S(1)}, bf16[2,256,1024]{2,1,0:T(8,128)(2,1)}, u32[]{:S(2)}, u32[]{:S(2)}) %collective-permute-start.8) | collective-permute-done | bytes 1048608 | tf_op jit(solution)/shard_map/ppermute | solution.py:50
  42.9 1.5 pad_maximum_fusion.1
  44.4 3.5 %collective-permute-start.13 = (bf16[2,2,256,1024]{3,2,1,0:T(8,128)(2,1)}, bf16[2,2,256,1024]{3,2,1,0:T(8,128)(2,1)}, u32[]{:S(2)}, u32[]{:S(2)}) collective-permute-start(bf16[2,2,256,1024]{3,2,1,0:T(8,128)(2,1)} %pad_maximum_fusion.1), channel_id=1, source_target_pairs={{0,2},{1,7},{2,4},{3,1},{4,6},{5,3},{6,0},{7,5},{8,10},{9,15},{10,... | collective-permute-start | bytes 6291464 | tf_op jit(solution)/shard_map/ppermute | solution.py:50
  47.9 0.8 slice_bitcast_fusion.3
  48.7 0.8 slice_bitcast_fusion.2
  49.6 2.7 %collective-permute-start.12 = (bf16[256,1024]{1,0:T(8,128)(2,1)}, bf16[256,1024]{1,0:T(8,128)(2,1)}, u32[]{:S(2)}, u32[]{:S(2)}) collective-permute-start(bf16[256,1024]{1,0:T(8,128)(2,1)} %slice_bitcast_fusion.2), channel_id=1, source_target_pairs={{0,24},{1,97},{2,26},{3,99},{4,28},{5,101},{6,30},{7,103},{8,0},{9... | collective-permute-start | bytes 1572872 | tf_op jit(solution)/shard_map/ppermute | solution.py:50
  52.3 0.6 gather_fusion
  53.1 15.0 %collective-permute-done.11.refs_5_ = bf16[256,1024]{1,0:T(8,128)(2,1)} collective-permute-done((bf16[256,1024]{1,0:T(8,128)(2,1)}, bf16[256,1024]{1,0:T(8,128)(2,1)}, u32[]{:S(2)}, u32[]{:S(2)}) %collective-permute-start.11) | collective-permute-done | bytes 524320 | tf_op jit(solution)/shard_map/ppermute | solution.py:50
  68.1 1.3 pad_maximum_fusion.3
  69.4 3.8 %collective-permute-start.16 = (bf16[2,256,1024]{2,1,0:T(8,128)(2,1)S(1)}, bf16[2,256,1024]{2,1,0:T(8,128)(2,1)S(1)}, u32[]{:S(2)}, u32[]{:S(2)}) collective-permute-start(bf16[2,256,1024]{2,1,0:T(8,128)(2,1)S(1)} %pad_maximum_fusion.3), channel_id=1, source_target_pairs={{0,2},{1,7},{2,4},{3,1},{4,6},{5,3},{6,0},{7,5},{8,10},{9,15},{10,... | collective-permute-start | bytes 3145736 | tf_op jit(solution)/shard_map/ppermute | solution.py:50
  73.2 1.3 slice_bitcast_fusion.1
  74.5 1.0 collective-permute-start.14
  75.5 1.3 slice_bitcast_fusion
  76.8 2.0 %collective-permute-start.15 = (bf16[256,2048]{1,0:T(8,128)(2,1)S(1)}, bf16[256,2048]{1,0:T(8,128)(2,1)S(1)}, u32[]{:S(2)}, u32[]{:S(2)}) collective-permute-start(bf16[256,2048]{1,0:T(8,128)(2,1)S(1)} %slice_bitcast_fusion), channel_id=1, source_target_pairs={{0,24},{1,97},{2,26},{3,99},{4,28},{5,101},{6,30},{7,103},{8,0},{9... | collective-permute-start | bytes 3145736 | tf_op jit(solution)/shard_map/ppermute | solution.py:50
  78.9 17.6 %shard_map.86 = (f32[4,600,256]{2,1,0:T(8,128)}, f32[4,4,64]{2,1,0:T(4,128)S(1)}, f32[4,600,256]{2,1,0:T(8,128)}, f32[4,4,64]{2,1,0:T(4,128)S(1)}, bf16[512,4096]{1,0:T(8,128)(2,1)}) custom-call(s32[3]{0:T(128)S(1)} %pad_add_fusion.scalar_ref, s32[2,256]{1,0:T(2,128)S(1)} %slice.55.ids_ref, bf16[2,256,2048]{2,1,0:T(8,128)(2,1)} %pad_maximum_fusion.refs_0_, ...), custom_call_target="tpu_custom_call" | custom-call | flops 9999220736 | bytes 19529728 | tf_op jit(solution)/shard_map/pallas_call | solution.py:192
  96.5 17.3 %shard_map.87 = (f32[4,600,256]{2,1,0:T(8,128)}, f32[4,4,64]{2,1,0:T(4,128)S(1)}, f32[4,600,256]{2,1,0:T(8,128)}, f32[4,4,64]{2,1,0:T(4,128)S(1)}, bf16[512,4096]{1,0:T(8,128)(2,1)}) custom-call(s32[3]{0:T(128)S(1)} %pad_add_fusion.scalar_ref, s32[2,256]{1,0:T(2,128)S(1)} %slice.71.ids_ref, bf16[2,256,2048]{2,1,0:T(8,128)(2,1)} %collective-permute-done.10.refs_0_, ...), custom_call_target="tpu_custom_call" | custom-call | flops 9999220736 | bytes 19529728 | tf_op jit(solution)/shard_map/pallas_call | solution.py:192
  113.8 2.1 %collective-permute-start.29 = (bf16[512,4096]{1,0:T(8,128)(2,1)}, bf16[512,4096]{1,0:T(8,128)(2,1)}, u32[]{:S(2)}, u32[]{:S(2)}) collective-permute-start(bf16[512,4096]{1,0:T(8,128)(2,1)} %get-tuple-element.71.refs_1_), channel_id=1, source_target_pairs={{0,1},{1,0},{2,3},{3,2},{4,5},{5,4},{6,7},{7,6},{8,9},{9,8},{10,11... | collective-permute-start | bytes 12582920 | tf_op jit(solution)/shard_map/ppermute | solution.py:50
  116.1 0.6 convert_reduce_fusion
  116.7 0.6 shard_map.88.refs_0_
  117.2 0.4 collective-permute-start.17
  117.7 3.0 %collective-permute-start.18 = (f32[4,16,64]{2,1,0:T(8,128)S(1)}, f32[4,16,64]{2,1,0:T(8,128)S(1)}, u32[]{:S(2)}, u32[]{:S(2)}) collective-permute-start(f32[4,16,64]{2,1,0:T(8,128)S(1)} %shard_map.88.refs_0_), channel_id=1, source_target_pairs={{0,96},{1,97},{2,98},{3,99},{4,100},{5,101},{6,102},{7,103},{8,104... | collective-permute-start | bytes 49160 | tf_op jit(solution)/shard_map/ppermute | solution.py:50
  120.7 1.1 collective-permute-start.19
  122.5 2.4 %collective-permute-done.19.refs_3_ = f32[4,16,64]{2,1,0:T(8,128)S(1)} collective-permute-done((f32[4,16,64]{2,1,0:T(8,128)S(1)}, f32[4,16,64]{2,1,0:T(8,128)S(1)}, u32[]{:S(2)}, u32[]{:S(2)}) %collective-permute-start.19) | collective-permute-done | bytes 16416 | tf_op jit(solution)/shard_map/ppermute | solution.py:50
  125.1 2.6 %collective-permute-start.21 = (f32[4,16,64]{2,1,0:T(8,128)S(1)}, f32[4,16,64]{2,1,0:T(8,128)S(1)}, u32[]{:S(2)}, u32[]{:S(2)}) collective-permute-start(f32[4,16,64]{2,1,0:T(8,128)S(1)} %shard_map.89.refs_0_), channel_id=1, source_target_pairs={{0,24},{1,25},{2,26},{3,27},{4,28},{5,29},{6,30},{7,31},{8,0},{9,1... | collective-permute-start | bytes 49160 | tf_op jit(solution)/shard_map/ppermute | solution.py:50
  127.9 0.6 divide_bitcast_fusion
  128.8 0.2 collective-permute-done.20.refs_1_
  129.0 3.0 %collective-permute-done.22.refs_3_ = f32[4,16,64]{2,1,0:T(8,128)S(1)} collective-permute-done((f32[4,16,64]{2,1,0:T(8,128)S(1)}, f32[4,16,64]{2,1,0:T(8,128)S(1)}, u32[]{:S(2)}, u32[]{:S(2)}) %collective-permute-start.22) | collective-permute-done | bytes 16416 | tf_op jit(solution)/shard_map/ppermute | solution.py:50
  132.0 1.7 %collective-permute-start.23 = (f32[4,16,64]{2,1,0:T(8,128)S(1)}, f32[4,16,64]{2,1,0:T(8,128)S(1)}, u32[]{:S(2)}, u32[]{:S(2)}) collective-permute-start(f32[4,16,64]{2,1,0:T(8,128)S(1)} %shard_map.90.refs_0_), channel_id=1, source_target_pairs={{0,2},{1,3},{2,4},{3,5},{4,6},{5,7},{6,0},{7,1},{8,10},{9,11},{10,... | collective-permute-start | bytes 49160 | tf_op jit(solution)/shard_map/ppermute | solution.py:50
  133.8 1.0 collective-permute-start.24
  134.8 2.1 %collective-permute-start.25 = (f32[4,16,64]{2,1,0:T(8,128)S(1)}, f32[4,16,64]{2,1,0:T(8,128)S(1)}, u32[]{:S(2)}, u32[]{:S(2)}) collective-permute-start(f32[4,16,64]{2,1,0:T(8,128)S(1)} %shard_map.90.refs_0_), channel_id=1, source_target_pairs={{0,4},{1,5},{2,6},{3,7},{4,0},{5,1},{6,2},{7,3},{8,12},{9,13},{10,... | collective-permute-start | bytes 49160 | tf_op jit(solution)/shard_map/ppermute | solution.py:50
  136.9 2.2 %collective-permute-done.25.refs_3_ = f32[4,16,64]{2,1,0:T(8,128)S(1)} collective-permute-done((f32[4,16,64]{2,1,0:T(8,128)S(1)}, f32[4,16,64]{2,1,0:T(8,128)S(1)}, u32[]{:S(2)}, u32[]{:S(2)}) %collective-permute-start.25) | collective-permute-done | bytes 16416 | tf_op jit(solution)/shard_map/ppermute | solution.py:50
  139.1 3.6 %shard_map.91 = (f32[4,4,256]{2,1,0:T(4,128)S(1)}, f32[1,1]{1,0:T(1,128)}, bf16[596,1024]{1,0:T(8,128)(2,1)S(1)}) custom-call(s32[16]{0:T(128)S(1)} %select_n.134.place_ref, s32[3]{0:T(128)S(1)} %pad_add_fusion.scalar_ref, f32[16,64]{1,0:T(8,128)S(1)} %get-tuple-element.83.factor_ref, f32[16,64]{1,0:T(8,128)S(1)} %get-tuple-element.82.weight_ref, ...), custom_call_target="tpu_custom_call" | custom-call | tf_op jit(solution)/shard_map/pallas_call | solution.py:293
  142.7 5.3 %collective-permute-start.27 = (bf16[596,1024]{1,0:T(8,128)(2,1)S(1)}, bf16[596,1024]{1,0:T(8,128)(2,1)S(1)}, u32[]{:S(2)}, u32[]{:S(2)}) collective-permute-start(bf16[596,1024]{1,0:T(8,128)(2,1)S(1)} %get-tuple-element.69), channel_id=1, source_target_pairs={{0,1},{1,0},{2,3},{3,2},{4,5},{5,4},{6,7},{7,6},{8,9},{9,8},{10,11... | collective-permute-start | bytes 3661832 | tf_op jit(solution)/shard_map/ppermute | solution.py:50
  148.1 3.2 %shard_map.92.ga_ref = bf16[596,1024]{1,0:T(8,128)(2,1)S(1)} custom-call(s32[3]{0:T(128)S(1)} %pad_add_fusion.scalar_ref, s32[4,256]{1,0:T(4,128)S(1)} %broadcast_select_fusion.1.ids_ref, f32[4,4,256]{2,1,0:T(4,128)S(1)} %get-tuple-element.68.coef_ref, f32[4,600,256]{2,1,0:T(8,128)} %get-tuple-element.63.refs_4_.refs_0_, ...), custom_call_target="tpu_custom_call" | custom-call | flops 6103040 | bytes 6103040 | tf_op jit(solution)/shard_map/pallas_call | solution.py:326
  151.3 15.6 %shard_map.93 = (bf16[596,4096]{1,0:T(8,128)(2,1)}, f32[1,1]{1,0:T(1,128)}) custom-call(f32[1,1]{1,0:T(1,128)} %get-tuple-element.67.kla_ref, f32[1,1]{1,0:T(1,128)} %collective-permute-done.26.klb_ref, bf16[596,1024]{1,0:T(8,128)(2,1)S(1)} %shard_map.92.ga_ref, bf16[596,1024]{1,0:T(8,128)(2,1)S(1)} %collective-permute-done.27.gb_ref, ...), custom_call_target="tpu_custom_call" | custom-call | flops 9999220736 | bytes 16777216 | tf_op jit(solution)/shard_map/pallas_call | solution.py:359
  (85 shorter events, 2.6 us)
Async XLA Ops:
  0.6 2.8 %copy-start = (bf16[128,4096]{1,0:T(8,128)(2,1)S(1)}, bf16[128,4096]{1,0:T(8,128)(2,1)}, u32[]{:S(2)}) copy-start(bf16[128,4096]{1,0:T(8,128)(2,1)} %param.7) | copy-start | bytes 3145732
  0.6 2.8 %copy-start.1 = (bf16[128,4096]{1,0:T(8,128)(2,1)S(1)}, bf16[128,4096]{1,0:T(8,128)(2,1)}, u32[]{:S(2)}) copy-start(bf16[128,4096]{1,0:T(8,128)(2,1)} %param.8) | copy-start | bytes 3145732
  0.6 23.8 %collective-permute-start.4 = (bf16[596,4096]{1,0:T(8,128)(2,1)}, bf16[596,4096]{1,0:T(8,128)(2,1)}, u32[]{:S(2)}, u32[]{:S(2)}) collective-permute-start(bf16[596,4096]{1,0:T(8,128)(2,1)} %bitcast.50), channel_id=1, source_target_pairs={{0,1},{1,0},{2,3},{3,2},{4,5},{5,4},{6,7},{7,6},{8,9},{9,8},{10,11... | collective-permute-start | bytes 14647304 | tf_op jit(solution)/shard_map/ppermute | solution.py:50
  2.2 22.3 %collective-permute-start.5 = (bf16[596,4096]{1,0:T(8,128)(2,1)}, bf16[596,4096]{1,0:T(8,128)(2,1)}, u32[]{:S(2)}, u32[]{:S(2)}) collective-permute-start(bf16[596,4096]{1,0:T(8,128)(2,1)} %bitcast.47), channel_id=1, source_target_pairs={{0,1},{1,0},{2,3},{3,2},{4,5},{5,4},{6,7},{7,6},{8,9},{9,8},{10,11... | collective-permute-start | bytes 14647304 | tf_op jit(solution)/shard_map/ppermute | solution.py:50
  3.5 1.5 copy-start.2
  3.5 12.6 %collective-permute-start = (bf16[2,64,3072]{2,1,0:T(8,128)(2,1)S(1)}, bf16[2,64,3072]{2,1,0:T(8,128)(2,1)S(1)}, u32[]{:S(2)}, u32[]{:S(2)}) collective-permute-start(bf16[2,64,3072]{2,1,0:T(8,128)(2,1)S(1)} %pad_maximum_fusion.5), channel_id=1, source_target_pairs={{0,32},{1,9},{2,34},{3,11},{4,36},{5,13},{6,38},{7,15},{8,40},{9,1... | collective-permute-start | bytes 2359304 | tf_op jit(solution)/shard_map/ppermute | solution.py:50
  5.0 11.2 %collective-permute-start.1 = (bf16[2,64,3072]{2,1,0:T(8,128)(2,1)S(1)}, bf16[2,64,3072]{2,1,0:T(8,128)(2,1)S(1)}, u32[]{:S(2)}, u32[]{:S(2)}) collective-permute-start(bf16[2,64,3072]{2,1,0:T(8,128)(2,1)S(1)} %pad_maximum_fusion.5), channel_id=1, source_target_pairs={{0,96},{1,25},{2,98},{3,27},{4,100},{5,29},{6,102},{7,31},{8,104},... | collective-permute-start | bytes 2359304 | tf_op jit(solution)/shard_map/ppermute | solution.py:50
  16.1 8.4 %copy-start.4 = (bf16[2,64,3072]{2,1,0:T(8,128)(2,1)}, bf16[2,64,3072]{2,1,0:T(8,128)(2,1)S(1)}, u32[]{:S(2)}) copy-start(bf16[2,64,3072]{2,1,0:T(8,128)(2,1)S(1)} %collective-permute-done) | copy-start | bytes 2359300
  16.1 8.2 %collective-permute-start.2 = (bf16[64,3072]{1,0:T(8,128)(2,1)S(1)}, bf16[64,3072]{1,0:T(8,128)(2,1)S(1)}, u32[]{:S(2)}, u32[]{:S(2)}) collective-permute-start(bf16[64,3072]{1,0:T(8,128)(2,1)S(1)} %slice_bitcast_fusion.5), channel_id=1, source_target_pairs={{0,32},{1,9},{2,34},{3,11},{4,36},{5,13},{6,38},{7,15},{8,40},{9,1... | collective-permute-start | bytes 1179656 | tf_op jit(solution)/shard_map/ppermute | solution.py:50
  16.2 8.3 %copy-start.5 = (bf16[2,64,3072]{2,1,0:T(8,128)(2,1)}, bf16[2,64,3072]{2,1,0:T(8,128)(2,1)S(1)}, u32[]{:S(2)}) copy-start(bf16[2,64,3072]{2,1,0:T(8,128)(2,1)S(1)} %collective-permute-done.1) | copy-start | bytes 2359300
  16.3 8.1 %collective-permute-start.3 = (bf16[64,3072]{1,0:T(8,128)(2,1)S(1)}, bf16[64,3072]{1,0:T(8,128)(2,1)S(1)}, u32[]{:S(2)}, u32[]{:S(2)}) collective-permute-start(bf16[64,3072]{1,0:T(8,128)(2,1)S(1)} %slice_bitcast_fusion.4), channel_id=1, source_target_pairs={{0,96},{1,25},{2,98},{3,27},{4,100},{5,29},{6,102},{7,31},{8,104},... | collective-permute-start | bytes 1179656 | tf_op jit(solution)/shard_map/ppermute | solution.py:50
  24.4 6.7 %copy-start.3 = (bf16[2,64,3072]{2,1,0:T(8,128)(2,1)S(1)}, bf16[2,64,3072]{2,1,0:T(8,128)(2,1)}, u32[]{:S(2)}) copy-start(bf16[2,64,3072]{2,1,0:T(8,128)(2,1)} %copy-done.2) | copy-start | bytes 2359300
  24.6 6.6 %slice-start = ((bf16[2,64,3072]{2,1,0:T(8,128)(2,1)}), bf16[2,64,2048]{2,1,0:T(8,128)(2,1)S(1)}, s32[]{:S(2)}) async-start(bf16[2,64,3072]{2,1,0:T(8,128)(2,1)} %copy-done.4), calls=%async_computation | async-start | bytes 1048576 | tf_op jit(solution)/shard_map/slice | solution.py:410
  24.6 6.6 %slice-start.1 = ((bf16[2,64,3072]{2,1,0:T(8,128)(2,1)}), bf16[2,64,2048]{2,1,0:T(8,128)(2,1)S(1)}, s32[]{:S(2)}) async-start(bf16[2,64,3072]{2,1,0:T(8,128)(2,1)} %copy-done.5), calls=%async_computation.1 | async-start | bytes 1048576 | tf_op jit(solution)/shard_map/slice | solution.py:410
  24.6 15.3 %collective-permute-start.6 = (bf16[2,256,1024]{2,1,0:T(8,128)(2,1)S(1)}, bf16[2,256,1024]{2,1,0:T(8,128)(2,1)S(1)}, u32[]{:S(2)}, u32[]{:S(2)}) collective-permute-start(bf16[2,256,1024]{2,1,0:T(8,128)(2,1)S(1)} %pad_maximum_fusion.2.refs_1_), channel_id=1, source_target_pairs={{0,8},{1,33},{2,10},{3,35},{4,12},{5,37},{6,14},{7,39},{8,16},{9,4... | collective-permute-start | bytes 3145736 | tf_op jit(solution)/shard_map/ppermute | solution.py:50
  25.6 14.3 %collective-permute-start.7 = (bf16[2,256,1024]{2,1,0:T(8,128)(2,1)S(1)}, bf16[2,256,1024]{2,1,0:T(8,128)(2,1)S(1)}, u32[]{:S(2)}, u32[]{:S(2)}) collective-permute-start(bf16[2,256,1024]{2,1,0:T(8,128)(2,1)S(1)} %pad_maximum_fusion.2.refs_1_), channel_id=1, source_target_pairs={{0,24},{1,97},{2,26},{3,99},{4,28},{5,101},{6,30},{7,103},{8,0},{9... | collective-permute-start | bytes 3145736 | tf_op jit(solution)/shard_map/ppermute | solution.py:50
  27.4 15.5 %collective-permute-start.8 = (bf16[2,256,1024]{2,1,0:T(8,128)(2,1)S(1)}, bf16[2,256,1024]{2,1,0:T(8,128)(2,1)}, u32[]{:S(2)}, u32[]{:S(2)}) collective-permute-start(bf16[2,256,1024]{2,1,0:T(8,128)(2,1)S(1)} %pad_maximum_fusion.2.refs_1_), channel_id=1, source_target_pairs={{0,2},{1,7},{2,4},{3,1},{4,6},{5,3},{6,0},{7,5},{8,10},{9,15},{10,... | collective-permute-start | bytes 3145736 | tf_op jit(solution)/shard_map/ppermute | solution.py:50
  31.2 3.1 %copy-start.8 = (s32[4]{0:T(128)S(1)}, s32[4]{0:T(128)}, u32[]{:S(2)}) copy-start(s32[4]{0:T(128)} %constant.152.clone) | copy-start | bytes 52
  31.3 3.3 %copy-start.7 = (s32[2048]{0:T(1024)S(1)}, s32[2048]{0:T(1024)}, u32[]{:S(2)}) copy-start(s32[2048]{0:T(1024)} %param.11) | copy-start | bytes 24580
  32.8 35.2 %collective-permute-start.10 = (bf16[2,256,2048]{2,1,0:T(8,128)(2,1)}, bf16[2,256,2048]{2,1,0:T(8,128)(2,1)}, u32[]{:S(2)}, u32[]{:S(2)}) collective-permute-start(bf16[2,256,2048]{2,1,0:T(8,128)(2,1)} %pad_maximum_fusion.refs_0_), channel_id=1, source_target_pairs={{0,24},{1,97},{2,26},{3,99},{4,28},{5,101},{6,30},{7,103},{8,0},{9... | collective-permute-start | bytes 6291464 | tf_op jit(solution)/shard_map/ppermute | solution.py:50
  34.1 34.0 %collective-permute-start.9 = (bf16[2,256,2048]{2,1,0:T(8,128)(2,1)}, bf16[2,256,2048]{2,1,0:T(8,128)(2,1)}, u32[]{:S(2)}, u32[]{:S(2)}) collective-permute-start(bf16[2,256,2048]{2,1,0:T(8,128)(2,1)} %pad_maximum_fusion.refs_0_), channel_id=1, source_target_pairs={{0,8},{1,33},{2,10},{3,35},{4,12},{5,37},{6,14},{7,39},{8,16},{9,4... | collective-permute-start | bytes 6291464 | tf_op jit(solution)/shard_map/ppermute | solution.py:50
  44.4 34.6 %collective-permute-start.13 = (bf16[2,2,256,1024]{3,2,1,0:T(8,128)(2,1)}, bf16[2,2,256,1024]{3,2,1,0:T(8,128)(2,1)}, u32[]{:S(2)}, u32[]{:S(2)}) collective-permute-start(bf16[2,2,256,1024]{3,2,1,0:T(8,128)(2,1)} %pad_maximum_fusion.1), channel_id=1, source_target_pairs={{0,2},{1,7},{2,4},{3,1},{4,6},{5,3},{6,0},{7,5},{8,10},{9,15},{10,... | collective-permute-start | bytes 6291464 | tf_op jit(solution)/shard_map/ppermute | solution.py:50
  48.7 19.3 %collective-permute-start.11 = (bf16[256,1024]{1,0:T(8,128)(2,1)}, bf16[256,1024]{1,0:T(8,128)(2,1)}, u32[]{:S(2)}, u32[]{:S(2)}) collective-permute-start(bf16[256,1024]{1,0:T(8,128)(2,1)} %slice_bitcast_fusion.3), channel_id=1, source_target_pairs={{0,8},{1,33},{2,10},{3,35},{4,12},{5,37},{6,14},{7,39},{8,16},{9,4... | collective-permute-start | bytes 1572872 | tf_op jit(solution)/shard_map/ppermute | solution.py:50
  49.6 18.5 %collective-permute-start.12 = (bf16[256,1024]{1,0:T(8,128)(2,1)}, bf16[256,1024]{1,0:T(8,128)(2,1)}, u32[]{:S(2)}, u32[]{:S(2)}) collective-permute-start(bf16[256,1024]{1,0:T(8,128)(2,1)} %slice_bitcast_fusion.2), channel_id=1, source_target_pairs={{0,24},{1,97},{2,26},{3,99},{4,28},{5,101},{6,30},{7,103},{8,0},{9... | collective-permute-start | bytes 1572872 | tf_op jit(solution)/shard_map/ppermute | solution.py:50
  69.4 27.1 %collective-permute-start.16 = (bf16[2,256,1024]{2,1,0:T(8,128)(2,1)S(1)}, bf16[2,256,1024]{2,1,0:T(8,128)(2,1)S(1)}, u32[]{:S(2)}, u32[]{:S(2)}) collective-permute-start(bf16[2,256,1024]{2,1,0:T(8,128)(2,1)S(1)} %pad_maximum_fusion.3), channel_id=1, source_target_pairs={{0,2},{1,7},{2,4},{3,1},{4,6},{5,3},{6,0},{7,5},{8,10},{9,15},{10,... | collective-permute-start | bytes 3145736 | tf_op jit(solution)/shard_map/ppermute | solution.py:50
  74.5 22.0 %collective-permute-start.14 = (bf16[256,2048]{1,0:T(8,128)(2,1)S(1)}, bf16[256,2048]{1,0:T(8,128)(2,1)S(1)}, u32[]{:S(2)}, u32[]{:S(2)}) collective-permute-start(bf16[256,2048]{1,0:T(8,128)(2,1)S(1)} %slice_bitcast_fusion.1), channel_id=1, source_target_pairs={{0,8},{1,33},{2,10},{3,35},{4,12},{5,37},{6,14},{7,39},{8,16},{9,4... | collective-permute-start | bytes 3145736 | tf_op jit(solution)/shard_map/ppermute | solution.py:50
  76.8 19.7 %collective-permute-start.15 = (bf16[256,2048]{1,0:T(8,128)(2,1)S(1)}, bf16[256,2048]{1,0:T(8,128)(2,1)S(1)}, u32[]{:S(2)}, u32[]{:S(2)}) collective-permute-start(bf16[256,2048]{1,0:T(8,128)(2,1)S(1)} %slice_bitcast_fusion), channel_id=1, source_target_pairs={{0,24},{1,97},{2,26},{3,99},{4,28},{5,101},{6,30},{7,103},{8,0},{9... | collective-permute-start | bytes 3145736 | tf_op jit(solution)/shard_map/ppermute | solution.py:50
  96.5 19.4 %copy-start.6 = (s32[2048]{0:T(1024)S(1)}, s32[2048]{0:T(1024)}, u32[]{:S(2)}) copy-start(s32[2048]{0:T(1024)} %param.12) | copy-start | bytes 24580
  113.8 37.5 %collective-permute-start.29 = (bf16[512,4096]{1,0:T(8,128)(2,1)}, bf16[512,4096]{1,0:T(8,128)(2,1)}, u32[]{:S(2)}, u32[]{:S(2)}) collective-permute-start(bf16[512,4096]{1,0:T(8,128)(2,1)} %get-tuple-element.71.refs_1_), channel_id=1, source_target_pairs={{0,1},{1,0},{2,3},{3,2},{4,5},{5,4},{6,7},{7,6},{8,9},{9,8},{10,11... | collective-permute-start | bytes 12582920 | tf_op jit(solution)/shard_map/ppermute | solution.py:50
  115.9 35.5 %collective-permute-start.28 = (bf16[512,4096]{1,0:T(8,128)(2,1)}, bf16[512,4096]{1,0:T(8,128)(2,1)}, u32[]{:S(2)}, u32[]{:S(2)}) collective-permute-start(bf16[512,4096]{1,0:T(8,128)(2,1)} %get-tuple-element.70.refs_0_), channel_id=1, source_target_pairs={{0,1},{1,0},{2,3},{3,2},{4,5},{5,4},{6,7},{7,6},{8,9},{9,8},{10,11... | collective-permute-start | bytes 12582920 | tf_op jit(solution)/shard_map/ppermute | solution.py:50
  117.2 5.2 %collective-permute-start.17 = (f32[4,16,64]{2,1,0:T(8,128)S(1)}, f32[4,16,64]{2,1,0:T(8,128)S(1)}, u32[]{:S(2)}, u32[]{:S(2)}) collective-permute-start(f32[4,16,64]{2,1,0:T(8,128)S(1)} %shard_map.88.refs_0_), channel_id=1, source_target_pairs={{0,32},{1,33},{2,34},{3,35},{4,36},{5,37},{6,38},{7,39},{8,40},{9,... | collective-permute-start | bytes 49160 | tf_op jit(solution)/shard_map/ppermute | solution.py:50
  117.7 4.8 %collective-permute-start.18 = (f32[4,16,64]{2,1,0:T(8,128)S(1)}, f32[4,16,64]{2,1,0:T(8,128)S(1)}, u32[]{:S(2)}, u32[]{:S(2)}) collective-permute-start(f32[4,16,64]{2,1,0:T(8,128)S(1)} %shard_map.88.refs_0_), channel_id=1, source_target_pairs={{0,96},{1,97},{2,98},{3,99},{4,100},{5,101},{6,102},{7,103},{8,104... | collective-permute-start | bytes 49160 | tf_op jit(solution)/shard_map/ppermute | solution.py:50
  120.7 4.3 %collective-permute-start.19 = (f32[4,16,64]{2,1,0:T(8,128)S(1)}, f32[4,16,64]{2,1,0:T(8,128)S(1)}, u32[]{:S(2)}, u32[]{:S(2)}) collective-permute-start(f32[4,16,64]{2,1,0:T(8,128)S(1)} %shard_map.88.refs_0_), channel_id=1, source_target_pairs={{0,64},{1,65},{2,66},{3,67},{4,68},{5,69},{6,70},{7,71},{8,72},{9,... | collective-permute-start | bytes 49160 | tf_op jit(solution)/shard_map/ppermute | solution.py:50
  125.0 4.0 %collective-permute-start.20 = (f32[4,16,64]{2,1,0:T(8,128)S(1)}, f32[4,16,64]{2,1,0:T(8,128)S(1)}, u32[]{:S(2)}, u32[]{:S(2)}) collective-permute-start(f32[4,16,64]{2,1,0:T(8,128)S(1)} %shard_map.89.refs_0_), channel_id=1, source_target_pairs={{0,8},{1,9},{2,10},{3,11},{4,12},{5,13},{6,14},{7,15},{8,16},{9,17... | collective-permute-start | bytes 49160 | tf_op jit(solution)/shard_map/ppermute | solution.py:50
  125.1 3.9 %collective-permute-start.21 = (f32[4,16,64]{2,1,0:T(8,128)S(1)}, f32[4,16,64]{2,1,0:T(8,128)S(1)}, u32[]{:S(2)}, u32[]{:S(2)}) collective-permute-start(f32[4,16,64]{2,1,0:T(8,128)S(1)} %shard_map.89.refs_0_), channel_id=1, source_target_pairs={{0,24},{1,25},{2,26},{3,27},{4,28},{5,29},{6,30},{7,31},{8,0},{9,1... | collective-permute-start | bytes 49160 | tf_op jit(solution)/shard_map/ppermute | solution.py:50
  127.7 4.3 %collective-permute-start.22 = (f32[4,16,64]{2,1,0:T(8,128)S(1)}, f32[4,16,64]{2,1,0:T(8,128)S(1)}, u32[]{:S(2)}, u32[]{:S(2)}) collective-permute-start(f32[4,16,64]{2,1,0:T(8,128)S(1)} %shard_map.89.refs_0_), channel_id=1, source_target_pairs={{0,16},{1,17},{2,18},{3,19},{4,20},{5,21},{6,22},{7,23},{8,24},{9,... | collective-permute-start | bytes 49160 | tf_op jit(solution)/shard_map/ppermute | solution.py:50
  132.0 4.9 %collective-permute-start.23 = (f32[4,16,64]{2,1,0:T(8,128)S(1)}, f32[4,16,64]{2,1,0:T(8,128)S(1)}, u32[]{:S(2)}, u32[]{:S(2)}) collective-permute-start(f32[4,16,64]{2,1,0:T(8,128)S(1)} %shard_map.90.refs_0_), channel_id=1, source_target_pairs={{0,2},{1,3},{2,4},{3,5},{4,6},{5,7},{6,0},{7,1},{8,10},{9,11},{10,... | collective-permute-start | bytes 49160 | tf_op jit(solution)/shard_map/ppermute | solution.py:50
  133.8 3.1 %collective-permute-start.24 = (f32[4,16,64]{2,1,0:T(8,128)S(1)}, f32[4,16,64]{2,1,0:T(8,128)S(1)}, u32[]{:S(2)}, u32[]{:S(2)}) collective-permute-start(f32[4,16,64]{2,1,0:T(8,128)S(1)} %shard_map.90.refs_0_), channel_id=1, source_target_pairs={{0,6},{1,7},{2,0},{3,1},{4,2},{5,3},{6,4},{7,5},{8,14},{9,15},{10,... | collective-permute-start | bytes 49160 | tf_op jit(solution)/shard_map/ppermute | solution.py:50
  134.8 4.3 %collective-permute-start.25 = (f32[4,16,64]{2,1,0:T(8,128)S(1)}, f32[4,16,64]{2,1,0:T(8,128)S(1)}, u32[]{:S(2)}, u32[]{:S(2)}) collective-permute-start(f32[4,16,64]{2,1,0:T(8,128)S(1)} %shard_map.90.refs_0_), channel_id=1, source_target_pairs={{0,4},{1,5},{2,6},{3,7},{4,0},{5,1},{6,2},{7,3},{8,12},{9,13},{10,... | collective-permute-start | bytes 49160 | tf_op jit(solution)/shard_map/ppermute | solution.py:50
  142.7 8.7 %collective-permute-start.27 = (bf16[596,1024]{1,0:T(8,128)(2,1)S(1)}, bf16[596,1024]{1,0:T(8,128)(2,1)S(1)}, u32[]{:S(2)}, u32[]{:S(2)}) collective-permute-start(bf16[596,1024]{1,0:T(8,128)(2,1)S(1)} %get-tuple-element.69), channel_id=1, source_target_pairs={{0,1},{1,0},{2,3},{3,2},{4,5},{5,4},{6,7},{7,6},{8,9},{9,8},{10,11... | collective-permute-start | bytes 3661832 | tf_op jit(solution)/shard_map/ppermute | solution.py:50
  148.0 3.3 %collective-permute-start.26 = (f32[1,1]{1,0:T(1,128)}, f32[1,1]{1,0:T(1,128)}, u32[]{:S(2)}, u32[]{:S(2)}) collective-permute-start(f32[1,1]{1,0:T(1,128)} %get-tuple-element.67.kla_ref), channel_id=1, source_target_pairs={{0,1},{1,0},{2,3},{3,2},{4,5},{5,4},{6,7},{7,6},{8,9},{9,8},{10,11... | collective-permute-start | bytes 20 | tf_op jit(solution)/shard_map/ppermute | solution.py:50
